TPU v7x, 32 devices: a whole 2x2x4 slice. The times are simulated.
32 devices in a mesh: occ: 8 (over y, x, core), vir: 4 (over z).
Axes of the slice: x: 2, y: 2, z: 4, core: 2. Of those that a mesh axis runs over, the one named last changes fastest.
Arguments:
- amplitudes: float32 [1024, 2048], P('occ'), may hold values from -6 to 6
- amp_cols: int32 [8, 32], P('occ'), may hold values from 0 to 63, all different within a row
- integrals: float32 [4, 8, 64, 1024], P('vir', 'occ'), may hold values from -0.25 to 0.25
- int_rows: int32 [4, 8, 16], P('vir', 'occ'), may hold values from 0 to 63
- int_cols: int32 [4, 8, 16], P('vir', 'occ'), may hold values from 0 to 31
Outputs:
- ladder: float32 [1024, 2048], P(('occ', 'vir'))
Inputs may be any that keep to these rules, and one draw needn't show every extreme that they name: `amp_cols`: each row names 32 different contracted tiles, and every tile is named by some row. `int_rows`: tiles may repeat; repeated tiles add.
All inputs are finite; a program needn't handle non-finite values.
Results may differ from a plain program's by a relative error of at most 0.0003.
Values sent between devices are 32-bit elements; how exact they have to be, the bound alone decides.
No kernel may reach another device: no remote copies, remote signals or barrier semaphores. Data moves between devices by JAX's collectives and lax.ppermute only.
A program may use at most 128 MiB of HBM per device.

v0:
```python
import math

import jax
import jax.numpy as jnp
from jax import lax
from jax.sharding import PartitionSpec as P

AB_TILES = 32


def contract(running, amp_blocks, slot_names, tile_block, row_block, col_block):
    tile_side = tile_block.shape[2]
    per_row = tile_block.shape[3] // tile_side
    tile_count = row_block.size
    tile_list = tile_block.reshape(tile_count // per_row, tile_side, per_row, tile_side)
    tile_list = tile_list.transpose(0, 2, 1, 3).reshape(tile_count, tile_side, tile_side)
    row_ids = row_block.reshape(tile_count)
    out_ids = col_block.reshape(tile_count)
    group_size = math.gcd(tile_count, 64)
    group_count = tile_count // group_size
    slot_ids = jnp.arange(slot_names.shape[0], dtype=jnp.int32)
    column_ids = jnp.arange(running.shape[1], dtype=jnp.int32)

    def one_group(current, entries):
        tile_group, row_group, col_group = entries
        matches = row_group[:, None] == slot_names[None, :]
        is_hit = jnp.any(matches, axis=1)
        slot_of = jnp.sum(jnp.where(matches, slot_ids[None, :], 0), axis=1)
        tile_group = jnp.where(is_hit[:, None, None], tile_group, jnp.zeros_like(tile_group))
        chosen = jnp.take(amp_blocks, slot_of, axis=1)
        product = jnp.einsum(
            "pnk,nkl->pnl",
            chosen,
            tile_group,
            precision=lax.Precision.HIGHEST,
            preferred_element_type=jnp.float32,
        )
        onehot = (col_group[:, None] == column_ids[None, :]).astype(jnp.float32)
        added = jnp.einsum(
            "pnl,nm->pml",
            product,
            onehot,
            precision=lax.Precision.HIGHEST,
            preferred_element_type=jnp.float32,
        )
        return (current + added, None)

    entries = (
        tile_list.reshape(group_count, group_size, tile_side, tile_side),
        row_ids.reshape(group_count, group_size),
        out_ids.reshape(group_count, group_size),
    )
    result, _ = lax.scan(one_group, running, entries)
    return result


def local(amplitudes, amp_cols, integrals, int_rows, int_cols):
    tile_side = integrals.shape[2]
    slots = amp_cols.shape[1]
    slot_names = amp_cols.reshape(slots)
    pair_rows = amplitudes.shape[0]
    amp_blocks = amplitudes.reshape(pair_rows, slots, tile_side)
    empty = jnp.zeros((pair_rows, AB_TILES, tile_side), jnp.float32)
    summed = contract(
        empty,
        amp_blocks,
        slot_names,
        lax.all_gather(integrals, "occ", axis=1, tiled=True),
        lax.all_gather(int_rows, "occ", axis=1, tiled=True),
        lax.all_gather(int_cols, "occ", axis=1, tiled=True),
    )
    partial_value = summed.reshape(pair_rows, AB_TILES * tile_side)
    return lax.psum_scatter(partial_value, "vir", scatter_dimension=0, tiled=True)


def solution(mesh):
    return jax.shard_map(
        local,
        mesh=mesh,
        in_specs=(
            P("occ", None),
            P("occ", None),
            P("vir", "occ", None, None),
            P("vir", "occ", None),
            P("vir", "occ", None),
        ),
        out_specs=P(("occ", "vir"), None),
        check_vma=False,
    )
```

profile of v0, /device:TPU:0, one launch (start us, length us, event | category | flops | bytes accessed | tf_op | source)
XLA Modules:
  0.0 109.5 jit_solution(13588619931249455003)
XLA Ops:
  6.5 0.0 all-gather.2.cloned.1.call-start
  6.5 0.7 all-gather.2.cloned.1.call-update
  7.3 0.0 reduce-scatter.4.cloned.1.call-start
  7.3 10.3 %all_gather.10 = s32[1,8,16]{2,0,1:T(1,128)S(1)} all-gather(s32[1,1,16]{2,0,1:T(1,128)} %bitcast.65), channel_id=1, replica_groups=mesh['occ'=8,'vir'=4] {'occ'}, dimensions={1}, use_global_device_ids=true | all-gather | bytes 576 | tf_op jit(solution)/shard_map/all_gather | solution.py:69
  17.6 0.5 broadcast.65
  18.1 0.6 reduce.7
  18.8 0.1 reshape_reshape.10
  18.9 8.6 %all_gather.9 = s32[1,8,16]{2,0,1:T(1,128)S(1)} all-gather(s32[1,1,16]{2,0,1:T(1,128)} %bitcast.66), channel_id=1, replica_groups=mesh['occ'=8,'vir'=4] {'occ'}, dimensions={1}, use_global_device_ids=true | all-gather | bytes 576 | tf_op jit(solution)/shard_map/all_gather | solution.py:70
  27.5 0.6 reduce.6
  28.1 0.1 reshape_reshape.9
  28.2 1.5 %copy.17 = f32[128,2048]{0,1:T(8,128)S(1)} copy(f32[128,2048]{1,0:T(8,128)} %param.7) | data formatting | bytes 2097152 | tf_op args[0]
  29.7 10.1 %all-gather.2.cloned.1.call-done = f32[1,8,64,1024]{3,2,0,1:T(8,128)} async-done(((f32[1,1,64,1024]{3,2,0,1:T(8,128)}), f32[1,8,64,1024]{3,2,0,1:T(8,128)}) %all-gather.2.cloned.1.call-update) | async-done | bytes 2097168 | tf_op jit(solution)/shard_map/all_gather | solution.py:68
  39.9 4.5 %reshape.33 = f32[8,64,16,64]{3,2,1,0:T(8,128)} reshape(f32[1,8,64,1024]{3,2,0,1:T(8,128)} %all-gather.2.cloned.1.call-done) | data formatting | bytes 4194304 | tf_op jit(solution)/shard_map/reshape | solution.py:15
  44.4 0.0 copy-start
  44.4 5.6 %copy.16 = f32[8,16,64,64]{2,3,1,0:T(8,128)} copy(f32[8,16,64,64]{3,1,2,0:T(8,128)} %bitcast.62) | data formatting | bytes 4194304 | tf_op jit(solution)/shard_map/transpose | solution.py:16
  50.0 0.0 copy-done
  50.0 22.2 %while.13 = (s32[]{:T(128)}, f32[128,32,64]{0,1,2:T(8,128)}, s32[2,64]{1,0:T(2,128)S(1)}, s32[2,64]{1,0:T(2,128)S(1)}, s32[1,32]{1,0:T(1,128)S(1)}, /*index=5*/f...) while((s32[]{:T(128)}, f32[128,32,64]{0,1,2:T(8,128)}, ...), condition=%wide.region_3.4_spmd.clone.clone, body=%wide.region_0.3_spmd.clone.clone.sunk | while | flops 605304256 | bytes 14688619 | solution.py:53
  50.0 0.1 fusion.43
  50.1 0.7 gather_fusion
  50.8 0.1 compare_reduce_fusion.2
  50.9 5.4 %fusion.45 = f32[128,64,64]{0,2,1:T(8,128)} fusion(f32[64,128,64]{1,2,0:T(8,128)S(1)} %gather_fusion, f32[2,64,64,64]{2,3,1,0:T(8,128)} %get-tuple-element.205, s32[]{:T(128)} %get-tuple-element.191, pred[64]{0:T(512)(128)(4,1)S(1)} %compare_and_fusion.2, pred[64]{0:T(512)(128)(4,1)S(1)} %compare_reduce_fusion.2), kind=kOutput, calls=%fused_computation.9.clone.1 | convolution fusion | flops 403439616 | bytes 6292096 | tf_op jit(solution)/shard_map/while/body/eval_jaxpr/pnk,nkl->pnl/dot_general | solution.py:31
  56.3 4.7 %fusion.46 = f32[128,32,64]{0,1,2:T(8,128)} fusion(f32[128,64,64]{0,2,1:T(8,128)} %fusion.45, f32[128,32,64]{0,1,2:T(8,128)} %get-tuple-element.192, pred[]{:T(512)S(6)} %compare.3, s32[64]{0:T(128)S(1)} %get-tuple-element.181), kind=kOutput, calls=%fused_computation.11.clone.1 | convolution fusion | flops 201852928 | bytes 4194561 | tf_op jit(solution)/shard_map/while/body/eval_jaxpr/pnl,nm->pml/dot_general | solution.py:39
  60.9 0.1 fusion.43
  61.0 0.7 gather_fusion
  61.7 0.1 compare_reduce_fusion.2
  61.8 5.4 %fusion.45 = f32[128,64,64]{0,2,1:T(8,128)} fusion(f32[64,128,64]{1,2,0:T(8,128)S(1)} %gather_fusion, f32[2,64,64,64]{2,3,1,0:T(8,128)} %get-tuple-element.205, s32[]{:T(128)} %get-tuple-element.191, pred[64]{0:T(512)(128)(4,1)S(1)} %compare_and_fusion.2, pred[64]{0:T(512)(128)(4,1)S(1)} %compare_reduce_fusion.2), kind=kOutput, calls=%fused_computation.9.clone.1 | convolution fusion | flops 403439616 | bytes 6292096 | tf_op jit(solution)/shard_map/while/body/eval_jaxpr/pnk,nkl->pnl/dot_general | solution.py:31
  67.2 4.9 %fusion.46 = f32[128,32,64]{0,1,2:T(8,128)} fusion(f32[128,64,64]{0,2,1:T(8,128)} %fusion.45, f32[128,32,64]{0,1,2:T(8,128)} %get-tuple-element.192, pred[]{:T(512)S(6)} %compare.3, s32[64]{0:T(128)S(1)} %get-tuple-element.181), kind=kOutput, calls=%fused_computation.11.clone.1 | convolution fusion | flops 201852928 | bytes 4194561 | tf_op jit(solution)/shard_map/while/body/eval_jaxpr/pnl,nm->pml/dot_general | solution.py:39
  72.2 1.8 %copy.18 = f32[128,32,64]{0,2,1:T(8,128)S(1)} copy(f32[128,32,64]{0,1,2:T(8,128)} %get-tuple-element.72) | data formatting | bytes 2097152 | tf_op jit(solution)/shard_map/while | solution.py:53
  74.0 1.3 %copy.20 = f32[128,2048]{1,0:T(8,128)} copy(f32[128,2048]{0,1:T(8,128)S(1)} %bitcast.63) | data formatting | bytes 2097152
  75.3 0.0 reduce-scatter.4.cloned.1.call-update
  75.3 27.3 %reduce-scatter.4.cloned.1.call-done = f32[32,2048]{1,0:T(8,128)} async-done(((f32[128,2048]{1,0:T(8,128)}), f32[32,2048]{1,0:T(8,128)}) %reduce-scatter.4.cloned.1.call-update) | async-done | bytes 262160 | tf_op jit(solution)/shard_map/reduce_scatter | solution.py:73
  (9 shorter events, 0.1 us)
Async XLA Ops:
  6.5 33.3 %all-gather.2.cloned.1.call-start = ((), (), s32[]{:S(2)}) async-start(), calls=%async_computation.1 | async-start | bytes 2359296 | tf_op jit(solution)/shard_map/all_gather | solution.py:68
  7.3 95.4 %reduce-scatter.4.cloned.1.call-start = ((), (), s32[]{:S(2)}) async-start(), calls=%async_computation.2 | async-start | bytes 1310720 | tf_op jit(solution)/shard_map/reduce_scatter | solution.py:73
  44.4 5.6 %copy-start = (s32[1,32]{1,0:T(1,128)S(1)}, s32[1,32]{1,0:T(1,128)}, u32[]{:S(2)}) copy-start(s32[1,32]{1,0:T(1,128)} %param.8) | copy-start | bytes 388
Sparse Core Ops, SparseCore 0:
  9.2 30.5 all-gather.1
  75.5 27.1 reduce-scatter.3
where the time goes:
time: 110 us; the launch traced here: 109 us
  waiting for transfers between devices  38.2 us (35%)
  matrix products  20.4 us (19%)
  blocking collectives  18.9 us (17%)
  local copies, waits for them, and re-layouts  16.8 us (15%)
  between operations  13.4 us (12%)
  other arithmetic  1.68 us (2%)
    reduce_scatter x1, waiting for transfers between devices, local(): lax.psum_scatter(partial_value, 'vir', scatter_dimension=0, tiled=True)  27.3 us
    dot_general x2, matrix products, one_group(): jnp.einsum('pnk,nkl->pnl', chosen, tile_group, precision=lax.Precision.HI...  10.8 us
    all_gather x1, blocking collectives, local(): lax.all_gather(int_rows, 'occ', axis=1, tiled=True)  10.3 us
    all_gather x1, waiting for transfers between devices, local(): lax.all_gather(integrals, 'occ', axis=1, tiled=True)  10.1 us
    dot_general x2, matrix products, one_group(): jnp.einsum('pnl,nm->pml', product, onehot, precision=lax.Precision.HIGHES...  9.58 us
    all_gather x1, blocking collectives, local(): lax.all_gather(int_cols, 'occ', axis=1, tiled=True)  8.6 us
    transpose x1, local copies, waits for them, and re-layouts, contract(): tile_list.transpose(0, 2, 1, 3).reshape(tile_count, tile_side, tile_side)  5.56 us
    reshape x1, local copies, waits for them, and re-layouts, contract(): tile_block.reshape(tile_count // per_row, tile_side, per_row, tile_side)  4.51 us
  transfers between devices with their start and end apart: 2, of which 2 were waited for; matrix products, arithmetic and copies ran while one was open for 3% of the time, Pallas kernels for 0%

commit v1 on v0

v1 whole, which is shorter than its diff:
```python
import functools

import jax
import jax.numpy as jnp
from jax import lax
from jax.experimental import pallas as pl
from jax.experimental.pallas import tpu as pltpu
from jax.sharding import PartitionSpec as P

AB_TILES = 32
CD_TILES = 64
LANES = 128
UNROLL = 4


def pack_kernel(tiles_ref, rows_ref, cols_ref, out_ref):
    side, width = tiles_ref.shape
    groups = width // LANES
    for g in range(groups):
        out_ref[g * side : (g + 1) * side, :] = tiles_ref[:, g * LANES : (g + 1) * LANES]
    count = rows_ref.shape[1]
    base = groups * side
    out_ref[base : base + 8, :] = jnp.zeros((8, LANES), jnp.float32)
    out_ref[base : base + 1, :count] = rows_ref[...].astype(jnp.float32)
    out_ref[base + 1 : base + 2, :count] = cols_ref[...].astype(jnp.float32)


def pack(tiles, rows, cols):
    side, width = tiles.shape
    return pl.pallas_call(
        pack_kernel,
        out_shape=jax.ShapeDtypeStruct((width // LANES * side + 8, LANES), jnp.float32),
        name="pack",
    )(tiles, rows, cols)


def split(value):
    high = value.astype(jnp.bfloat16)
    low = (value - high.astype(jnp.float32)).astype(jnp.bfloat16)
    return high, low


def product_kernel(n_in, n_out, side, count, names_ref, blocks_ref, amp_ref, *refs):
    packs = refs[:n_in]
    outs = refs[n_in : n_in + n_out]
    tiles, ids, three, total, slot_of, entry, sems = refs[n_in + n_out :]
    body = packs[0].shape[0] - 8
    copies = []
    for j in range(n_in):
        id_copy = pltpu.make_async_copy(packs[j].at[pl.ds(body, 8)], ids.at[j], sems.at[j, 0])
        id_copy.start()
        tile_copy = pltpu.make_async_copy(
            packs[j].at[pl.ds(0, body)], tiles.at[pl.ds(j * body, body)], sems.at[j, 1]
        )
        tile_copy.start()
        copies.append((id_copy, tile_copy))

    slots = names_ref.shape[1]

    @pl.loop(0, CD_TILES)
    def _(r):
        slot_of[r] = -1

    @pl.loop(0, slots)
    def _(s):
        slot_of[names_ref[0, s]] = s

    lane = lax.broadcasted_iota(jnp.int32, (1, LANES), 1)
    left = lane < side
    for g in range(amp_ref.shape[1] // LANES):
        both = amp_ref[:, g * LANES : (g + 1) * LANES]
        high = both.astype(jnp.bfloat16).astype(jnp.float32)
        low = both - high
        high_turned = pltpu.roll(high, side, 1)
        low_turned = pltpu.roll(low, side, 1)
        three[2 * g, :, :LANES] = jnp.where(left, high, low_turned).astype(jnp.bfloat16)
        three[2 * g, :, LANES:] = high[:, :side].astype(jnp.bfloat16)
        three[2 * g + 1, :, :LANES] = jnp.where(left, high_turned, low).astype(jnp.bfloat16)
        three[2 * g + 1, :, LANES:] = high_turned[:, :side].astype(jnp.bfloat16)

    total[...] = jnp.zeros_like(total)

    for id_copy, tile_copy in copies:
        id_copy.wait()

    found = 0
    for j in range(n_in):
        for t in range(count):
            row = ids[j, 0, t].astype(jnp.int32)
            col = ids[j, 1, t].astype(jnp.int32)
            slot = slot_of[row]
            entry[found, 0] = slot
            entry[found, 1] = col
            entry[found, 2] = (j * count + t) // 2 * side
            entry[found, 3] = t % 2
            found = found + (slot >= 0).astype(jnp.int32)
    for k in range(UNROLL):
        entry[found + k, 0] = 0
        entry[found + k, 1] = -2
        entry[found + k, 2] = 0
        entry[found + k, 3] = 0
    for id_copy, tile_copy in copies:
        tile_copy.wait()

    @pl.loop(0, (found + UNROLL - 1) // UNROLL)
    def _(step):
        products = []
        for k in range(UNROLL):
            n = step * UNROLL + k
            slot, col, base, half = (entry[n, f] for f in range(4))
            goal = lax.rem(col + 2, 2)
            pair = tiles[pl.ds(pl.multiple_of(base, side), side), :]
            turned = jnp.where(half == goal, pair, pltpu.roll(pair, side, 1))
            keep = (lane >= goal * side) & (lane < goal * side + side) & (col >= 0)
            high, low = split(jnp.where(keep, turned, 0.0))
            weights = jnp.concatenate([high, high, low], axis=0)
            products.append(
                (
                    jnp.maximum(col, 0) // 2,
                    jnp.dot(three[slot], weights, preferred_element_type=jnp.float32),
                )
            )
        for group, product in products:
            total[group] += product

    for b, out_ref in enumerate(outs):
        height = out_ref.shape[0]
        base = pl.multiple_of(blocks_ref[b] * height, height)
        for g in range(total.shape[0]):
            out_ref[:, g * LANES : (g + 1) * LANES] = total[g, pl.ds(base, height), :]


def products(names, blocks, amplitudes, packs, side, count, n_out):
    rows, slots = amplitudes.shape[0], names.shape[1]
    n_in = len(packs)
    body = packs[0].shape[0] - 8
    groups = AB_TILES * side // LANES
    smem = pl.BlockSpec(memory_space=pltpu.SMEM)
    vmem = pl.BlockSpec(memory_space=pltpu.VMEM)
    block = jax.ShapeDtypeStruct((rows // n_out, AB_TILES * side), jnp.float32)
    return pl.pallas_call(
        functools.partial(product_kernel, n_in, n_out, side, count),
        out_shape=[block] * n_out,
        in_specs=[smem, smem, vmem] + [pl.BlockSpec(memory_space=pl.ANY)] * n_in,
        out_specs=[vmem] * n_out,
        scratch_shapes=[
            pltpu.VMEM((n_in * body, LANES), jnp.float32),
            pltpu.SMEM((n_in, 8, LANES), jnp.float32),
            pltpu.VMEM((slots, rows, 3 * side), jnp.bfloat16),
            pltpu.VMEM((groups, rows, LANES), jnp.float32),
            pltpu.SMEM((CD_TILES,), jnp.int32),
            pltpu.SMEM((n_in * count + UNROLL, 4), jnp.int32),
            pltpu.SemaphoreType.DMA((n_in, 2)),
        ],
        compiler_params=pltpu.CompilerParams(vmem_limit_bytes=40 * 1024 * 1024),
        name="products",
    )(names, blocks, amplitudes, *packs)


def local(n_occ, n_vir, amplitudes, amp_cols, integrals, int_rows, int_cols):
    side, width = integrals.shape[2:]
    count = width // side
    own = pack(
        integrals.reshape(side, width),
        int_rows.reshape(1, count),
        int_cols.reshape(1, count),
    )

    def swap(value, mask):
        return lax.ppermute(value, "occ", [(i, i ^ mask) for i in range(n_occ)])

    def along(value, pairs):
        return lax.ppermute(value, "vir", pairs)

    if n_occ == 8:
        first, second, third = swap(own, 2), swap(own, 4), swap(own, 6)
        mine = [own, first, second, third]
        packs = mine + [swap(value, 1) for value in mine]
    else:
        everyone = lax.all_gather(own, "occ", axis=0)
        packs = [everyone[i] for i in range(n_occ)]

    place = lax.axis_index("vir")
    if n_vir == 4:
        table = jnp.array([[3, 1, 2, 0], [0, 2, 3, 1], [3, 1, 0, 2], [0, 2, 1, 3]], jnp.int32)
        near, mid, far, mine = products(
            amp_cols, table[place], amplitudes, packs, side, count, n_vir
        )
        at_end = (place == 0) | (place == 3)
        near = along(near, [(0, 1), (1, 0), (2, 3), (3, 2)])
        middle = along(mid, [(1, 2), (2, 1)])
        far = far + jnp.where(at_end, 0.0, near)
        far = along(far, [(0, 2), (1, 3), (2, 0), (3, 1)])
        outer = along(mid, [(0, 1), (3, 2)])
        return mine + jnp.where(at_end, near, 0.0) + middle + far + outer
    (whole,) = products(amp_cols, jnp.zeros((1,), jnp.int32), amplitudes, packs, side, count, 1)
    return lax.psum_scatter(whole, "vir", scatter_dimension=0, tiled=True)


def solution(mesh):
    return jax.shard_map(
        functools.partial(local, mesh.shape["occ"], mesh.shape["vir"]),
        mesh=mesh,
        in_specs=(
            P("occ", None),
            P("occ", None),
            P("vir", "occ", None, None),
            P("vir", "occ", None),
            P("vir", "occ", None),
        ),
        out_specs=P(("occ", "vir"), None),
        check_vma=False,
    )
```

time: 110 us -> 56.4 us (0.51)
  matrix products: 20.4 us -> 0 us
  blocking collectives: 18.9 us -> 0 us
  local copies, waits for them, and re-layouts: 16.8 us -> 2.88 us
  between operations: 13.4 us -> 0.04 us
  starting transfers between devices: 0.04 us -> 13.2 us
  Pallas kernels: 0 us -> 9.72 us
  waiting for transfers between devices: 38.2 us -> 29.3 us
    ppermute x0 -> x11, waiting for transfers between devices: none -> 29.3 us  [the longest x4 16.6 us: along(): return lax.ppermute(value, 'vir', pairs)]
    reduce_scatter x1 -> x0, waiting for transfers between devices: 27.3 us -> none  [local(): lax.psum_scatter(partial_value, 'vir', scatter_dimension=0, tiled=True)]
    dot_general x4 -> x0, matrix products: 20.4 us -> none  [the longest x2 10.8 us: one_group(): jnp.einsum('pnk,nkl->pnl', chosen, tile_group, precision=lax.Precision.HI...]
    all_gather x2 -> x0, blocking collectives: 18.9 us -> none  [the longest x1 10.3 us: local(): lax.all_gather(int_rows, 'occ', axis=1, tiled=True)]
    ppermute x0 -> x11, starting transfers between devices: none -> 13.2 us  [the longest x4 8.54 us: along(): return lax.ppermute(value, 'vir', pairs)]
    all_gather x1 -> x0, waiting for transfers between devices: 10.1 us -> none  [local(): lax.all_gather(integrals, 'occ', axis=1, tiled=True)]
    pallas_call x0 -> x2, Pallas kernels: none -> 9.72 us  [the longest x1 8.03 us: products(): pl.pallas_call(functools.partial(product_kernel, n_in, n_out, side, count...]
    transpose x1 -> x0, local copies, waits for them, and re-layouts: 5.56 us -> none  [contract(): tile_list.transpose(0, 2, 1, 3).reshape(tile_count, tile_side, tile_side)]
  transfers between devices with their start and end apart: 2 -> 11, of which waited for: 2 -> 8; matrix products, arithmetic and copies ran while one was open for 3% -> 1% of each run, Pallas kernels for 0% -> 0%
where the time goes in v1:
time: 56.4 us; the launch traced here: 56 us
  waiting for transfers between devices  29.3 us (52%)
  starting transfers between devices  13.2 us (23%)
  Pallas kernels  9.72 us (17%)
  local copies, waits for them, and re-layouts  2.88 us (5%)
  other arithmetic  0.83 us (1%)
    ppermute x4, waiting for transfers between devices, along(): return lax.ppermute(value, 'vir', pairs)  16.6 us
    ppermute x7, waiting for transfers between devices, swap(): return lax.ppermute(value, 'occ', [(i, i ^ mask) for i in range(n_occ)])  12.7 us
    ppermute x4, starting transfers between devices, along(): return lax.ppermute(value, 'vir', pairs)  8.54 us
    pallas_call x1, Pallas kernels, products(): pl.pallas_call(functools.partial(product_kernel, n_in, n_out, side, count...  8.03 us
    ppermute x7, starting transfers between devices, swap(): return lax.ppermute(value, 'occ', [(i, i ^ mask) for i in range(n_occ)])  4.7 us
    unnamed x6, local copies, waits for them, and re-layouts  2.18 us
    pallas_call x1, Pallas kernels, pack(): pl.pallas_call(pack_kernel, out_shape=jax.ShapeDtypeStruct((width // LANE...  1.69 us
  transfers between devices with their start and end apart: 11, of which 8 were waited for; matrix products, arithmetic and copies ran while one was open for 1% of the time, Pallas kernels for 0%

profile of v1, /device:TPU:0, one launch (start us, length us, event | category | flops | bytes accessed | tf_op | source)
XLA Modules:
  0.0 56.0 jit_solution(18275452757133773422)
XLA Ops:
  0.0 1.7 %pack.1.refs_0_ = f32[520,128]{1,0:T(8,128)} custom-call(f32[64,1024]{1,0:T(8,128)} %bitcast.5, s32[1,16]{1,0:T(1,128)} %bitcast.6, s32[1,16]{1,0:T(1,128)} %bitcast.7), custom_call_target="tpu_custom_call" | custom-call | tf_op jit(solution)/shard_map/pack/pallas_call | solution.py:30
  1.7 3.9 %collective-permute-start.2 = (f32[520,128]{1,0:T(8,128)}, f32[520,128]{1,0:T(8,128)S(1)}, u32[]{:S(2)}, u32[]{:S(2)}) collective-permute-start(f32[520,128]{1,0:T(8,128)} %pack.1.refs_0_), channel_id=1, source_target_pairs={{0,24},{4,28},{8,16},{12,20},{16,8},{20,12},{24,0},{28,4},{1,25},{... | collective-permute-start | bytes 798728 | tf_op jit(solution)/shard_map/ppermute | solution.py:170
  5.6 0.5 collective-permute-start.1
  6.1 0.1 collective-permute-start
  6.2 0.0 collective-permute-start.3
  6.2 6.9 %collective-permute-done.2.refs_3_ = f32[520,128]{1,0:T(8,128)S(1)} collective-permute-done((f32[520,128]{1,0:T(8,128)}, f32[520,128]{1,0:T(8,128)S(1)}, u32[]{:S(2)}, u32[]{:S(2)}) %collective-permute-start.2) | collective-permute-done | bytes 266272 | tf_op jit(solution)/shard_map/ppermute | solution.py:170
  13.1 0.0 collective-permute-start.6
  13.1 4.8 %collective-permute-done.1.refs_2_ = f32[520,128]{1,0:T(8,128)S(1)} collective-permute-done((f32[520,128]{1,0:T(8,128)}, f32[520,128]{1,0:T(8,128)S(1)}, u32[]{:S(2)}, u32[]{:S(2)}) %collective-permute-start.1) | collective-permute-done | bytes 266272 | tf_op jit(solution)/shard_map/ppermute | solution.py:170
  17.9 0.0 collective-permute-start.5
  17.9 0.3 collective-permute-done.refs_1_
  18.2 0.2 collective-permute-start.4
  18.4 0.0 copy-start.2
  18.4 0.7 %dynamic-slice_bitcast_fusion.blocks_ref = s32[4]{0:T(128)S(1)} fusion(s32[4,4]{1,0:T(4,128)} %constant.14.clone, s32[]{:T(128)S(6)} %select_n.17), kind=kLoop, calls=%fused_computation.2 | loop fusion | bytes 36 | tf_op jit(solution)/shard_map/squeeze | solution.py:187
  19.1 0.0 collective-permute-done.3.refs_4_
  19.1 0.0 collective-permute-done.6.refs_7_
  19.1 0.3 collective-permute-done.5.refs_6_
  19.4 0.4 collective-permute-done.4.refs_5_
  19.8 0.0 copy-done.2
  19.8 0.0 copy-start
  19.8 1.0 %copy-done = f32[520,128]{1,0:T(8,128)S(1)} copy-done((f32[520,128]{1,0:T(8,128)S(1)}, f32[520,128]{1,0:T(8,128)}, u32[]{:S(2)}) %copy-start) | copy-done | bytes 266264
  20.8 0.0 copy-start.1
  20.8 1.2 %copy-done.1 = f32[128,2048]{1,0:T(8,128)S(1)} copy-done((f32[128,2048]{1,0:T(8,128)S(1)}, f32[128,2048]{1,0:T(8,128)}, u32[]{:S(2)}) %copy-start.1) | copy-done | bytes 1048600
  22.0 8.0 %products.1 = (f32[32,2048]{1,0:T(8,128)S(1)}, f32[32,2048]{1,0:T(8,128)S(1)}, f32[32,2048]{1,0:T(8,128)S(1)}, f32[32,2048]{1,0:T(8,128)S(1)}) custom-call(s32[1,32]{1,0:T(1,128)S(1)} %copy-done.2, s32[4]{0:T(128)S(1)} %dynamic-slice_bitcast_fusion.blocks_ref, f32[128,2048]{1,0:T(8,128)S(1)} %copy-done.1, f32[520,128]{1,0:T(8,128)S(1)} %copy-done, ...), custom_call_target="tpu_custom_call" | custom-call | tf_op jit(solution)/shard_map/products/pallas_call | solution.py:141
  30.0 2.4 %collective-permute-start.7 = (f32[32,2048]{1,0:T(8,128)S(1)}, f32[32,2048]{1,0:T(8,128)S(1)}, u32[]{:S(2)}, u32[]{:S(2)}) collective-permute-start(f32[32,2048]{1,0:T(8,128)S(1)} %get-tuple-element.10), channel_id=1, source_target_pairs={{0,1},{1,0},{2,3},{3,2},{4,5},{5,4},{6,7},{7,6},{8,9},{9,8},{10,11... | collective-permute-start | bytes 786440 | tf_op jit(solution)/shard_map/ppermute | solution.py:173
  32.5 1.9 %collective-permute-start.10 = (f32[32,2048]{1,0:T(8,128)S(1)}, f32[32,2048]{1,0:T(8,128)S(1)}, u32[]{:S(2)}, u32[]{:S(2)}) collective-permute-start(f32[32,2048]{1,0:T(8,128)S(1)} %get-tuple-element.11), channel_id=1, source_target_pairs={{0,1},{3,2},{4,5},{7,6},{8,9},{11,10},{12,13},{15,14},{16,17},{19,... | collective-permute-start | bytes 786440 | tf_op jit(solution)/shard_map/ppermute | solution.py:173
  34.4 0.7 %collective-permute-start.8 = (f32[32,2048]{1,0:T(8,128)S(1)}, f32[32,2048]{1,0:T(8,128)S(1)}, u32[]{:S(2)}, u32[]{:S(2)}) collective-permute-start(f32[32,2048]{1,0:T(8,128)S(1)} %get-tuple-element.11), channel_id=1, source_target_pairs={{1,2},{2,1},{5,6},{6,5},{9,10},{10,9},{13,14},{14,13},{17,18},{18,... | collective-permute-start | bytes 786440 | tf_op jit(solution)/shard_map/ppermute | solution.py:173
  35.1 4.1 %collective-permute-done.7 = f32[32,2048]{1,0:T(8,128)S(1)} collective-permute-done((f32[32,2048]{1,0:T(8,128)S(1)}, f32[32,2048]{1,0:T(8,128)S(1)}, u32[]{:S(2)}, u32[]{:S(2)}) %collective-permute-start.7) | collective-permute-done | bytes 262176 | tf_op jit(solution)/shard_map/ppermute | solution.py:173
  39.3 3.5 %collective-permute-start.9 = (f32[32,2048]{1,0:T(8,128)S(1)}, f32[32,2048]{1,0:T(8,128)S(1)}, u32[]{:S(2)}, u32[]{:S(2)}) collective-permute-start(f32[32,2048]{1,0:T(8,128)S(1)} %select_add_fusion), channel_id=1, source_target_pairs={{0,2},{1,3},{2,0},{3,1},{4,6},{5,7},{6,4},{7,5},{8,10},{9,11},{10,... | collective-permute-start | bytes 786440 | tf_op jit(solution)/shard_map/ppermute | solution.py:173
  42.7 1.3 %collective-permute-done.10 = f32[32,2048]{1,0:T(8,128)S(1)} collective-permute-done((f32[32,2048]{1,0:T(8,128)S(1)}, f32[32,2048]{1,0:T(8,128)S(1)}, u32[]{:S(2)}, u32[]{:S(2)}) %collective-permute-start.10) | collective-permute-done | bytes 262176 | tf_op jit(solution)/shard_map/ppermute | solution.py:173
  44.1 0.0 collective-permute-done.8
  44.1 11.1 %collective-permute-done.9 = f32[32,2048]{1,0:T(8,128)S(1)} collective-permute-done((f32[32,2048]{1,0:T(8,128)S(1)}, f32[32,2048]{1,0:T(8,128)S(1)}, u32[]{:S(2)}, u32[]{:S(2)}) %collective-permute-start.9) | collective-permute-done | bytes 262176 | tf_op jit(solution)/shard_map/ppermute | solution.py:173
  55.2 0.8 %add_add_fusion = f32[32,2048]{1,0:T(8,128)} fusion(f32[32,2048]{1,0:T(8,128)S(1)} %collective-permute-done.10, f32[32,2048]{1,0:T(8,128)S(1)} %collective-permute-done.9, f32[32,2048]{1,0:T(8,128)S(1)} %collective-permute-done.8, f32[32,2048]{1,0:T(8,128)S(1)} %get-tuple-element.9, f32[32,2048]{1,0:T(8,128)S(1)} %collective-permute-done.7, pred[]{:T(512)S(6)} %or.3), kind=kLoop, calls=%fused_computation | loop fusion | flops 327680 | bytes 1572865 | tf_op jit(solution)/shard_map/add | solution.py:195
  (1 shorter events, 0.0 us)
Async XLA Ops:
  1.7 11.4 %collective-permute-start.2 = (f32[520,128]{1,0:T(8,128)}, f32[520,128]{1,0:T(8,128)S(1)}, u32[]{:S(2)}, u32[]{:S(2)}) collective-permute-start(f32[520,128]{1,0:T(8,128)} %pack.1.refs_0_), channel_id=1, source_target_pairs={{0,24},{4,28},{8,16},{12,20},{16,8},{20,12},{24,0},{28,4},{1,25},{... | collective-permute-start | bytes 798728 | tf_op jit(solution)/shard_map/ppermute | solution.py:170
  5.6 12.3 %collective-permute-start.1 = (f32[520,128]{1,0:T(8,128)}, f32[520,128]{1,0:T(8,128)S(1)}, u32[]{:S(2)}, u32[]{:S(2)}) collective-permute-start(f32[520,128]{1,0:T(8,128)} %pack.1.refs_0_), channel_id=1, source_target_pairs={{0,16},{4,20},{8,24},{12,28},{16,0},{20,4},{24,8},{28,12},{1,17},{... | collective-permute-start | bytes 798728 | tf_op jit(solution)/shard_map/ppermute | solution.py:170
  6.1 12.1 %collective-permute-start = (f32[520,128]{1,0:T(8,128)}, f32[520,128]{1,0:T(8,128)S(1)}, u32[]{:S(2)}, u32[]{:S(2)}) collective-permute-start(f32[520,128]{1,0:T(8,128)} %pack.1.refs_0_), channel_id=1, source_target_pairs={{0,8},{4,12},{8,0},{12,4},{16,24},{20,28},{24,16},{28,20},{1,9},{5... | collective-permute-start | bytes 798728 | tf_op jit(solution)/shard_map/ppermute | solution.py:170
  6.2 13.0 %collective-permute-start.3 = (f32[520,128]{1,0:T(8,128)}, f32[520,128]{1,0:T(8,128)S(1)}, u32[]{:S(2)}, u32[]{:S(2)}) collective-permute-start(f32[520,128]{1,0:T(8,128)} %pack.1.refs_0_), channel_id=1, source_target_pairs={{0,4},{4,0},{8,12},{12,8},{16,20},{20,16},{24,28},{28,24},{1,5},{5... | collective-permute-start | bytes 798728 | tf_op jit(solution)/shard_map/ppermute | solution.py:170
  13.1 6.1 %collective-permute-start.6 = (f32[520,128]{1,0:T(8,128)S(1)}, f32[520,128]{1,0:T(8,128)S(1)}, u32[]{:S(2)}, u32[]{:S(2)}) collective-permute-start(f32[520,128]{1,0:T(8,128)S(1)} %collective-permute-done.2.refs_3_), channel_id=1, source_target_pairs={{0,4},{4,0},{8,12},{12,8},{16,20},{20,16},{24,28},{28,24},{1,5},{5... | collective-permute-start | bytes 798728 | tf_op jit(solution)/shard_map/ppermute | solution.py:170
  17.9 1.5 %collective-permute-start.5 = (f32[520,128]{1,0:T(8,128)S(1)}, f32[520,128]{1,0:T(8,128)S(1)}, u32[]{:S(2)}, u32[]{:S(2)}) collective-permute-start(f32[520,128]{1,0:T(8,128)S(1)} %collective-permute-done.1.refs_2_), channel_id=1, source_target_pairs={{0,4},{4,0},{8,12},{12,8},{16,20},{20,16},{24,28},{28,24},{1,5},{5... | collective-permute-start | bytes 798728 | tf_op jit(solution)/shard_map/ppermute | solution.py:170
  18.2 1.6 %collective-permute-start.4 = (f32[520,128]{1,0:T(8,128)S(1)}, f32[520,128]{1,0:T(8,128)S(1)}, u32[]{:S(2)}, u32[]{:S(2)}) collective-permute-start(f32[520,128]{1,0:T(8,128)S(1)} %collective-permute-done.refs_1_), channel_id=1, source_target_pairs={{0,4},{4,0},{8,12},{12,8},{16,20},{20,16},{24,28},{28,24},{1,5},{5... | collective-permute-start | bytes 798728 | tf_op jit(solution)/shard_map/ppermute | solution.py:170
  18.4 1.4 %copy-start.2 = (s32[1,32]{1,0:T(1,128)S(1)}, s32[1,32]{1,0:T(1,128)}, u32[]{:S(2)}) copy-start(s32[1,32]{1,0:T(1,128)} %names_ref.1) | copy-start | bytes 388
  19.8 1.0 %copy-start = (f32[520,128]{1,0:T(8,128)S(1)}, f32[520,128]{1,0:T(8,128)}, u32[]{:S(2)}) copy-start(f32[520,128]{1,0:T(8,128)} %pack.1.refs_0_) | copy-start | bytes 798724
  20.8 1.2 %copy-start.1 = (f32[128,2048]{1,0:T(8,128)S(1)}, f32[128,2048]{1,0:T(8,128)}, u32[]{:S(2)}) copy-start(f32[128,2048]{1,0:T(8,128)} %amp_ref.1) | copy-start | bytes 3145732
  30.0 9.2 %collective-permute-start.7 = (f32[32,2048]{1,0:T(8,128)S(1)}, f32[32,2048]{1,0:T(8,128)S(1)}, u32[]{:S(2)}, u32[]{:S(2)}) collective-permute-start(f32[32,2048]{1,0:T(8,128)S(1)} %get-tuple-element.10), channel_id=1, source_target_pairs={{0,1},{1,0},{2,3},{3,2},{4,5},{5,4},{6,7},{7,6},{8,9},{9,8},{10,11... | collective-permute-start | bytes 786440 | tf_op jit(solution)/shard_map/ppermute | solution.py:173
  32.5 11.6 %collective-permute-start.10 = (f32[32,2048]{1,0:T(8,128)S(1)}, f32[32,2048]{1,0:T(8,128)S(1)}, u32[]{:S(2)}, u32[]{:S(2)}) collective-permute-start(f32[32,2048]{1,0:T(8,128)S(1)} %get-tuple-element.11), channel_id=1, source_target_pairs={{0,1},{3,2},{4,5},{7,6},{8,9},{11,10},{12,13},{15,14},{16,17},{19,... | collective-permute-start | bytes 786440 | tf_op jit(solution)/shard_map/ppermute | solution.py:173
  34.4 9.6 %collective-permute-start.8 = (f32[32,2048]{1,0:T(8,128)S(1)}, f32[32,2048]{1,0:T(8,128)S(1)}, u32[]{:S(2)}, u32[]{:S(2)}) collective-permute-start(f32[32,2048]{1,0:T(8,128)S(1)} %get-tuple-element.11), channel_id=1, source_target_pairs={{1,2},{2,1},{5,6},{6,5},{9,10},{10,9},{13,14},{14,13},{17,18},{18,... | collective-permute-start | bytes 786440 | tf_op jit(solution)/shard_map/ppermute | solution.py:173
  39.3 15.9 %collective-permute-start.9 = (f32[32,2048]{1,0:T(8,128)S(1)}, f32[32,2048]{1,0:T(8,128)S(1)}, u32[]{:S(2)}, u32[]{:S(2)}) collective-permute-start(f32[32,2048]{1,0:T(8,128)S(1)} %select_add_fusion), channel_id=1, source_target_pairs={{0,2},{1,3},{2,0},{3,1},{4,6},{5,7},{6,4},{7,5},{8,10},{9,11},{10,... | collective-permute-start | bytes 786440 | tf_op jit(solution)/shard_map/ppermute | solution.py:173

commit v2 on v0

v2 whole, which is shorter than its diff:
```python
import functools

import jax
import jax.numpy as jnp
from jax import lax
from jax.experimental import pallas as pl
from jax.experimental.pallas import tpu as pltpu
from jax.sharding import PartitionSpec as P

AB_TILES = 32
LANES = 128
UNROLL = 8
PIECES = 2
HBM = pl.BlockSpec(memory_space=pltpu.HBM)
SMEM = pl.BlockSpec(memory_space=pltpu.SMEM)
VMEM = pl.BlockSpec(memory_space=pltpu.VMEM)
PARAMS = pltpu.CompilerParams(vmem_limit_bytes=8 * 1024 * 1024)


def in_vmem(value):
    return pltpu.with_memory_space_constraint(value, pltpu.VMEM)


def in_hbm(value):
    return pltpu.with_memory_space_constraint(value, pltpu.HBM)


def together(*values):
    return lax.optimization_barrier(values)


def pack_kernel(tiles_ref, rows_ref, cols_ref, *refs):
    outs, numbers, sems = refs[:-2], refs[-2], refs[-1]
    side, width = tiles_ref.shape
    count = rows_ref.shape[1] // len(outs)
    groups = width // LANES // len(outs)
    base = groups * side
    copies = [
        pltpu.make_async_copy(rows_ref, numbers.at[0], sems.at[0]),
        pltpu.make_async_copy(cols_ref, numbers.at[1], sems.at[1]),
    ]
    for p, out_ref in enumerate(outs):
        for g in range(groups):
            n = p * groups + g
            copies.append(
                pltpu.make_async_copy(
                    tiles_ref.at[:, pl.ds(n * LANES, LANES)],
                    out_ref.at[pl.ds(g * side, side)],
                    sems.at[2 + n],
                )
            )
    for copy in copies:
        copy.start()
    for out_ref in outs:
        out_ref[base : base + 8, :] = jnp.zeros((8, LANES), jnp.float32)
    for copy in copies[:2]:
        copy.wait()
    for p, out_ref in enumerate(outs):
        for k in range(2):
            values = numbers[k][:, p * count : (p + 1) * count]
            out_ref[base + k : base + k + 1, :count] = values.astype(jnp.float32)
    for copy in copies[2:]:
        copy.wait()


def pack(tiles, rows, cols, parts):
    side, width = tiles.shape
    groups = width // LANES
    return pl.pallas_call(
        pack_kernel,
        out_shape=[pltpu.VMEM((groups // parts * side + 8, LANES), jnp.float32)] * parts,
        in_specs=[HBM] * 3,
        out_specs=[VMEM] * parts,
        scratch_shapes=[
            pltpu.VMEM((2, 1, rows.shape[1]), jnp.int32),
            pltpu.SemaphoreType.DMA((2 + groups,)),
        ],
        compiler_params=PARAMS,
        name="pack",
    )(in_hbm(tiles), in_hbm(rows), in_hbm(cols))


def split(value):
    high = value.astype(jnp.bfloat16)
    low = (value - high.astype(jnp.float32)).astype(jnp.bfloat16)
    return high, low


def prepare_kernel(n_blocks, side, place_ref, names_in, amp_ref, three_ref, names_out, names_ref, amps, sems):
    place = place_ref[0]
    rows = amp_ref.shape[0]
    height = rows // n_blocks
    names_copy = pltpu.make_async_copy(names_in, names_ref, sems.at[n_blocks])
    names_copy.start()
    copies = []
    for b in range(n_blocks):
        source = pl.ds(pl.multiple_of((place ^ b) * height, height), height)
        copy = pltpu.make_async_copy(amp_ref.at[source], amps.at[b], sems.at[b])
        copy.start()
        copies.append(copy)
    names_copy.wait()
    for s in range(names_ref.shape[1]):
        names_out[s : s + 1, :] = jnp.full((1, LANES), names_ref[0, s], jnp.int32)
    lane = lax.broadcasted_iota(jnp.int32, (1, LANES), 1)
    left = lane < side
    for b in range(n_blocks):
        here = slice(b * height, (b + 1) * height)
        copies[b].wait()
        for g in range(amp_ref.shape[1] // LANES):
            both = amps[b, :, g * LANES : (g + 1) * LANES]
            high = both.astype(jnp.bfloat16).astype(jnp.float32)
            low = both - high
            high_turned = pltpu.roll(high, side, 1)
            low_turned = pltpu.roll(low, side, 1)
            three_ref[2 * g, here, :LANES] = jnp.where(left, high, low_turned).astype(jnp.bfloat16)
            three_ref[2 * g, here, LANES:] = high[:, :side].astype(jnp.bfloat16)
            three_ref[2 * g + 1, here, :LANES] = jnp.where(left, high_turned, low).astype(jnp.bfloat16)
            three_ref[2 * g + 1, here, LANES:] = high_turned[:, :side].astype(jnp.bfloat16)


def prepare(place, names, amplitudes, n_blocks):
    rows, width = amplitudes.shape
    slots = names.shape[1]
    side = width // slots
    return pl.pallas_call(
        functools.partial(prepare_kernel, n_blocks, side),
        out_shape=[
            pltpu.VMEM((slots, rows, 3 * side), jnp.bfloat16),
            pltpu.VMEM((slots, LANES), jnp.int32),
        ],
        in_specs=[SMEM, HBM, HBM],
        out_specs=[VMEM, VMEM],
        scratch_shapes=[
            pltpu.SMEM((1, slots), jnp.int32),
            pltpu.VMEM((n_blocks, rows // n_blocks, width), jnp.float32),
            pltpu.SemaphoreType.DMA((n_blocks + 1,)),
        ],
        compiler_params=PARAMS,
        name="prepare",
        cost_estimate=pl.CostEstimate(flops=0, bytes_accessed=0, transcendentals=0),
    )(place, in_hbm(names), in_hbm(amplitudes))


def product_kernel(n_in, n_outs, first, side, count, names_ref, three_ref, *refs):
    packs = refs[:n_in]
    outs = refs[-n_outs - 3 : -3]
    numbers, words, sem = refs[-3:]
    body = packs[0].shape[0] - 8
    slots = names_ref.shape[0]
    slot_id = lax.broadcasted_iota(jnp.int32, (slots, LANES), 0) + 1
    for j in range(n_in):
        rows = packs[j][body : body + 1, :].astype(jnp.int32)
        slot = jnp.sum(jnp.where(names_ref[...] == rows, slot_id, 0), axis=0, keepdims=True)
        cols = packs[j][body + 1 : body + 2, :].astype(jnp.int32)
        numbers[j : j + 1, :] = slot * AB_TILES + cols
    copy = pltpu.make_async_copy(numbers, words, sem)
    copy.start()
    if first:
        for out_ref in outs:
            out_ref[...] = jnp.zeros_like(out_ref)
    copy.wait()

    lane = lax.broadcasted_iota(jnp.int32, (1, LANES), 1)
    tiles = [(j, t) for j in range(n_in) for t in range(count)]
    for start in range(0, len(tiles), UNROLL):
        products = []
        for j, t in tiles[start : start + UNROLL]:
            word = words[j, t]
            col = word & (AB_TILES - 1)
            slot = word // AB_TILES
            goal = col & 1
            pair = packs[j][t // 2 * side : (t // 2 + 1) * side, :]
            turned = jnp.where(goal == t % 2, pair, pltpu.roll(pair, side, 1))
            keep = (lane >= goal * side) & (lane < goal * side + side) & (slot > 0)
            high, low = split(jnp.where(keep, turned, 0.0))
            weights = jnp.concatenate([high, high, low], axis=0)
            values = three_ref[jnp.maximum(slot - 1, 0)]
            products.append(
                (
                    pl.multiple_of(col // 2 * LANES, LANES),
                    jnp.dot(values, weights, preferred_element_type=jnp.float32),
                )
            )
        for column, product in products:
            for b, out_ref in enumerate(outs):
                height = out_ref.shape[0]
                out_ref[:, pl.ds(column, LANES)] += product[b * height : (b + 1) * height]


def accumulate(names, three, packs, totals, n_outs, side, count):
    rows, n_in = three.shape[1], len(packs)
    block = pltpu.VMEM((rows // n_outs, AB_TILES * side), jnp.float32)
    carried = [] if totals is None else [in_vmem(total) for total in totals]
    return pl.pallas_call(
        functools.partial(product_kernel, n_in, n_outs, totals is None, side, count),
        out_shape=[block] * n_outs,
        in_specs=[VMEM] * (2 + n_in + len(carried)),
        out_specs=[VMEM] * n_outs,
        input_output_aliases={2 + n_in + b: b for b in range(len(carried))},
        scratch_shapes=[
            pltpu.VMEM((8, LANES), jnp.int32),
            pltpu.SMEM((8, LANES), jnp.int32),
            pltpu.SemaphoreType.DMA,
        ],
        compiler_params=PARAMS,
        name="products",
        cost_estimate=pl.CostEstimate(flops=0, bytes_accessed=0, transcendentals=0),
    )(in_vmem(names), in_vmem(three), *map(in_vmem, packs), *carried)


def add_kernel(carried_ref, more_ref, out_ref):
    out_ref[...] = carried_ref[...] + more_ref[...]


def added(carried, more):
    return pl.pallas_call(
        add_kernel,
        out_shape=pltpu.VMEM(carried.shape, carried.dtype),
        in_specs=[VMEM, VMEM],
        out_specs=VMEM,
        input_output_aliases={0: 0},
        compiler_params=PARAMS,
        name="added",
    )(in_vmem(carried), in_vmem(more))


def local(n_occ, n_vir, amplitudes, amp_cols, integrals, int_rows, int_cols):
    side, width = integrals.shape[2:]
    count = width // side
    place = lax.axis_index("vir").astype(jnp.int32).reshape(1)

    def swap(value, mask):
        return lax.ppermute(value, "occ", [(i, i ^ mask) for i in range(n_occ)])

    def along(value, mask):
        return lax.ppermute(value, "vir", [(i, i ^ mask) for i in range(n_vir)])

    low, high = pack(
        integrals.reshape(side, width),
        int_rows.reshape(1, count),
        int_cols.reshape(1, count),
        2,
    )

    def add(packs, blocks):
        return accumulate(names, three, packs, blocks, PIECES * n_vir, side, count // 2)

    if n_occ == 8:
        x_low, y_high, x_high, y_low = swap(low, 2), swap(high, 4), swap(high, 2), swap(low, 4)
        close = [swap(low, 1), swap(high, 1)]
        three, names = prepare(place, amp_cols, amplitudes, n_vir)
        blocks = add([low, high], None)
        x_low, y_high, blocks = together(x_low, y_high, blocks)
        far_low, far_high = swap(x_low, 4), swap(y_high, 2)
        turned = [swap(x_low, 1), swap(y_high, 1)]
        blocks = add([x_low, y_high] + close, blocks)
        x_high, y_low, blocks = together(x_high, y_low, blocks)
        later = [swap(x_high, 1), swap(y_low, 1)]
        blocks = add([x_high, y_low] + turned, blocks)
        far_low, far_high, blocks = together(far_low, far_high, blocks)
        last = [swap(far_low, 1), swap(far_high, 1)]
        blocks = add([far_low, far_high] + later, blocks)
        blocks = list(add(last, blocks))
    else:
        three, names = prepare(place, amp_cols, amplitudes, n_vir)
        blocks = add([low, high], None)
        for mask in range(1, n_occ):
            blocks = add([swap(low, mask), swap(high, mask)], blocks)
        blocks = list(blocks)

    blocks = [blocks[r * PIECES : (r + 1) * PIECES] for r in range(n_vir)]
    bit = 1
    while bit < n_vir:
        sent = range(n_vir - bit, 0, -2 * bit)
        got = {r: [along(piece, bit) for piece in blocks[r]] for r in sent}
        for r in sent:
            blocks[r ^ bit] = [added(old, new) for old, new in zip(blocks[r ^ bit], got[r])]
        bit *= 2
    return jnp.concatenate(blocks[0], axis=0)


def solution(mesh):
    return jax.shard_map(
        functools.partial(local, mesh.shape["occ"], mesh.shape["vir"]),
        mesh=mesh,
        in_specs=(
            P("occ", None),
            P("occ", None),
            P("vir", "occ", None, None),
            P("vir", "occ", None),
            P("vir", "occ", None),
        ),
        out_specs=P(("occ", "vir"), None),
        check_vma=False,
    )
```

time: 110 us -> 44.4 us (0.40)
  waiting for transfers between devices: 38.2 us -> 14.6 us
  matrix products: 20.4 us -> 0 us
  starting transfers between devices: 0.04 us -> 19.1 us
  blocking collectives: 18.9 us -> 0 us
  local copies, waits for them, and re-layouts: 16.8 us -> 0 us
  between operations: 13.4 us -> 0.16 us
  Pallas kernels: 0 us -> 9.55 us
    reduce_scatter x1 -> x0, waiting for transfers between devices: 27.3 us -> none  [local(): lax.psum_scatter(partial_value, 'vir', scatter_dimension=0, tiled=True)]
    dot_general x4 -> x0, matrix products: 20.4 us -> none  [the longest x2 10.8 us: one_group(): jnp.einsum('pnk,nkl->pnl', chosen, tile_group, precision=lax.Precision.HI...]
    ppermute x0 -> x20, starting transfers between devices: none -> 19.1 us  [the longest x14 10.7 us: swap(): return lax.ppermute(value, 'occ', [(i, i ^ mask) for i in range(n_occ)])]
    all_gather x2 -> x0, blocking collectives: 18.9 us -> none  [the longest x1 10.3 us: local(): lax.all_gather(int_rows, 'occ', axis=1, tiled=True)]
    ppermute x0 -> x20, waiting for transfers between devices: none -> 14.6 us  [the longest x6 13.6 us: along(): return lax.ppermute(value, 'vir', [(i, i ^ mask) for i in range(n_vir)])]
    all_gather x1 -> x0, waiting for transfers between devices: 10.1 us -> none  [local(): lax.all_gather(integrals, 'occ', axis=1, tiled=True)]
    pallas_call x0 -> x13, Pallas kernels: none -> 9.55 us  [the longest x5 6.84 us: accumulate(): pl.pallas_call(functools.partial(product_kernel, n_in, n_outs, totals is...]
    transpose x1 -> x0, local copies, waits for them, and re-layouts: 5.56 us -> none  [contract(): tile_list.transpose(0, 2, 1, 3).reshape(tile_count, tile_side, tile_side)]
  transfers between devices with their start and end apart: 2 -> 20, of which waited for: 2 -> 6; matrix products, arithmetic and copies ran while one was open for 3% -> 0% of each run, Pallas kernels for 0% -> 17%
where the time goes in v2:
time: 44.4 us; the launch traced here: 44.2 us
  starting transfers between devices  19.1 us (43%)
  waiting for transfers between devices  14.6 us (33%)
  Pallas kernels  9.55 us (22%)
  other arithmetic  0.72 us (2%)
    ppermute x6, waiting for transfers between devices, along(): return lax.ppermute(value, 'vir', [(i, i ^ mask) for i in range(n_vir)])  13.6 us
    ppermute x14, starting transfers between devices, swap(): return lax.ppermute(value, 'occ', [(i, i ^ mask) for i in range(n_occ)])  10.7 us
    ppermute x6, starting transfers between devices, along(): return lax.ppermute(value, 'vir', [(i, i ^ mask) for i in range(n_vir)])  8.41 us
    pallas_call x5, Pallas kernels, accumulate(): pl.pallas_call(functools.partial(product_kernel, n_in, n_outs, totals is...  6.84 us
    pallas_call x1, Pallas kernels, prepare(): pl.pallas_call(functools.partial(prepare_kernel, n_blocks, side), out_sha...  1.56 us
    pallas_call x1, Pallas kernels, pack(): pl.pallas_call(pack_kernel, out_shape=[pltpu.VMEM((groups // parts * side...  0.99 us
    ppermute x14, waiting for transfers between devices, swap(): return lax.ppermute(value, 'occ', [(i, i ^ mask) for i in range(n_occ)])  0.99 us
  transfers between devices with their start and end apart: 20, of which 6 were waited for; matrix products, arithmetic and copies ran while one was open for 0% of the time, Pallas kernels for 17%

profile of v2, /device:TPU:0, one launch (start us, length us, event | category | flops | bytes accessed | tf_op | source)
XLA Modules:
  0.0 44.2 jit_solution(16310697073868176579)
XLA Ops:
  0.0 1.0 %pack.1 = (f32[264,128]{1,0:T(8,128)S(1)}, f32[264,128]{1,0:T(8,128)S(1)}) custom-call(f32[64,1024]{1,0:T(8,128)} %bitcast.4, s32[1,16]{1,0:T(1,128)} %bitcast.5, s32[1,16]{1,0:T(1,128)} %bitcast.6), custom_call_target="tpu_custom_call" | custom-call | tf_op jit(solution)/shard_map/pack/pallas_call | solution.py:69
  1.0 3.0 %collective-permute-start = (f32[264,128]{1,0:T(8,128)S(1)}, f32[264,128]{1,0:T(8,128)S(1)}, u32[]{:S(2)}, u32[]{:S(2)}) collective-permute-start(f32[264,128]{1,0:T(8,128)S(1)} %get-tuple-element.81.refs_0_), channel_id=1, source_target_pairs={{0,8},{4,12},{8,0},{12,4},{16,24},{20,28},{24,16},{28,20},{1,9},{5... | collective-permute-start | bytes 405512 | tf_op jit(solution)/shard_map/ppermute | solution.py:233
  4.0 1.5 %collective-permute-start.1 = (f32[264,128]{1,0:T(8,128)S(1)}, f32[264,128]{1,0:T(8,128)S(1)}, u32[]{:S(2)}, u32[]{:S(2)}) collective-permute-start(f32[264,128]{1,0:T(8,128)S(1)} %get-tuple-element.82.refs_1_), channel_id=1, source_target_pairs={{0,16},{4,20},{8,24},{12,28},{16,0},{20,4},{24,8},{28,12},{1,17},{... | collective-permute-start | bytes 405512 | tf_op jit(solution)/shard_map/ppermute | solution.py:233
  5.5 0.0 collective-permute-start.6
  5.5 0.5 %collective-permute-start.7 = (f32[264,128]{1,0:T(8,128)S(1)}, f32[264,128]{1,0:T(8,128)S(1)}, u32[]{:S(2)}, u32[]{:S(2)}) collective-permute-start(f32[264,128]{1,0:T(8,128)S(1)} %get-tuple-element.82.refs_1_), channel_id=1, source_target_pairs={{0,4},{4,0},{8,12},{12,8},{16,20},{20,16},{24,28},{28,24},{1,5},{5... | collective-permute-start | bytes 405512 | tf_op jit(solution)/shard_map/ppermute | solution.py:233
  6.0 0.5 %collective-permute-start.4 = (f32[264,128]{1,0:T(8,128)S(1)}, f32[264,128]{1,0:T(8,128)S(1)}, u32[]{:S(2)}, u32[]{:S(2)}) collective-permute-start(f32[264,128]{1,0:T(8,128)S(1)} %get-tuple-element.82.refs_1_), channel_id=1, source_target_pairs={{0,8},{4,12},{8,0},{12,4},{16,24},{20,28},{24,16},{28,20},{1,9},{5... | collective-permute-start | bytes 405512 | tf_op jit(solution)/shard_map/ppermute | solution.py:233
  6.6 1.6 %prepare.1 = (bf16[32,128,192]{2,1,0:T(8,128)(2,1)S(1)}, s32[32,128]{1,0:T(8,128)S(1)}) custom-call(s32[1]{0:T(128)} %bitcast.place_ref, s32[1,32]{1,0:T(1,128)} %names_in.1, f32[128,2048]{1,0:T(8,128)} %amp_ref.1), custom_call_target="tpu_custom_call" | custom-call | tf_op jit(solution)/shard_map/prepare/pallas_call | solution.py:125
  8.1 1.2 %products.5 = (f32[16,2048]{1,0:T(8,128)S(1)}, f32[16,2048]{1,0:T(8,128)S(1)}, f32[16,2048]{1,0:T(8,128)S(1)}, f32[16,2048]{1,0:T(8,128)S(1)}, f32[16,2048]{1,0:...) custom-call(s32[32,128]{1,0:T(8,128)S(1)} %get-tuple-element.79.names_ref, ...), custom_call_target="tpu_custom_call" | custom-call | tf_op jit(solution)/shard_map/products/pallas_call | solution.py:194
  9.4 0.0 collective-permute-done.refs_0_
  9.4 0.1 collective-permute-start.5
  9.5 0.0 collective-permute-done.1.refs_1_
  9.5 0.0 collective-permute-start.8
  9.6 0.0 collective-permute-done.6.refs_2_
  9.6 0.5 %collective-permute-start.9 = (f32[264,128]{1,0:T(8,128)S(1)}, f32[264,128]{1,0:T(8,128)S(1)}, u32[]{:S(2)}, u32[]{:S(2)}) collective-permute-start(f32[264,128]{1,0:T(8,128)S(1)} %collective-permute-done.1.refs_1_), channel_id=1, source_target_pairs={{0,4},{4,0},{8,12},{12,8},{16,20},{20,16},{24,28},{28,24},{1,5},{5... | collective-permute-start | bytes 405512 | tf_op jit(solution)/shard_map/ppermute | solution.py:233
  10.1 0.0 collective-permute-done.7.refs_3_
  10.1 1.9 %collective-permute-start.2 = (f32[264,128]{1,0:T(8,128)S(1)}, f32[264,128]{1,0:T(8,128)S(1)}, u32[]{:S(2)}, u32[]{:S(2)}) collective-permute-start(f32[264,128]{1,0:T(8,128)S(1)} %collective-permute-done.refs_0_), channel_id=1, source_target_pairs={{0,16},{4,20},{8,24},{12,28},{16,0},{20,4},{24,8},{28,12},{1,17},{... | collective-permute-start | bytes 405512 | tf_op jit(solution)/shard_map/ppermute | solution.py:233
  12.0 0.0 collective-permute-done.4.refs_0_
  12.0 1.5 %collective-permute-start.3 = (f32[264,128]{1,0:T(8,128)S(1)}, f32[264,128]{1,0:T(8,128)S(1)}, u32[]{:S(2)}, u32[]{:S(2)}) collective-permute-start(f32[264,128]{1,0:T(8,128)S(1)} %collective-permute-done.1.refs_1_), channel_id=1, source_target_pairs={{0,8},{4,12},{8,0},{12,4},{16,24},{20,28},{24,16},{28,20},{1,9},{5... | collective-permute-start | bytes 405512 | tf_op jit(solution)/shard_map/ppermute | solution.py:233
  13.5 1.5 %products.6 = (f32[16,2048]{1,0:T(8,128)S(1)}, f32[16,2048]{1,0:T(8,128)S(1)}, f32[16,2048]{1,0:T(8,128)S(1)}, f32[16,2048]{1,0:T(8,128)S(1)}, f32[16,2048]{1,0:...) custom-call(s32[32,128]{1,0:T(8,128)S(1)} %get-tuple-element.79.name, ...), custom_call_target="tpu_custom_call", output_to_operand_aliasing={{0}: (6, {}), {1}: (7, {}), {2}: (8, {}), {3}: (9, {}), {4}... | custom-call | tf_op jit(solution)/shard_map/products/pallas_call | solution.py:194
  15.0 1.0 %collective-permute-done.5.refs_1_ = f32[264,128]{1,0:T(8,128)S(1)} collective-permute-done((f32[264,128]{1,0:T(8,128)S(1)}, f32[264,128]{1,0:T(8,128)S(1)}, u32[]{:S(2)}, u32[]{:S(2)}) %collective-permute-start.5) | collective-permute-done | bytes 135200 | tf_op jit(solution)/shard_map/ppermute | solution.py:233
  15.9 0.0 collective-permute-start.12
  15.9 0.0 collective-permute-done.8.refs_2_
  15.9 0.5 %collective-permute-start.13 = (f32[264,128]{1,0:T(8,128)S(1)}, f32[264,128]{1,0:T(8,128)S(1)}, u32[]{:S(2)}, u32[]{:S(2)}) collective-permute-start(f32[264,128]{1,0:T(8,128)S(1)} %collective-permute-done.5.refs_1_), channel_id=1, source_target_pairs={{0,4},{4,0},{8,12},{12,8},{16,20},{20,16},{24,28},{28,24},{1,5},{5... | collective-permute-start | bytes 405512 | tf_op jit(solution)/shard_map/ppermute | solution.py:233
  16.5 0.0 collective-permute-done.9.refs_3_
  16.5 1.5 %products.7 = (f32[16,2048]{1,0:T(8,128)S(1)}, f32[16,2048]{1,0:T(8,128)S(1)}, f32[16,2048]{1,0:T(8,128)S(1)}, f32[16,2048]{1,0:T(8,128)S(1)}, f32[16,2048]{1,0:...) custom-call(s32[32,128]{1,0:T(8,128)S(1)} %get-tuple-element.79.name, ...), custom_call_target="tpu_custom_call", output_to_operand_aliasing={{0}: (6, {}), {1}: (7, {}), {2}: (8, {}), {3}: (9, {}), {4}... | custom-call | tf_op jit(solution)/shard_map/products/pallas_call | solution.py:194
  17.9 0.0 collective-permute-done.2.refs_0_
  18.0 0.0 collective-permute-done.3.refs_1_
  18.0 0.1 collective-permute-start.10
  18.0 0.5 %collective-permute-start.11 = (f32[264,128]{1,0:T(8,128)S(1)}, f32[264,128]{1,0:T(8,128)S(1)}, u32[]{:S(2)}, u32[]{:S(2)}) collective-permute-start(f32[264,128]{1,0:T(8,128)S(1)} %collective-permute-done.3.refs_1_), channel_id=1, source_target_pairs={{0,4},{4,0},{8,12},{12,8},{16,20},{20,16},{24,28},{28,24},{1,5},{5... | collective-permute-start | bytes 405512 | tf_op jit(solution)/shard_map/ppermute | solution.py:233
  18.5 0.0 collective-permute-done.12.refs_2_
  18.5 0.0 collective-permute-done.13.refs_3_
  18.5 1.5 %products.8 = (f32[16,2048]{1,0:T(8,128)S(1)}, f32[16,2048]{1,0:T(8,128)S(1)}, f32[16,2048]{1,0:T(8,128)S(1)}, f32[16,2048]{1,0:T(8,128)S(1)}, f32[16,2048]{1,0:...) custom-call(s32[32,128]{1,0:T(8,128)S(1)} %get-tuple-element.79.name, ...), custom_call_target="tpu_custom_call", output_to_operand_aliasing={{0}: (6, {}), {1}: (7, {}), {2}: (8, {}), {3}: (9, {}), {4}... | custom-call | tf_op jit(solution)/shard_map/products/pallas_call | solution.py:194
  20.0 0.0 collective-permute-done.10.refs_0_
  20.0 0.0 collective-permute-done.11.refs_1_
  20.0 1.2 %products.9 = (f32[16,2048]{1,0:T(8,128)S(1)}, f32[16,2048]{1,0:T(8,128)S(1)}, f32[16,2048]{1,0:T(8,128)S(1)}, f32[16,2048]{1,0:T(8,128)S(1)}, f32[16,2048]{1,0:...) custom-call(s32[32,128]{1,0:T(8,128)S(1)} %get-tuple-element.79.name, ...), custom_call_target="tpu_custom_call", output_to_operand_aliasing={{0}: (4, {}), {1}: (5, {}), {2}: (6, {}), {3}: (7, {}), {4}... | custom-call | tf_op jit(solution)/shard_map/products/pallas_call | solution.py:194
  21.2 1.7 %collective-permute-start.15 = (f32[16,2048]{1,0:T(8,128)S(1)}, f32[16,2048]{1,0:T(8,128)S(1)}, u32[]{:S(2)}, u32[]{:S(2)}) collective-permute-start(f32[16,2048]{1,0:T(8,128)S(1)} %get-tuple-element.148), channel_id=1, source_target_pairs={{0,1},{1,0},{2,3},{3,2},{4,5},{5,4},{6,7},{7,6},{8,9},{9,8},{10,11... | collective-permute-start | bytes 393224 | tf_op jit(solution)/shard_map/ppermute | solution.py:236
  22.9 0.4 collective-permute-start.18
  23.3 1.6 %collective-permute-start.14 = (f32[16,2048]{1,0:T(8,128)S(1)}, f32[16,2048]{1,0:T(8,128)S(1)}, u32[]{:S(2)}, u32[]{:S(2)}) collective-permute-start(f32[16,2048]{1,0:T(8,128)S(1)} %get-tuple-element.146), channel_id=1, source_target_pairs={{0,1},{1,0},{2,3},{3,2},{4,5},{5,4},{6,7},{7,6},{8,9},{9,8},{10,11... | collective-permute-start | bytes 393224 | tf_op jit(solution)/shard_map/ppermute | solution.py:236
  24.9 0.4 collective-permute-start.17
  25.4 2.3 %collective-permute-done.15.more_ref = f32[16,2048]{1,0:T(8,128)S(1)} collective-permute-done((f32[16,2048]{1,0:T(8,128)S(1)}, f32[16,2048]{1,0:T(8,128)S(1)}, u32[]{:S(2)}, u32[]{:S(2)}) %collective-permute-start.15) | collective-permute-done | bytes 131104 | tf_op jit(solution)/shard_map/ppermute | solution.py:236
  27.7 2.7 %collective-permute-start.16 = (f32[16,2048]{1,0:T(8,128)S(1)}, f32[16,2048]{1,0:T(8,128)S(1)}, u32[]{:S(2)}, u32[]{:S(2)}) collective-permute-start(f32[16,2048]{1,0:T(8,128)S(1)} %added.7), channel_id=1, source_target_pairs={{0,2},{1,3},{2,0},{3,1},{4,6},{5,7},{6,4},{7,5},{8,10},{9,11},{10,... | collective-permute-start | bytes 393224 | tf_op jit(solution)/shard_map/ppermute | solution.py:236
  30.3 1.5 %collective-permute-done.18.more_ref = f32[16,2048]{1,0:T(8,128)S(1)} collective-permute-done((f32[16,2048]{1,0:T(8,128)S(1)}, f32[16,2048]{1,0:T(8,128)S(1)}, u32[]{:S(2)}, u32[]{:S(2)}) %collective-permute-start.18) | collective-permute-done | bytes 131104 | tf_op jit(solution)/shard_map/ppermute | solution.py:236
  31.9 1.6 %collective-permute-start.19 = (f32[16,2048]{1,0:T(8,128)S(1)}, f32[16,2048]{1,0:T(8,128)S(1)}, u32[]{:S(2)}, u32[]{:S(2)}) collective-permute-start(f32[16,2048]{1,0:T(8,128)S(1)} %added.10), channel_id=1, source_target_pairs={{0,2},{1,3},{2,0},{3,1},{4,6},{5,7},{6,4},{7,5},{8,10},{9,11},{10,... | collective-permute-start | bytes 393224 | tf_op jit(solution)/shard_map/ppermute | solution.py:236
  33.5 4.9 %collective-permute-done.14.more_ref = f32[16,2048]{1,0:T(8,128)S(1)} collective-permute-done((f32[16,2048]{1,0:T(8,128)S(1)}, f32[16,2048]{1,0:T(8,128)S(1)}, u32[]{:S(2)}, u32[]{:S(2)}) %collective-permute-start.14) | collective-permute-done | bytes 131104 | tf_op jit(solution)/shard_map/ppermute | solution.py:236
  38.5 1.9 %collective-permute-done.17.more_ref = f32[16,2048]{1,0:T(8,128)S(1)} collective-permute-done((f32[16,2048]{1,0:T(8,128)S(1)}, f32[16,2048]{1,0:T(8,128)S(1)}, u32[]{:S(2)}, u32[]{:S(2)}) %collective-permute-start.17) | collective-permute-done | bytes 131104 | tf_op jit(solution)/shard_map/ppermute | solution.py:236
  40.4 0.0 collective-permute-done.16.more_ref
  40.5 3.0 %collective-permute-done.19.more_ref = f32[16,2048]{1,0:T(8,128)S(1)} collective-permute-done((f32[16,2048]{1,0:T(8,128)S(1)}, f32[16,2048]{1,0:T(8,128)S(1)}, u32[]{:S(2)}, u32[]{:S(2)}) %collective-permute-start.19) | collective-permute-done | bytes 131104 | tf_op jit(solution)/shard_map/ppermute | solution.py:236
  43.5 0.7 %pad_maximum_fusion = f32[32,2048]{1,0:T(8,128)} fusion(f32[16,2048]{1,0:T(8,128)S(1)} %added.11, f32[16,2048]{1,0:T(8,128)S(1)} %added.8), kind=kLoop, calls=%fused_computation | loop fusion | flops 65536 | bytes 524288 | tf_op jit(solution)/shard_map/concatenate | solution.py:279
  (6 shorter events, 0.2 us)
Async XLA Ops:
  1.0 8.4 %collective-permute-start = (f32[264,128]{1,0:T(8,128)S(1)}, f32[264,128]{1,0:T(8,128)S(1)}, u32[]{:S(2)}, u32[]{:S(2)}) collective-permute-start(f32[264,128]{1,0:T(8,128)S(1)} %get-tuple-element.81.refs_0_), channel_id=1, source_target_pairs={{0,8},{4,12},{8,0},{12,4},{16,24},{20,28},{24,16},{28,20},{1,9},{5... | collective-permute-start | bytes 405512 | tf_op jit(solution)/shard_map/ppermute | solution.py:233
  4.0 5.5 %collective-permute-start.1 = (f32[264,128]{1,0:T(8,128)S(1)}, f32[264,128]{1,0:T(8,128)S(1)}, u32[]{:S(2)}, u32[]{:S(2)}) collective-permute-start(f32[264,128]{1,0:T(8,128)S(1)} %get-tuple-element.82.refs_1_), channel_id=1, source_target_pairs={{0,16},{4,20},{8,24},{12,28},{16,0},{20,4},{24,8},{28,12},{1,17},{... | collective-permute-start | bytes 405512 | tf_op jit(solution)/shard_map/ppermute | solution.py:233
  5.5 4.0 %collective-permute-start.6 = (f32[264,128]{1,0:T(8,128)S(1)}, f32[264,128]{1,0:T(8,128)S(1)}, u32[]{:S(2)}, u32[]{:S(2)}) collective-permute-start(f32[264,128]{1,0:T(8,128)S(1)} %get-tuple-element.81.refs_0_), channel_id=1, source_target_pairs={{0,4},{4,0},{8,12},{12,8},{16,20},{20,16},{24,28},{28,24},{1,5},{5... | collective-permute-start | bytes 405512 | tf_op jit(solution)/shard_map/ppermute | solution.py:233
  5.5 4.5 %collective-permute-start.7 = (f32[264,128]{1,0:T(8,128)S(1)}, f32[264,128]{1,0:T(8,128)S(1)}, u32[]{:S(2)}, u32[]{:S(2)}) collective-permute-start(f32[264,128]{1,0:T(8,128)S(1)} %get-tuple-element.82.refs_1_), channel_id=1, source_target_pairs={{0,4},{4,0},{8,12},{12,8},{16,20},{20,16},{24,28},{28,24},{1,5},{5... | collective-permute-start | bytes 405512 | tf_op jit(solution)/shard_map/ppermute | solution.py:233
  6.0 6.0 %collective-permute-start.4 = (f32[264,128]{1,0:T(8,128)S(1)}, f32[264,128]{1,0:T(8,128)S(1)}, u32[]{:S(2)}, u32[]{:S(2)}) collective-permute-start(f32[264,128]{1,0:T(8,128)S(1)} %get-tuple-element.82.refs_1_), channel_id=1, source_target_pairs={{0,8},{4,12},{8,0},{12,4},{16,24},{20,28},{24,16},{28,20},{1,9},{5... | collective-permute-start | bytes 405512 | tf_op jit(solution)/shard_map/ppermute | solution.py:233
  9.4 6.6 %collective-permute-start.5 = (f32[264,128]{1,0:T(8,128)S(1)}, f32[264,128]{1,0:T(8,128)S(1)}, u32[]{:S(2)}, u32[]{:S(2)}) collective-permute-start(f32[264,128]{1,0:T(8,128)S(1)} %get-tuple-element.81.refs_0_), channel_id=1, source_target_pairs={{0,16},{4,20},{8,24},{12,28},{16,0},{20,4},{24,8},{28,12},{1,17},{... | collective-permute-start | bytes 405512 | tf_op jit(solution)/shard_map/ppermute | solution.py:233
  9.5 6.4 %collective-permute-start.8 = (f32[264,128]{1,0:T(8,128)S(1)}, f32[264,128]{1,0:T(8,128)S(1)}, u32[]{:S(2)}, u32[]{:S(2)}) collective-permute-start(f32[264,128]{1,0:T(8,128)S(1)} %collective-permute-done.refs_0_), channel_id=1, source_target_pairs={{0,4},{4,0},{8,12},{12,8},{16,20},{20,16},{24,28},{28,24},{1,5},{5... | collective-permute-start | bytes 405512 | tf_op jit(solution)/shard_map/ppermute | solution.py:233
  9.6 6.9 %collective-permute-start.9 = (f32[264,128]{1,0:T(8,128)S(1)}, f32[264,128]{1,0:T(8,128)S(1)}, u32[]{:S(2)}, u32[]{:S(2)}) collective-permute-start(f32[264,128]{1,0:T(8,128)S(1)} %collective-permute-done.1.refs_1_), channel_id=1, source_target_pairs={{0,4},{4,0},{8,12},{12,8},{16,20},{20,16},{24,28},{28,24},{1,5},{5... | collective-permute-start | bytes 405512 | tf_op jit(solution)/shard_map/ppermute | solution.py:233
  10.1 7.9 %collective-permute-start.2 = (f32[264,128]{1,0:T(8,128)S(1)}, f32[264,128]{1,0:T(8,128)S(1)}, u32[]{:S(2)}, u32[]{:S(2)}) collective-permute-start(f32[264,128]{1,0:T(8,128)S(1)} %collective-permute-done.refs_0_), channel_id=1, source_target_pairs={{0,16},{4,20},{8,24},{12,28},{16,0},{20,4},{24,8},{28,12},{1,17},{... | collective-permute-start | bytes 405512 | tf_op jit(solution)/shard_map/ppermute | solution.py:233
  12.0 6.0 %collective-permute-start.3 = (f32[264,128]{1,0:T(8,128)S(1)}, f32[264,128]{1,0:T(8,128)S(1)}, u32[]{:S(2)}, u32[]{:S(2)}) collective-permute-start(f32[264,128]{1,0:T(8,128)S(1)} %collective-permute-done.1.refs_1_), channel_id=1, source_target_pairs={{0,8},{4,12},{8,0},{12,4},{16,24},{20,28},{24,16},{28,20},{1,9},{5... | collective-permute-start | bytes 405512 | tf_op jit(solution)/shard_map/ppermute | solution.py:233
  15.9 2.6 %collective-permute-start.12 = (f32[264,128]{1,0:T(8,128)S(1)}, f32[264,128]{1,0:T(8,128)S(1)}, u32[]{:S(2)}, u32[]{:S(2)}) collective-permute-start(f32[264,128]{1,0:T(8,128)S(1)} %collective-permute-done.4.refs_0_), channel_id=1, source_target_pairs={{0,4},{4,0},{8,12},{12,8},{16,20},{20,16},{24,28},{28,24},{1,5},{5... | collective-permute-start | bytes 405512 | tf_op jit(solution)/shard_map/ppermute | solution.py:233
  15.9 2.6 %collective-permute-start.13 = (f32[264,128]{1,0:T(8,128)S(1)}, f32[264,128]{1,0:T(8,128)S(1)}, u32[]{:S(2)}, u32[]{:S(2)}) collective-permute-start(f32[264,128]{1,0:T(8,128)S(1)} %collective-permute-done.5.refs_1_), channel_id=1, source_target_pairs={{0,4},{4,0},{8,12},{12,8},{16,20},{20,16},{24,28},{28,24},{1,5},{5... | collective-permute-start | bytes 405512 | tf_op jit(solution)/shard_map/ppermute | solution.py:233
  18.0 2.1 %collective-permute-start.10 = (f32[264,128]{1,0:T(8,128)S(1)}, f32[264,128]{1,0:T(8,128)S(1)}, u32[]{:S(2)}, u32[]{:S(2)}) collective-permute-start(f32[264,128]{1,0:T(8,128)S(1)} %collective-permute-done.2.refs_0_), channel_id=1, source_target_pairs={{0,4},{4,0},{8,12},{12,8},{16,20},{20,16},{24,28},{28,24},{1,5},{5... | collective-permute-start | bytes 405512 | tf_op jit(solution)/shard_map/ppermute | solution.py:233
  18.0 2.0 %collective-permute-start.11 = (f32[264,128]{1,0:T(8,128)S(1)}, f32[264,128]{1,0:T(8,128)S(1)}, u32[]{:S(2)}, u32[]{:S(2)}) collective-permute-start(f32[264,128]{1,0:T(8,128)S(1)} %collective-permute-done.3.refs_1_), channel_id=1, source_target_pairs={{0,4},{4,0},{8,12},{12,8},{16,20},{20,16},{24,28},{28,24},{1,5},{5... | collective-permute-start | bytes 405512 | tf_op jit(solution)/shard_map/ppermute | solution.py:233
  21.2 6.4 %collective-permute-start.15 = (f32[16,2048]{1,0:T(8,128)S(1)}, f32[16,2048]{1,0:T(8,128)S(1)}, u32[]{:S(2)}, u32[]{:S(2)}) collective-permute-start(f32[16,2048]{1,0:T(8,128)S(1)} %get-tuple-element.148), channel_id=1, source_target_pairs={{0,1},{1,0},{2,3},{3,2},{4,5},{5,4},{6,7},{7,6},{8,9},{9,8},{10,11... | collective-permute-start | bytes 393224 | tf_op jit(solution)/shard_map/ppermute | solution.py:236
  22.9 9.0 %collective-permute-start.18 = (f32[16,2048]{1,0:T(8,128)S(1)}, f32[16,2048]{1,0:T(8,128)S(1)}, u32[]{:S(2)}, u32[]{:S(2)}) collective-permute-start(f32[16,2048]{1,0:T(8,128)S(1)} %get-tuple-element.152), channel_id=1, source_target_pairs={{0,1},{1,0},{2,3},{3,2},{4,5},{5,4},{6,7},{7,6},{8,9},{9,8},{10,11... | collective-permute-start | bytes 393224 | tf_op jit(solution)/shard_map/ppermute | solution.py:236
  23.3 15.1 %collective-permute-start.14 = (f32[16,2048]{1,0:T(8,128)S(1)}, f32[16,2048]{1,0:T(8,128)S(1)}, u32[]{:S(2)}, u32[]{:S(2)}) collective-permute-start(f32[16,2048]{1,0:T(8,128)S(1)} %get-tuple-element.146), channel_id=1, source_target_pairs={{0,1},{1,0},{2,3},{3,2},{4,5},{5,4},{6,7},{7,6},{8,9},{9,8},{10,11... | collective-permute-start | bytes 393224 | tf_op jit(solution)/shard_map/ppermute | solution.py:236
  24.9 15.5 %collective-permute-start.17 = (f32[16,2048]{1,0:T(8,128)S(1)}, f32[16,2048]{1,0:T(8,128)S(1)}, u32[]{:S(2)}, u32[]{:S(2)}) collective-permute-start(f32[16,2048]{1,0:T(8,128)S(1)} %get-tuple-element.150), channel_id=1, source_target_pairs={{0,1},{1,0},{2,3},{3,2},{4,5},{5,4},{6,7},{7,6},{8,9},{9,8},{10,11... | collective-permute-start | bytes 393224 | tf_op jit(solution)/shard_map/ppermute | solution.py:236
  27.7 12.7 %collective-permute-start.16 = (f32[16,2048]{1,0:T(8,128)S(1)}, f32[16,2048]{1,0:T(8,128)S(1)}, u32[]{:S(2)}, u32[]{:S(2)}) collective-permute-start(f32[16,2048]{1,0:T(8,128)S(1)} %added.7), channel_id=1, source_target_pairs={{0,2},{1,3},{2,0},{3,1},{4,6},{5,7},{6,4},{7,5},{8,10},{9,11},{10,... | collective-permute-start | bytes 393224 | tf_op jit(solution)/shard_map/ppermute | solution.py:236
  31.9 11.6 %collective-permute-start.19 = (f32[16,2048]{1,0:T(8,128)S(1)}, f32[16,2048]{1,0:T(8,128)S(1)}, u32[]{:S(2)}, u32[]{:S(2)}) collective-permute-start(f32[16,2048]{1,0:T(8,128)S(1)} %added.10), channel_id=1, source_target_pairs={{0,2},{1,3},{2,0},{3,1},{4,6},{5,7},{6,4},{7,5},{8,10},{9,11},{10,... | collective-permute-start | bytes 393224 | tf_op jit(solution)/shard_map/ppermute | solution.py:236

commit v3 on v2

--- a/solution.py
+++ b/solution.py
@@ -10,7 +10,7 @@
 AB_TILES = 32
 LANES = 128
 UNROLL = 8
-PIECES = 2
+PARTS = 1
 HBM = pl.BlockSpec(memory_space=pltpu.HBM)
 SMEM = pl.BlockSpec(memory_space=pltpu.SMEM)
 VMEM = pl.BlockSpec(memory_space=pltpu.VMEM)
@@ -29,48 +29,46 @@
     return lax.optimization_barrier(values)
 
 
-def pack_kernel(tiles_ref, rows_ref, cols_ref, *refs):
-    outs, numbers, sems = refs[:-2], refs[-2], refs[-1]
+def pack_kernel(tiles_ref, rows_ref, cols_ref, out_ref, numbers, sems):
     side, width = tiles_ref.shape
-    count = rows_ref.shape[1] // len(outs)
-    groups = width // LANES // len(outs)
-    base = groups * side
+    count = rows_ref.shape[1] // PARTS
+    groups = width // LANES // PARTS
+    rows = groups * side + 8
     copies = [
         pltpu.make_async_copy(rows_ref, numbers.at[0], sems.at[0]),
         pltpu.make_async_copy(cols_ref, numbers.at[1], sems.at[1]),
     ]
-    for p, out_ref in enumerate(outs):
-        for g in range(groups):
-            n = p * groups + g
-            copies.append(
-                pltpu.make_async_copy(
-                    tiles_ref.at[:, pl.ds(n * LANES, LANES)],
-                    out_ref.at[pl.ds(g * side, side)],
-                    sems.at[2 + n],
-                )
+    for n in range(PARTS * groups):
+        copies.append(
+            pltpu.make_async_copy(
+                tiles_ref.at[:, pl.ds(n * LANES, LANES)],
+                out_ref.at[pl.ds(n // groups * rows + n % groups * side, side)],
+                sems.at[2 + n],
             )
+        )
     for copy in copies:
         copy.start()
-    for out_ref in outs:
-        out_ref[base : base + 8, :] = jnp.zeros((8, LANES), jnp.float32)
+    for p in range(PARTS):
+        out_ref[(p + 1) * rows - 8 : (p + 1) * rows, :] = jnp.zeros((8, LANES), jnp.float32)
     for copy in copies[:2]:
         copy.wait()
-    for p, out_ref in enumerate(outs):
+    for p in range(PARTS):
         for k in range(2):
+            place = (p + 1) * rows - 8 + k
             values = numbers[k][:, p * count : (p + 1) * count]
-            out_ref[base + k : base + k + 1, :count] = values.astype(jnp.float32)
+            out_ref[place : place + 1, :count] = values.astype(jnp.float32)
     for copy in copies[2:]:
         copy.wait()
 
 
-def pack(tiles, rows, cols, parts):
+def pack(tiles, rows, cols):
     side, width = tiles.shape
     groups = width // LANES
     return pl.pallas_call(
         pack_kernel,
-        out_shape=[pltpu.VMEM((groups // parts * side + 8, LANES), jnp.float32)] * parts,
+        out_shape=pltpu.VMEM((groups * side + PARTS * 8, LANES), jnp.float32),
         in_specs=[HBM] * 3,
-        out_specs=[VMEM] * parts,
+        out_specs=VMEM,
         scratch_shapes=[
             pltpu.VMEM((2, 1, rows.shape[1]), jnp.int32),
             pltpu.SemaphoreType.DMA((2 + groups,)),
@@ -137,7 +135,7 @@
         ],
         compiler_params=PARAMS,
         name="prepare",
-        cost_estimate=pl.CostEstimate(flops=0, bytes_accessed=0, transcendentals=0),
+        cost_estimate=pl.CostEstimate(flops=100, bytes_accessed=100, transcendentals=0),
     )(place, in_hbm(names), in_hbm(amplitudes))
 
 
@@ -145,14 +143,15 @@
     packs = refs[:n_in]
     outs = refs[-n_outs - 3 : -3]
     numbers, words, sem = refs[-3:]
-    body = packs[0].shape[0] - 8
+    rows = count // 2 * side + 8
+    parts = [(pack, base) for pack in packs for base in range(0, pack.shape[0], rows)]
     slots = names_ref.shape[0]
     slot_id = lax.broadcasted_iota(jnp.int32, (slots, LANES), 0) + 1
-    for j in range(n_in):
-        rows = packs[j][body : body + 1, :].astype(jnp.int32)
-        slot = jnp.sum(jnp.where(names_ref[...] == rows, slot_id, 0), axis=0, keepdims=True)
-        cols = packs[j][body + 1 : body + 2, :].astype(jnp.int32)
-        numbers[j : j + 1, :] = slot * AB_TILES + cols
+    for j, (pack, base) in enumerate(parts):
+        row = pack[base + rows - 8 : base + rows - 7, :].astype(jnp.int32)
+        slot = jnp.sum(jnp.where(names_ref[...] == row, slot_id, 0), axis=0, keepdims=True)
+        col = pack[base + rows - 7 : base + rows - 6, :].astype(jnp.int32)
+        numbers[j : j + 1, :] = slot * AB_TILES + col
     copy = pltpu.make_async_copy(numbers, words, sem)
     copy.start()
     if first:
@@ -161,7 +160,7 @@
     copy.wait()
 
     lane = lax.broadcasted_iota(jnp.int32, (1, LANES), 1)
-    tiles = [(j, t) for j in range(n_in) for t in range(count)]
+    tiles = [(j, t) for j in range(len(parts)) for t in range(count)]
     for start in range(0, len(tiles), UNROLL):
         products = []
         for j, t in tiles[start : start + UNROLL]:
@@ -169,7 +168,8 @@
             col = word & (AB_TILES - 1)
             slot = word // AB_TILES
             goal = col & 1
-            pair = packs[j][t // 2 * side : (t // 2 + 1) * side, :]
+            pack, base = parts[j]
+            pair = pack[base + t // 2 * side : base + (t // 2 + 1) * side, :]
             turned = jnp.where(goal == t % 2, pair, pltpu.roll(pair, side, 1))
             keep = (lane >= goal * side) & (lane < goal * side + side) & (slot > 0)
             high, low = split(jnp.where(keep, turned, 0.0))
@@ -182,20 +182,22 @@
                 )
             )
         for column, product in products:
-            for b, out_ref in enumerate(outs):
+            top = 0
+            for out_ref in outs:
                 height = out_ref.shape[0]
-                out_ref[:, pl.ds(column, LANES)] += product[b * height : (b + 1) * height]
-
-
-def accumulate(names, three, packs, totals, n_outs, side, count):
-    rows, n_in = three.shape[1], len(packs)
-    block = pltpu.VMEM((rows // n_outs, AB_TILES * side), jnp.float32)
+                out_ref[:, pl.ds(column, LANES)] += product[top : top + height]
+                top += height
+
+
+def accumulate(names, three, packs, totals, heights, side, count):
+    n_in = len(packs)
+    blocks = [pltpu.VMEM((height, AB_TILES * side), jnp.float32) for height in heights]
     carried = [] if totals is None else [in_vmem(total) for total in totals]
     return pl.pallas_call(
-        functools.partial(product_kernel, n_in, n_outs, totals is None, side, count),
-        out_shape=[block] * n_outs,
+        functools.partial(product_kernel, n_in, len(heights), totals is None, side, count),
+        out_shape=blocks,
         in_specs=[VMEM] * (2 + n_in + len(carried)),
-        out_specs=[VMEM] * n_outs,
+        out_specs=[VMEM] * len(heights),
         input_output_aliases={2 + n_in + b: b for b in range(len(carried))},
         scratch_shapes=[
             pltpu.VMEM((8, LANES), jnp.int32),
@@ -204,7 +206,7 @@
         ],
         compiler_params=PARAMS,
         name="products",
-        cost_estimate=pl.CostEstimate(flops=0, bytes_accessed=0, transcendentals=0),
+        cost_estimate=pl.CostEstimate(flops=100, bytes_accessed=100, transcendentals=0),
     )(in_vmem(names), in_vmem(three), *map(in_vmem, packs), *carried)
 
 
@@ -221,6 +223,7 @@
         input_output_aliases={0: 0},
         compiler_params=PARAMS,
         name="added",
+        cost_estimate=pl.CostEstimate(flops=0, bytes_accessed=8 << 20, transcendentals=0),
     )(in_vmem(carried), in_vmem(more))
 
 
@@ -235,48 +238,52 @@
     def along(value, mask):
         return lax.ppermute(value, "vir", [(i, i ^ mask) for i in range(n_vir)])
 
-    low, high = pack(
+    own = pack(
         integrals.reshape(side, width),
         int_rows.reshape(1, count),
         int_cols.reshape(1, count),
-        2,
     )
+    height = amplitudes.shape[0] // n_vir
+    pieces = [2] * n_vir
+    heights = [height // pieces[r] for r in range(n_vir) for _ in range(pieces[r])]
 
     def add(packs, blocks):
-        return accumulate(names, three, packs, blocks, PIECES * n_vir, side, count // 2)
+        return accumulate(names, three, packs, blocks, heights, side, count // PARTS)
 
     if n_occ == 8:
-        x_low, y_high, x_high, y_low = swap(low, 2), swap(high, 4), swap(high, 2), swap(low, 4)
-        close = [swap(low, 1), swap(high, 1)]
+        x, y, far, close = (swap(own, mask) for mask in (2, 4, 6, 1))
         three, names = prepare(place, amp_cols, amplitudes, n_vir)
-        blocks = add([low, high], None)
-        x_low, y_high, blocks = together(x_low, y_high, blocks)
-        far_low, far_high = swap(x_low, 4), swap(y_high, 2)
-        turned = [swap(x_low, 1), swap(y_high, 1)]
-        blocks = add([x_low, y_high] + close, blocks)
-        x_high, y_low, blocks = together(x_high, y_low, blocks)
-        later = [swap(x_high, 1), swap(y_low, 1)]
-        blocks = add([x_high, y_low] + turned, blocks)
-        far_low, far_high, blocks = together(far_low, far_high, blocks)
-        last = [swap(far_low, 1), swap(far_high, 1)]
-        blocks = add([far_low, far_high] + later, blocks)
-        blocks = list(add(last, blocks))
+        blocks = add([own], None)
+        x, y, blocks = together(x, y, blocks)
+        x_turned, y_turned = swap(x, 1), swap(y, 1)
+        blocks = add([x, y, close], blocks)
+        far, blocks = together(far, blocks)
+        far_turned = swap(far, 1)
+        blocks = add([x_turned, y_turned, far], blocks)
+        blocks = add([far_turned], blocks)
     else:
         three, names = prepare(place, amp_cols, amplitudes, n_vir)
-        blocks = add([low, high], None)
+        blocks = add([own], None)
         for mask in range(1, n_occ):
-            blocks = add([swap(low, mask), swap(high, mask)], blocks)
-        blocks = list(blocks)
-
-    blocks = [blocks[r * PIECES : (r + 1) * PIECES] for r in range(n_vir)]
+            blocks = add([swap(own, mask)], blocks)
+
+    blocks = iter(blocks)
+    blocks = [[next(blocks) for _ in range(pieces[r])] for r in range(n_vir)]
     bit = 1
     while bit < n_vir:
-        sent = range(n_vir - bit, 0, -2 * bit)
-        got = {r: [along(piece, bit) for piece in blocks[r]] for r in sent}
-        for r in sent:
-            blocks[r ^ bit] = [added(old, new) for old, new in zip(blocks[r ^ bit], got[r])]
+        for r in range(n_vir - bit, 1, -2 * bit):
+            got = [along(piece, bit) for piece in blocks[r]]
+            goal = blocks[r ^ bit]
+            goal[0] = added(goal[0], got[0])
+            if r == 2:
+                upper = along(blocks[1][0], 1)
+                upper, goal[0], goal[1] = together(upper, goal[0], goal[1])
+            goal[1] = added(goal[1], got[1])
+        if bit == 1:
+            blocks[2][0], *blocks[1] = together(blocks[2][0], *blocks[1])
         bit *= 2
-    return jnp.concatenate(blocks[0], axis=0)
+    lower = along(blocks[1][1], 1)
+    return jnp.concatenate(blocks[0], axis=0) + jnp.concatenate([upper, lower], axis=0)
 
 
 def solution(mesh):

time: 44.4 us -> 42.2 us (0.950)
  starting transfers between devices: 19.1 us -> 14.2 us
  waiting for transfers between devices: 14.6 us -> 18.4 us
  Pallas kernels: 9.55 us -> 8.62 us
    ppermute x14 -> x7, waiting for transfers between devices: 0.99 us -> 6.73 us  [swap(): return lax.ppermute(value, 'occ', [(i, i ^ mask) for i in range(n_occ)])]
    ppermute x14 -> x7, starting transfers between devices: 10.7 us -> 5.09 us  [swap(): return lax.ppermute(value, 'occ', [(i, i ^ mask) for i in range(n_occ)])]
    ppermute x6, waiting for transfers between devices: 13.6 us -> 11.7 us  [along(): return lax.ppermute(value, 'vir', [(i, i ^ mask) for i in range(n_vir)])]
    pallas_call x6 -> x5, Pallas kernels: 7.83 us -> 6.95 us  [the longest x4 5.96 us: accumulate(): pl.pallas_call(functools.partial(product_kernel, n_in, len(heights), tota...]
    add x0 -> x1, other arithmetic: none -> 0.74 us  [local(): jnp.concatenate(blocks[0], axis=0) + jnp.concatenate([upper, lower], axis=0)]
    concatenate x1 -> x0, other arithmetic: 0.72 us -> none  [local(): return jnp.concatenate(blocks[0], axis=0)]
    ppermute x6, starting transfers between devices: 8.41 us -> 9.11 us  [along(): return lax.ppermute(value, 'vir', [(i, i ^ mask) for i in range(n_vir)])]
  transfers between devices with their start and end apart: 20 -> 13, of which waited for: 6 -> 8; matrix products, arithmetic and copies ran while one was open for 0% -> 0% of each run, Pallas kernels for 17% -> 15%
where the time goes in v3:
time: 42.2 us; the launch traced here: 42.1 us
  waiting for transfers between devices  18.4 us (44%)
  starting transfers between devices  14.2 us (34%)
  Pallas kernels  8.62 us (20%)
  other arithmetic  0.74 us (2%)
    ppermute x6, waiting for transfers between devices, along(): return lax.ppermute(value, 'vir', [(i, i ^ mask) for i in range(n_vir)])  11.7 us
    ppermute x6, starting transfers between devices, along(): return lax.ppermute(value, 'vir', [(i, i ^ mask) for i in range(n_vir)])  9.11 us
    ppermute x7, waiting for transfers between devices, swap(): return lax.ppermute(value, 'occ', [(i, i ^ mask) for i in range(n_occ)])  6.73 us
    pallas_call x4, Pallas kernels, accumulate(): pl.pallas_call(functools.partial(product_kernel, n_in, len(heights), tota...  5.96 us
    ppermute x7, starting transfers between devices, swap(): return lax.ppermute(value, 'occ', [(i, i ^ mask) for i in range(n_occ)])  5.09 us
    pallas_call x1, Pallas kernels, prepare(): pl.pallas_call(functools.partial(prepare_kernel, n_blocks, side), out_sha...  1.56 us
    pallas_call x1, Pallas kernels, pack(): pl.pallas_call(pack_kernel, out_shape=pltpu.VMEM((groups * side + PARTS *...  0.99 us
  transfers between devices with their start and end apart: 13, of which 8 were waited for; matrix products, arithmetic and copies ran while one was open for 0% of the time, Pallas kernels for 15%

profile of v3, /device:TPU:0, one launch (start us, length us, event | category | flops | bytes accessed | tf_op | source)
XLA Modules:
  0.0 42.1 jit_solution(12287304346533790169)
XLA Ops:
  0.0 1.0 %pack.1.refs_0_ = f32[520,128]{1,0:T(8,128)S(1)} custom-call(f32[64,1024]{1,0:T(8,128)} %bitcast.4, s32[1,16]{1,0:T(1,128)} %bitcast.5, s32[1,16]{1,0:T(1,128)} %bitcast.6), custom_call_target="tpu_custom_call" | custom-call | tf_op jit(solution)/shard_map/pack/pallas_call | solution.py:67
  1.0 3.0 %collective-permute-start.2 = (f32[520,128]{1,0:T(8,128)S(1)}, f32[520,128]{1,0:T(8,128)S(1)}, u32[]{:S(2)}, u32[]{:S(2)}) collective-permute-start(f32[520,128]{1,0:T(8,128)S(1)} %pack.1.refs_0_), channel_id=1, source_target_pairs={{0,16},{4,20},{8,24},{12,28},{16,0},{20,4},{24,8},{28,12},{1,17},{... | collective-permute-start | bytes 798728 | tf_op jit(solution)/shard_map/ppermute | solution.py:236
  4.0 1.5 %collective-permute-start.1 = (f32[520,128]{1,0:T(8,128)S(1)}, f32[520,128]{1,0:T(8,128)S(1)}, u32[]{:S(2)}, u32[]{:S(2)}) collective-permute-start(f32[520,128]{1,0:T(8,128)S(1)} %pack.1.refs_0_), channel_id=1, source_target_pairs={{0,8},{4,12},{8,0},{12,4},{16,24},{20,28},{24,16},{28,20},{1,9},{5... | collective-permute-start | bytes 798728 | tf_op jit(solution)/shard_map/ppermute | solution.py:236
  5.5 0.0 collective-permute-start.3
  5.5 0.0 collective-permute-start
  5.6 1.6 %prepare.1 = (bf16[32,128,192]{2,1,0:T(8,128)(2,1)S(1)}, s32[32,128]{1,0:T(8,128)S(1)}) custom-call(s32[1]{0:T(128)} %bitcast.place_ref, s32[1,32]{1,0:T(1,128)} %names_in.1, f32[128,2048]{1,0:T(8,128)} %amp_ref.1), custom_call_target="tpu_custom_call" | custom-call | flops 100 | bytes 100 | tf_op jit(solution)/shard_map/prepare/pallas_call | solution.py:123
  7.1 1.2 %products.4 = (f32[16,2048]{1,0:T(8,128)S(1)}, f32[16,2048]{1,0:T(8,128)S(1)}, f32[16,2048]{1,0:T(8,128)S(1)}, f32[16,2048]{1,0:T(8,128)S(1)}, f32[16,2048]{1,0:...) custom-call(s32[32,128]{1,0:T(8,128)S(1)} %get-tuple-element.64.names_ref, ...), custom_call_target="tpu_custom_call" | custom-call | flops 100 | bytes 100 | tf_op jit(solution)/shard_map/products/pallas_call | solution.py:196
  8.4 2.1 %collective-permute-done.2.refs_1_ = f32[520,128]{1,0:T(8,128)S(1)} collective-permute-done((f32[520,128]{1,0:T(8,128)S(1)}, f32[520,128]{1,0:T(8,128)S(1)}, u32[]{:S(2)}, u32[]{:S(2)}) %collective-permute-start.2) | collective-permute-done | bytes 266272 | tf_op jit(solution)/shard_map/ppermute | solution.py:236
  10.4 2.9 %collective-permute-done.1.refs_0_ = f32[520,128]{1,0:T(8,128)S(1)} collective-permute-done((f32[520,128]{1,0:T(8,128)S(1)}, f32[520,128]{1,0:T(8,128)S(1)}, u32[]{:S(2)}, u32[]{:S(2)}) %collective-permute-start.1) | collective-permute-done | bytes 266272 | tf_op jit(solution)/shard_map/ppermute | solution.py:236
  13.3 0.0 collective-permute-start.5
  13.4 0.5 %collective-permute-start.6 = (f32[520,128]{1,0:T(8,128)S(1)}, f32[520,128]{1,0:T(8,128)S(1)}, u32[]{:S(2)}, u32[]{:S(2)}) collective-permute-start(f32[520,128]{1,0:T(8,128)S(1)} %collective-permute-done.2.refs_1_), channel_id=1, source_target_pairs={{0,4},{4,0},{8,12},{12,8},{16,20},{20,16},{24,28},{28,24},{1,5},{5... | collective-permute-start | bytes 798728 | tf_op jit(solution)/shard_map/ppermute | solution.py:236
  13.9 0.0 collective-permute-done.3.refs_2_
  13.9 1.8 %products.5 = (f32[16,2048]{1,0:T(8,128)S(1)}, f32[16,2048]{1,0:T(8,128)S(1)}, f32[16,2048]{1,0:T(8,128)S(1)}, f32[16,2048]{1,0:T(8,128)S(1)}, f32[16,2048]{1,0:...) custom-call(s32[32,128]{1,0:T(8,128)S(1)} %get-tuple-element.64.name, ...), custom_call_target="tpu_custom_call", output_to_operand_aliasing={{0}: (5, {}), {1}: (6, {}), {2}: (7, {}), {3}: (8, {}), {4}... | custom-call | flops 100 | bytes 100 | tf_op jit(solution)/shard_map/products/pallas_call | solution.py:196
  15.6 1.7 %collective-permute-done.refs_2_ = f32[520,128]{1,0:T(8,128)S(1)} collective-permute-done((f32[520,128]{1,0:T(8,128)S(1)}, f32[520,128]{1,0:T(8,128)S(1)}, u32[]{:S(2)}, u32[]{:S(2)}) %collective-permute-start) | collective-permute-done | bytes 266272 | tf_op jit(solution)/shard_map/ppermute | solution.py:236
  17.4 0.0 collective-permute-start.4
  17.4 0.0 collective-permute-done.5.refs_0_
  17.4 0.0 collective-permute-done.6.refs_1_
  17.4 1.8 %products.6 = (f32[16,2048]{1,0:T(8,128)S(1)}, f32[16,2048]{1,0:T(8,128)S(1)}, f32[16,2048]{1,0:T(8,128)S(1)}, f32[16,2048]{1,0:T(8,128)S(1)}, f32[16,2048]{1,0:...) custom-call(s32[32,128]{1,0:T(8,128)S(1)} %get-tuple-element.64.name, ...), custom_call_target="tpu_custom_call", output_to_operand_aliasing={{0}: (5, {}), {1}: (6, {}), {2}: (7, {}), {3}: (8, {}), {4}... | custom-call | flops 100 | bytes 100 | tf_op jit(solution)/shard_map/products/pallas_call | solution.py:196
  19.2 0.0 collective-permute-done.4.refs_0_
  19.2 1.2 %products.7 = (f32[16,2048]{1,0:T(8,128)S(1)}, f32[16,2048]{1,0:T(8,128)S(1)}, f32[16,2048]{1,0:T(8,128)S(1)}, f32[16,2048]{1,0:T(8,128)S(1)}, f32[16,2048]{1,0:...) custom-call(s32[32,128]{1,0:T(8,128)S(1)} %get-tuple-element.64.name, ...), custom_call_target="tpu_custom_call", output_to_operand_aliasing={{0}: (3, {}), {1}: (4, {}), {2}: (5, {}), {3}: (6, {}), {4}... | custom-call | flops 100 | bytes 100 | tf_op jit(solution)/shard_map/products/pallas_call | solution.py:196
  20.4 1.8 %collective-permute-start.7 = (f32[16,2048]{1,0:T(8,128)S(1)}, f32[16,2048]{1,0:T(8,128)S(1)}, u32[]{:S(2)}, u32[]{:S(2)}) collective-permute-start(f32[16,2048]{1,0:T(8,128)S(1)} %get-tuple-element.110), channel_id=1, source_target_pairs={{0,1},{1,0},{2,3},{3,2},{4,5},{5,4},{6,7},{7,6},{8,9},{9,8},{10,11... | collective-permute-start | bytes 393224 | tf_op jit(solution)/shard_map/ppermute | solution.py:239
  22.2 0.3 collective-permute-start.10
  22.5 4.3 %collective-permute-done.7.more_ref = f32[16,2048]{1,0:T(8,128)S(1)} collective-permute-done((f32[16,2048]{1,0:T(8,128)S(1)}, f32[16,2048]{1,0:T(8,128)S(1)}, u32[]{:S(2)}, u32[]{:S(2)}) %collective-permute-start.7) | collective-permute-done | bytes 131104 | tf_op jit(solution)/shard_map/ppermute | solution.py:239
  26.8 2.8 %collective-permute-start.9 = (f32[16,2048]{1,0:T(8,128)S(1)}, f32[16,2048]{1,0:T(8,128)S(1)}, u32[]{:S(2)}, u32[]{:S(2)}) collective-permute-start(f32[16,2048]{1,0:T(8,128)S(1)} %added.4), channel_id=1, source_target_pairs={{0,2},{1,3},{2,0},{3,1},{4,6},{5,7},{6,4},{7,5},{8,10},{9,11},{10,... | collective-permute-start | bytes 393224 | tf_op jit(solution)/shard_map/ppermute | solution.py:239
  29.6 1.6 %collective-permute-start.8 = (f32[16,2048]{1,0:T(8,128)S(1)}, f32[16,2048]{1,0:T(8,128)S(1)}, u32[]{:S(2)}, u32[]{:S(2)}) collective-permute-start(f32[16,2048]{1,0:T(8,128)S(1)} %get-tuple-element.113), channel_id=1, source_target_pairs={{0,1},{1,0},{2,3},{3,2},{4,5},{5,4},{6,7},{7,6},{8,9},{9,8},{10,11... | collective-permute-start | bytes 393224 | tf_op jit(solution)/shard_map/ppermute | solution.py:239
  31.2 0.0 collective-permute-done.10.more_ref
  31.2 1.2 %collective-permute-start.11 = (f32[16,2048]{1,0:T(8,128)S(1)}, f32[16,2048]{1,0:T(8,128)S(1)}, u32[]{:S(2)}, u32[]{:S(2)}) collective-permute-start(f32[16,2048]{1,0:T(8,128)S(1)} %added.6), channel_id=1, source_target_pairs={{0,2},{1,3},{2,0},{3,1},{4,6},{5,7},{6,4},{7,5},{8,10},{9,11},{10,... | collective-permute-start | bytes 393224 | tf_op jit(solution)/shard_map/ppermute | solution.py:239
  32.4 1.5 %collective-permute-start.12 = (f32[16,2048]{1,0:T(8,128)S(1)}, f32[16,2048]{1,0:T(8,128)S(1)}, u32[]{:S(2)}, u32[]{:S(2)}) collective-permute-start(f32[16,2048]{1,0:T(8,128)S(1)} %get-tuple-element.122), channel_id=1, source_target_pairs={{0,1},{1,0},{2,3},{3,2},{4,5},{5,4},{6,7},{7,6},{8,9},{9,8},{10,11... | collective-permute-start | bytes 393224 | tf_op jit(solution)/shard_map/ppermute | solution.py:239
  33.8 3.1 %collective-permute-done.9.more_ref = f32[16,2048]{1,0:T(8,128)S(1)} collective-permute-done((f32[16,2048]{1,0:T(8,128)S(1)}, f32[16,2048]{1,0:T(8,128)S(1)}, u32[]{:S(2)}, u32[]{:S(2)}) %collective-permute-start.9) | collective-permute-done | bytes 131104 | tf_op jit(solution)/shard_map/ppermute | solution.py:239
  37.0 1.2 %collective-permute-done.8 = f32[16,2048]{1,0:T(8,128)S(1)} collective-permute-done((f32[16,2048]{1,0:T(8,128)S(1)}, f32[16,2048]{1,0:T(8,128)S(1)}, u32[]{:S(2)}, u32[]{:S(2)}) %collective-permute-start.8) | collective-permute-done | bytes 131104 | tf_op jit(solution)/shard_map/ppermute | solution.py:239
  38.2 3.0 %collective-permute-done.11.more_ref = f32[16,2048]{1,0:T(8,128)S(1)} collective-permute-done((f32[16,2048]{1,0:T(8,128)S(1)}, f32[16,2048]{1,0:T(8,128)S(1)}, u32[]{:S(2)}, u32[]{:S(2)}) %collective-permute-start.11) | collective-permute-done | bytes 131104 | tf_op jit(solution)/shard_map/ppermute | solution.py:239
  41.2 0.1 collective-permute-done.12
  41.3 0.7 %maximum_add_fusion = f32[32,2048]{1,0:T(8,128)} fusion(f32[16,2048]{1,0:T(8,128)S(1)} %added.7, f32[16,2048]{1,0:T(8,128)S(1)} %added.5, f32[16,2048]{1,0:T(8,128)S(1)} %collective-permute-done.12, f32[16,2048]{1,0:T(8,128)S(1)} %collective-permute-done.8), kind=kLoop, calls=%fused_computation | loop fusion | flops 196608 | bytes 786432 | tf_op jit(solution)/shard_map/add | solution.py:286
  (4 shorter events, 0.1 us)
Async XLA Ops:
  1.0 9.4 %collective-permute-start.2 = (f32[520,128]{1,0:T(8,128)S(1)}, f32[520,128]{1,0:T(8,128)S(1)}, u32[]{:S(2)}, u32[]{:S(2)}) collective-permute-start(f32[520,128]{1,0:T(8,128)S(1)} %pack.1.refs_0_), channel_id=1, source_target_pairs={{0,16},{4,20},{8,24},{12,28},{16,0},{20,4},{24,8},{28,12},{1,17},{... | collective-permute-start | bytes 798728 | tf_op jit(solution)/shard_map/ppermute | solution.py:236
  4.0 9.3 %collective-permute-start.1 = (f32[520,128]{1,0:T(8,128)S(1)}, f32[520,128]{1,0:T(8,128)S(1)}, u32[]{:S(2)}, u32[]{:S(2)}) collective-permute-start(f32[520,128]{1,0:T(8,128)S(1)} %pack.1.refs_0_), channel_id=1, source_target_pairs={{0,8},{4,12},{8,0},{12,4},{16,24},{20,28},{24,16},{28,20},{1,9},{5... | collective-permute-start | bytes 798728 | tf_op jit(solution)/shard_map/ppermute | solution.py:236
  5.5 8.3 %collective-permute-start.3 = (f32[520,128]{1,0:T(8,128)S(1)}, f32[520,128]{1,0:T(8,128)S(1)}, u32[]{:S(2)}, u32[]{:S(2)}) collective-permute-start(f32[520,128]{1,0:T(8,128)S(1)} %pack.1.refs_0_), channel_id=1, source_target_pairs={{0,4},{4,0},{8,12},{12,8},{16,20},{20,16},{24,28},{28,24},{1,5},{5... | collective-permute-start | bytes 798728 | tf_op jit(solution)/shard_map/ppermute | solution.py:236
  5.5 11.9 %collective-permute-start = (f32[520,128]{1,0:T(8,128)S(1)}, f32[520,128]{1,0:T(8,128)S(1)}, u32[]{:S(2)}, u32[]{:S(2)}) collective-permute-start(f32[520,128]{1,0:T(8,128)S(1)} %pack.1.refs_0_), channel_id=1, source_target_pairs={{0,24},{4,28},{8,16},{12,20},{16,8},{20,12},{24,0},{28,4},{1,25},{... | collective-permute-start | bytes 798728 | tf_op jit(solution)/shard_map/ppermute | solution.py:236
  13.3 4.0 %collective-permute-start.5 = (f32[520,128]{1,0:T(8,128)S(1)}, f32[520,128]{1,0:T(8,128)S(1)}, u32[]{:S(2)}, u32[]{:S(2)}) collective-permute-start(f32[520,128]{1,0:T(8,128)S(1)} %collective-permute-done.1.refs_0_), channel_id=1, source_target_pairs={{0,4},{4,0},{8,12},{12,8},{16,20},{20,16},{24,28},{28,24},{1,5},{5... | collective-permute-start | bytes 798728 | tf_op jit(solution)/shard_map/ppermute | solution.py:236
  13.4 4.0 %collective-permute-start.6 = (f32[520,128]{1,0:T(8,128)S(1)}, f32[520,128]{1,0:T(8,128)S(1)}, u32[]{:S(2)}, u32[]{:S(2)}) collective-permute-start(f32[520,128]{1,0:T(8,128)S(1)} %collective-permute-done.2.refs_1_), channel_id=1, source_target_pairs={{0,4},{4,0},{8,12},{12,8},{16,20},{20,16},{24,28},{28,24},{1,5},{5... | collective-permute-start | bytes 798728 | tf_op jit(solution)/shard_map/ppermute | solution.py:236
  17.4 1.8 %collective-permute-start.4 = (f32[520,128]{1,0:T(8,128)S(1)}, f32[520,128]{1,0:T(8,128)S(1)}, u32[]{:S(2)}, u32[]{:S(2)}) collective-permute-start(f32[520,128]{1,0:T(8,128)S(1)} %collective-permute-done.refs_2_), channel_id=1, source_target_pairs={{0,4},{4,0},{8,12},{12,8},{16,20},{20,16},{24,28},{28,24},{1,5},{5... | collective-permute-start | bytes 798728 | tf_op jit(solution)/shard_map/ppermute | solution.py:236
  20.4 6.4 %collective-permute-start.7 = (f32[16,2048]{1,0:T(8,128)S(1)}, f32[16,2048]{1,0:T(8,128)S(1)}, u32[]{:S(2)}, u32[]{:S(2)}) collective-permute-start(f32[16,2048]{1,0:T(8,128)S(1)} %get-tuple-element.110), channel_id=1, source_target_pairs={{0,1},{1,0},{2,3},{3,2},{4,5},{5,4},{6,7},{7,6},{8,9},{9,8},{10,11... | collective-permute-start | bytes 393224 | tf_op jit(solution)/shard_map/ppermute | solution.py:239
  22.2 9.0 %collective-permute-start.10 = (f32[16,2048]{1,0:T(8,128)S(1)}, f32[16,2048]{1,0:T(8,128)S(1)}, u32[]{:S(2)}, u32[]{:S(2)}) collective-permute-start(f32[16,2048]{1,0:T(8,128)S(1)} %get-tuple-element.120), channel_id=1, source_target_pairs={{0,1},{1,0},{2,3},{3,2},{4,5},{5,4},{6,7},{7,6},{8,9},{9,8},{10,11... | collective-permute-start | bytes 393224 | tf_op jit(solution)/shard_map/ppermute | solution.py:239
  26.8 10.1 %collective-permute-start.9 = (f32[16,2048]{1,0:T(8,128)S(1)}, f32[16,2048]{1,0:T(8,128)S(1)}, u32[]{:S(2)}, u32[]{:S(2)}) collective-permute-start(f32[16,2048]{1,0:T(8,128)S(1)} %added.4), channel_id=1, source_target_pairs={{0,2},{1,3},{2,0},{3,1},{4,6},{5,7},{6,4},{7,5},{8,10},{9,11},{10,... | collective-permute-start | bytes 393224 | tf_op jit(solution)/shard_map/ppermute | solution.py:239
  29.6 8.6 %collective-permute-start.8 = (f32[16,2048]{1,0:T(8,128)S(1)}, f32[16,2048]{1,0:T(8,128)S(1)}, u32[]{:S(2)}, u32[]{:S(2)}) collective-permute-start(f32[16,2048]{1,0:T(8,128)S(1)} %get-tuple-element.113), channel_id=1, source_target_pairs={{0,1},{1,0},{2,3},{3,2},{4,5},{5,4},{6,7},{7,6},{8,9},{9,8},{10,11... | collective-permute-start | bytes 393224 | tf_op jit(solution)/shard_map/ppermute | solution.py:239
  31.2 10.0 %collective-permute-start.11 = (f32[16,2048]{1,0:T(8,128)S(1)}, f32[16,2048]{1,0:T(8,128)S(1)}, u32[]{:S(2)}, u32[]{:S(2)}) collective-permute-start(f32[16,2048]{1,0:T(8,128)S(1)} %added.6), channel_id=1, source_target_pairs={{0,2},{1,3},{2,0},{3,1},{4,6},{5,7},{6,4},{7,5},{8,10},{9,11},{10,... | collective-permute-start | bytes 393224 | tf_op jit(solution)/shard_map/ppermute | solution.py:239
  32.4 9.0 %collective-permute-start.12 = (f32[16,2048]{1,0:T(8,128)S(1)}, f32[16,2048]{1,0:T(8,128)S(1)}, u32[]{:S(2)}, u32[]{:S(2)}) collective-permute-start(f32[16,2048]{1,0:T(8,128)S(1)} %get-tuple-element.122), channel_id=1, source_target_pairs={{0,1},{1,0},{2,3},{3,2},{4,5},{5,4},{6,7},{7,6},{8,9},{9,8},{10,11... | collective-permute-start | bytes 393224 | tf_op jit(solution)/shard_map/ppermute | solution.py:239

commit v4 on v3

--- a/solution.py
+++ b/solution.py
@@ -141,8 +141,8 @@
 
 def product_kernel(n_in, n_outs, first, side, count, names_ref, three_ref, *refs):
     packs = refs[:n_in]
-    outs = refs[-n_outs - 3 : -3]
-    numbers, words, sem = refs[-3:]
+    outs = refs[-n_outs:]
+    words = []
     rows = count // 2 * side + 8
     parts = [(pack, base) for pack in packs for base in range(0, pack.shape[0], rows)]
     slots = names_ref.shape[0]
@@ -151,20 +151,17 @@
         row = pack[base + rows - 8 : base + rows - 7, :].astype(jnp.int32)
         slot = jnp.sum(jnp.where(names_ref[...] == row, slot_id, 0), axis=0, keepdims=True)
         col = pack[base + rows - 7 : base + rows - 6, :].astype(jnp.int32)
-        numbers[j : j + 1, :] = slot * AB_TILES + col
-    copy = pltpu.make_async_copy(numbers, words, sem)
-    copy.start()
+        words.append(slot * AB_TILES + col)
     if first:
         for out_ref in outs:
             out_ref[...] = jnp.zeros_like(out_ref)
-    copy.wait()
 
     lane = lax.broadcasted_iota(jnp.int32, (1, LANES), 1)
     tiles = [(j, t) for j in range(len(parts)) for t in range(count)]
     for start in range(0, len(tiles), UNROLL):
         products = []
         for j, t in tiles[start : start + UNROLL]:
-            word = words[j, t]
+            word = words[j][0, t]
             col = word & (AB_TILES - 1)
             slot = word // AB_TILES
             goal = col & 1
@@ -199,11 +196,6 @@
         in_specs=[VMEM] * (2 + n_in + len(carried)),
         out_specs=[VMEM] * len(heights),
         input_output_aliases={2 + n_in + b: b for b in range(len(carried))},
-        scratch_shapes=[
-            pltpu.VMEM((8, LANES), jnp.int32),
-            pltpu.SMEM((8, LANES), jnp.int32),
-            pltpu.SemaphoreType.DMA,
-        ],
         compiler_params=PARAMS,
         name="products",
         cost_estimate=pl.CostEstimate(flops=100, bytes_accessed=100, transcendentals=0),

time: 42.2 us -> 41 us (0.972)
  Pallas kernels: 8.62 us -> 6.14 us
  waiting for transfers between devices: 18.4 us -> 19.6 us
    pallas_call x4, Pallas kernels: 5.96 us -> 3.49 us  [accumulate(): pl.pallas_call(functools.partial(product_kernel, n_in, len(heights), tota...]
    ppermute x7, waiting for transfers between devices: 6.73 us -> 8.33 us  [swap(): return lax.ppermute(value, 'occ', [(i, i ^ mask) for i in range(n_occ)])]
    ppermute x6, waiting for transfers between devices: 11.7 us -> 11.3 us  [along(): return lax.ppermute(value, 'vir', [(i, i ^ mask) for i in range(n_vir)])]
  transfers between devices with their start and end apart: 13 -> 13, of which waited for: 8 -> 9; matrix products, arithmetic and copies ran while one was open for 0% -> 0% of each run, Pallas kernels for 15% -> 11%
where the time goes in v4:
time: 41 us; the launch traced here: 40.8 us
  waiting for transfers between devices  19.6 us (48%)
  starting transfers between devices  14.2 us (35%)
  Pallas kernels  6.14 us (15%)
  other arithmetic  0.74 us (2%)
    ppermute x6, waiting for transfers between devices, along(): return lax.ppermute(value, 'vir', [(i, i ^ mask) for i in range(n_vir)])  11.3 us
    ppermute x6, starting transfers between devices, along(): return lax.ppermute(value, 'vir', [(i, i ^ mask) for i in range(n_vir)])  9.16 us
    ppermute x7, waiting for transfers between devices, swap(): return lax.ppermute(value, 'occ', [(i, i ^ mask) for i in range(n_occ)])  8.33 us
    ppermute x7, starting transfers between devices, swap(): return lax.ppermute(value, 'occ', [(i, i ^ mask) for i in range(n_occ)])  5.09 us
    pallas_call x4, Pallas kernels, accumulate(): pl.pallas_call(functools.partial(product_kernel, n_in, len(heights), tota...  3.49 us
    pallas_call x1, Pallas kernels, prepare(): pl.pallas_call(functools.partial(prepare_kernel, n_blocks, side), out_sha...  1.56 us
    pallas_call x1, Pallas kernels, pack(): pl.pallas_call(pack_kernel, out_shape=pltpu.VMEM((groups * side + PARTS *...  0.99 us
  transfers between devices with their start and end apart: 13, of which 9 were waited for; matrix products, arithmetic and copies ran while one was open for 0% of the time, Pallas kernels for 11%

profile of v4, /device:TPU:0, one launch (start us, length us, event | category | flops | bytes accessed | tf_op | source)
XLA Modules:
  0.0 40.8 jit_solution(2833804537668815729)
XLA Ops:
  0.0 1.0 %pack.1.refs_0_ = f32[520,128]{1,0:T(8,128)S(1)} custom-call(f32[64,1024]{1,0:T(8,128)} %bitcast.4, s32[1,16]{1,0:T(1,128)} %bitcast.5, s32[1,16]{1,0:T(1,128)} %bitcast.6), custom_call_target="tpu_custom_call" | custom-call | tf_op jit(solution)/shard_map/pack/pallas_call | solution.py:67
  1.0 3.0 %collective-permute-start.2 = (f32[520,128]{1,0:T(8,128)S(1)}, f32[520,128]{1,0:T(8,128)S(1)}, u32[]{:S(2)}, u32[]{:S(2)}) collective-permute-start(f32[520,128]{1,0:T(8,128)S(1)} %pack.1.refs_0_), channel_id=1, source_target_pairs={{0,16},{4,20},{8,24},{12,28},{16,0},{20,4},{24,8},{28,12},{1,17},{... | collective-permute-start | bytes 798728 | tf_op jit(solution)/shard_map/ppermute | solution.py:228
  4.0 1.5 %collective-permute-start.1 = (f32[520,128]{1,0:T(8,128)S(1)}, f32[520,128]{1,0:T(8,128)S(1)}, u32[]{:S(2)}, u32[]{:S(2)}) collective-permute-start(f32[520,128]{1,0:T(8,128)S(1)} %pack.1.refs_0_), channel_id=1, source_target_pairs={{0,8},{4,12},{8,0},{12,4},{16,24},{20,28},{24,16},{28,20},{1,9},{5... | collective-permute-start | bytes 798728 | tf_op jit(solution)/shard_map/ppermute | solution.py:228
  5.5 0.0 collective-permute-start.3
  5.5 0.0 collective-permute-start
  5.6 1.6 %prepare.1 = (bf16[32,128,192]{2,1,0:T(8,128)(2,1)S(1)}, s32[32,128]{1,0:T(8,128)S(1)}) custom-call(s32[1]{0:T(128)} %bitcast.place_ref, s32[1,32]{1,0:T(1,128)} %names_in.1, f32[128,2048]{1,0:T(8,128)} %amp_ref.1), custom_call_target="tpu_custom_call" | custom-call | flops 100 | bytes 100 | tf_op jit(solution)/shard_map/prepare/pallas_call | solution.py:123
  7.1 0.6 %products.4 = (f32[16,2048]{1,0:T(8,128)S(1)}, f32[16,2048]{1,0:T(8,128)S(1)}, f32[16,2048]{1,0:T(8,128)S(1)}, f32[16,2048]{1,0:T(8,128)S(1)}, f32[16,2048]{1,0:...) custom-call(s32[32,128]{1,0:T(8,128)S(1)} %get-tuple-element.64.names_ref, ...), custom_call_target="tpu_custom_call" | custom-call | flops 100 | bytes 100 | tf_op jit(solution)/shard_map/products/pallas_call | solution.py:193
  7.7 2.7 %collective-permute-done.2.refs_1_ = f32[520,128]{1,0:T(8,128)S(1)} collective-permute-done((f32[520,128]{1,0:T(8,128)S(1)}, f32[520,128]{1,0:T(8,128)S(1)}, u32[]{:S(2)}, u32[]{:S(2)}) %collective-permute-start.2) | collective-permute-done | bytes 266272 | tf_op jit(solution)/shard_map/ppermute | solution.py:228
  10.4 2.9 %collective-permute-done.1.refs_0_ = f32[520,128]{1,0:T(8,128)S(1)} collective-permute-done((f32[520,128]{1,0:T(8,128)S(1)}, f32[520,128]{1,0:T(8,128)S(1)}, u32[]{:S(2)}, u32[]{:S(2)}) %collective-permute-start.1) | collective-permute-done | bytes 266272 | tf_op jit(solution)/shard_map/ppermute | solution.py:228
  13.3 0.0 collective-permute-start.5
  13.4 0.5 %collective-permute-start.6 = (f32[520,128]{1,0:T(8,128)S(1)}, f32[520,128]{1,0:T(8,128)S(1)}, u32[]{:S(2)}, u32[]{:S(2)}) collective-permute-start(f32[520,128]{1,0:T(8,128)S(1)} %collective-permute-done.2.refs_1_), channel_id=1, source_target_pairs={{0,4},{4,0},{8,12},{12,8},{16,20},{20,16},{24,28},{28,24},{1,5},{5... | collective-permute-start | bytes 798728 | tf_op jit(solution)/shard_map/ppermute | solution.py:228
  13.9 0.0 collective-permute-done.3.refs_2_
  13.9 1.2 %products.5 = (f32[16,2048]{1,0:T(8,128)S(1)}, f32[16,2048]{1,0:T(8,128)S(1)}, f32[16,2048]{1,0:T(8,128)S(1)}, f32[16,2048]{1,0:T(8,128)S(1)}, f32[16,2048]{1,0:...) custom-call(s32[32,128]{1,0:T(8,128)S(1)} %get-tuple-element.64.name, ...), custom_call_target="tpu_custom_call", output_to_operand_aliasing={{0}: (5, {}), {1}: (6, {}), {2}: (7, {}), {3}: (8, {}), {4}... | custom-call | flops 100 | bytes 100 | tf_op jit(solution)/shard_map/products/pallas_call | solution.py:193
  15.0 2.4 %collective-permute-done.refs_2_ = f32[520,128]{1,0:T(8,128)S(1)} collective-permute-done((f32[520,128]{1,0:T(8,128)S(1)}, f32[520,128]{1,0:T(8,128)S(1)}, u32[]{:S(2)}, u32[]{:S(2)}) %collective-permute-start) | collective-permute-done | bytes 266272 | tf_op jit(solution)/shard_map/ppermute | solution.py:228
  17.4 0.0 collective-permute-start.4
  17.4 0.0 collective-permute-done.5.refs_0_
  17.4 0.0 collective-permute-done.6.refs_1_
  17.4 1.2 %products.6 = (f32[16,2048]{1,0:T(8,128)S(1)}, f32[16,2048]{1,0:T(8,128)S(1)}, f32[16,2048]{1,0:T(8,128)S(1)}, f32[16,2048]{1,0:T(8,128)S(1)}, f32[16,2048]{1,0:...) custom-call(s32[32,128]{1,0:T(8,128)S(1)} %get-tuple-element.64.name, ...), custom_call_target="tpu_custom_call", output_to_operand_aliasing={{0}: (5, {}), {1}: (6, {}), {2}: (7, {}), {3}: (8, {}), {4}... | custom-call | flops 100 | bytes 100 | tf_op jit(solution)/shard_map/products/pallas_call | solution.py:193
  18.6 0.3 collective-permute-done.4.refs_0_
  18.9 0.6 %products.7 = (f32[16,2048]{1,0:T(8,128)S(1)}, f32[16,2048]{1,0:T(8,128)S(1)}, f32[16,2048]{1,0:T(8,128)S(1)}, f32[16,2048]{1,0:T(8,128)S(1)}, f32[16,2048]{1,0:...) custom-call(s32[32,128]{1,0:T(8,128)S(1)} %get-tuple-element.64.name, ...), custom_call_target="tpu_custom_call", output_to_operand_aliasing={{0}: (3, {}), {1}: (4, {}), {2}: (5, {}), {3}: (6, {}), {4}... | custom-call | flops 100 | bytes 100 | tf_op jit(solution)/shard_map/products/pallas_call | solution.py:193
  19.5 1.8 %collective-permute-start.7 = (f32[16,2048]{1,0:T(8,128)S(1)}, f32[16,2048]{1,0:T(8,128)S(1)}, u32[]{:S(2)}, u32[]{:S(2)}) collective-permute-start(f32[16,2048]{1,0:T(8,128)S(1)} %get-tuple-element.110), channel_id=1, source_target_pairs={{0,1},{1,0},{2,3},{3,2},{4,5},{5,4},{6,7},{7,6},{8,9},{9,8},{10,11... | collective-permute-start | bytes 393224 | tf_op jit(solution)/shard_map/ppermute | solution.py:231
  21.3 0.3 collective-permute-start.10
  21.6 4.3 %collective-permute-done.7.more_ref = f32[16,2048]{1,0:T(8,128)S(1)} collective-permute-done((f32[16,2048]{1,0:T(8,128)S(1)}, f32[16,2048]{1,0:T(8,128)S(1)}, u32[]{:S(2)}, u32[]{:S(2)}) %collective-permute-start.7) | collective-permute-done | bytes 131104 | tf_op jit(solution)/shard_map/ppermute | solution.py:231
  25.9 2.8 %collective-permute-start.9 = (f32[16,2048]{1,0:T(8,128)S(1)}, f32[16,2048]{1,0:T(8,128)S(1)}, u32[]{:S(2)}, u32[]{:S(2)}) collective-permute-start(f32[16,2048]{1,0:T(8,128)S(1)} %added.4), channel_id=1, source_target_pairs={{0,2},{1,3},{2,0},{3,1},{4,6},{5,7},{6,4},{7,5},{8,10},{9,11},{10,... | collective-permute-start | bytes 393224 | tf_op jit(solution)/shard_map/ppermute | solution.py:231
  28.7 1.6 %collective-permute-start.8 = (f32[16,2048]{1,0:T(8,128)S(1)}, f32[16,2048]{1,0:T(8,128)S(1)}, u32[]{:S(2)}, u32[]{:S(2)}) collective-permute-start(f32[16,2048]{1,0:T(8,128)S(1)} %get-tuple-element.113), channel_id=1, source_target_pairs={{0,1},{1,0},{2,3},{3,2},{4,5},{5,4},{6,7},{7,6},{8,9},{9,8},{10,11... | collective-permute-start | bytes 393224 | tf_op jit(solution)/shard_map/ppermute | solution.py:231
  30.3 0.0 collective-permute-done.10.more_ref
  30.3 1.2 %collective-permute-start.11 = (f32[16,2048]{1,0:T(8,128)S(1)}, f32[16,2048]{1,0:T(8,128)S(1)}, u32[]{:S(2)}, u32[]{:S(2)}) collective-permute-start(f32[16,2048]{1,0:T(8,128)S(1)} %added.6), channel_id=1, source_target_pairs={{0,2},{1,3},{2,0},{3,1},{4,6},{5,7},{6,4},{7,5},{8,10},{9,11},{10,... | collective-permute-start | bytes 393224 | tf_op jit(solution)/shard_map/ppermute | solution.py:231
  31.5 1.5 %collective-permute-start.12 = (f32[16,2048]{1,0:T(8,128)S(1)}, f32[16,2048]{1,0:T(8,128)S(1)}, u32[]{:S(2)}, u32[]{:S(2)}) collective-permute-start(f32[16,2048]{1,0:T(8,128)S(1)} %get-tuple-element.122), channel_id=1, source_target_pairs={{0,1},{1,0},{2,3},{3,2},{4,5},{5,4},{6,7},{7,6},{8,9},{9,8},{10,11... | collective-permute-start | bytes 393224 | tf_op jit(solution)/shard_map/ppermute | solution.py:231
  33.0 2.7 %collective-permute-done.9.more_ref = f32[16,2048]{1,0:T(8,128)S(1)} collective-permute-done((f32[16,2048]{1,0:T(8,128)S(1)}, f32[16,2048]{1,0:T(8,128)S(1)}, u32[]{:S(2)}, u32[]{:S(2)}) %collective-permute-start.9) | collective-permute-done | bytes 131104 | tf_op jit(solution)/shard_map/ppermute | solution.py:231
  35.8 2.0 %collective-permute-done.8 = f32[16,2048]{1,0:T(8,128)S(1)} collective-permute-done((f32[16,2048]{1,0:T(8,128)S(1)}, f32[16,2048]{1,0:T(8,128)S(1)}, u32[]{:S(2)}, u32[]{:S(2)}) %collective-permute-start.8) | collective-permute-done | bytes 131104 | tf_op jit(solution)/shard_map/ppermute | solution.py:231
  37.7 1.6 %collective-permute-done.11.more_ref = f32[16,2048]{1,0:T(8,128)S(1)} collective-permute-done((f32[16,2048]{1,0:T(8,128)S(1)}, f32[16,2048]{1,0:T(8,128)S(1)}, u32[]{:S(2)}, u32[]{:S(2)}) %collective-permute-start.11) | collective-permute-done | bytes 131104 | tf_op jit(solution)/shard_map/ppermute | solution.py:231
  39.4 0.6 %collective-permute-done.12 = f32[16,2048]{1,0:T(8,128)S(1)} collective-permute-done((f32[16,2048]{1,0:T(8,128)S(1)}, f32[16,2048]{1,0:T(8,128)S(1)}, u32[]{:S(2)}, u32[]{:S(2)}) %collective-permute-start.12) | collective-permute-done | bytes 131104 | tf_op jit(solution)/shard_map/ppermute | solution.py:231
  40.0 0.7 %maximum_add_fusion = f32[32,2048]{1,0:T(8,128)} fusion(f32[16,2048]{1,0:T(8,128)S(1)} %added.7, f32[16,2048]{1,0:T(8,128)S(1)} %added.5, f32[16,2048]{1,0:T(8,128)S(1)} %collective-permute-done.12, f32[16,2048]{1,0:T(8,128)S(1)} %collective-permute-done.8), kind=kLoop, calls=%fused_computation | loop fusion | flops 196608 | bytes 786432 | tf_op jit(solution)/shard_map/add | solution.py:278
  (4 shorter events, 0.1 us)
Async XLA Ops:
  1.0 9.4 %collective-permute-start.2 = (f32[520,128]{1,0:T(8,128)S(1)}, f32[520,128]{1,0:T(8,128)S(1)}, u32[]{:S(2)}, u32[]{:S(2)}) collective-permute-start(f32[520,128]{1,0:T(8,128)S(1)} %pack.1.refs_0_), channel_id=1, source_target_pairs={{0,16},{4,20},{8,24},{12,28},{16,0},{20,4},{24,8},{28,12},{1,17},{... | collective-permute-start | bytes 798728 | tf_op jit(solution)/shard_map/ppermute | solution.py:228
  4.0 9.3 %collective-permute-start.1 = (f32[520,128]{1,0:T(8,128)S(1)}, f32[520,128]{1,0:T(8,128)S(1)}, u32[]{:S(2)}, u32[]{:S(2)}) collective-permute-start(f32[520,128]{1,0:T(8,128)S(1)} %pack.1.refs_0_), channel_id=1, source_target_pairs={{0,8},{4,12},{8,0},{12,4},{16,24},{20,28},{24,16},{28,20},{1,9},{5... | collective-permute-start | bytes 798728 | tf_op jit(solution)/shard_map/ppermute | solution.py:228
  5.5 8.3 %collective-permute-start.3 = (f32[520,128]{1,0:T(8,128)S(1)}, f32[520,128]{1,0:T(8,128)S(1)}, u32[]{:S(2)}, u32[]{:S(2)}) collective-permute-start(f32[520,128]{1,0:T(8,128)S(1)} %pack.1.refs_0_), channel_id=1, source_target_pairs={{0,4},{4,0},{8,12},{12,8},{16,20},{20,16},{24,28},{28,24},{1,5},{5... | collective-permute-start | bytes 798728 | tf_op jit(solution)/shard_map/ppermute | solution.py:228
  5.5 11.9 %collective-permute-start = (f32[520,128]{1,0:T(8,128)S(1)}, f32[520,128]{1,0:T(8,128)S(1)}, u32[]{:S(2)}, u32[]{:S(2)}) collective-permute-start(f32[520,128]{1,0:T(8,128)S(1)} %pack.1.refs_0_), channel_id=1, source_target_pairs={{0,24},{4,28},{8,16},{12,20},{16,8},{20,12},{24,0},{28,4},{1,25},{... | collective-permute-start | bytes 798728 | tf_op jit(solution)/shard_map/ppermute | solution.py:228
  13.3 4.0 %collective-permute-start.5 = (f32[520,128]{1,0:T(8,128)S(1)}, f32[520,128]{1,0:T(8,128)S(1)}, u32[]{:S(2)}, u32[]{:S(2)}) collective-permute-start(f32[520,128]{1,0:T(8,128)S(1)} %collective-permute-done.1.refs_0_), channel_id=1, source_target_pairs={{0,4},{4,0},{8,12},{12,8},{16,20},{20,16},{24,28},{28,24},{1,5},{5... | collective-permute-start | bytes 798728 | tf_op jit(solution)/shard_map/ppermute | solution.py:228
  13.4 4.0 %collective-permute-start.6 = (f32[520,128]{1,0:T(8,128)S(1)}, f32[520,128]{1,0:T(8,128)S(1)}, u32[]{:S(2)}, u32[]{:S(2)}) collective-permute-start(f32[520,128]{1,0:T(8,128)S(1)} %collective-permute-done.2.refs_1_), channel_id=1, source_target_pairs={{0,4},{4,0},{8,12},{12,8},{16,20},{20,16},{24,28},{28,24},{1,5},{5... | collective-permute-start | bytes 798728 | tf_op jit(solution)/shard_map/ppermute | solution.py:228
  17.4 1.5 %collective-permute-start.4 = (f32[520,128]{1,0:T(8,128)S(1)}, f32[520,128]{1,0:T(8,128)S(1)}, u32[]{:S(2)}, u32[]{:S(2)}) collective-permute-start(f32[520,128]{1,0:T(8,128)S(1)} %collective-permute-done.refs_2_), channel_id=1, source_target_pairs={{0,4},{4,0},{8,12},{12,8},{16,20},{20,16},{24,28},{28,24},{1,5},{5... | collective-permute-start | bytes 798728 | tf_op jit(solution)/shard_map/ppermute | solution.py:228
  19.5 6.4 %collective-permute-start.7 = (f32[16,2048]{1,0:T(8,128)S(1)}, f32[16,2048]{1,0:T(8,128)S(1)}, u32[]{:S(2)}, u32[]{:S(2)}) collective-permute-start(f32[16,2048]{1,0:T(8,128)S(1)} %get-tuple-element.110), channel_id=1, source_target_pairs={{0,1},{1,0},{2,3},{3,2},{4,5},{5,4},{6,7},{7,6},{8,9},{9,8},{10,11... | collective-permute-start | bytes 393224 | tf_op jit(solution)/shard_map/ppermute | solution.py:231
  21.3 9.0 %collective-permute-start.10 = (f32[16,2048]{1,0:T(8,128)S(1)}, f32[16,2048]{1,0:T(8,128)S(1)}, u32[]{:S(2)}, u32[]{:S(2)}) collective-permute-start(f32[16,2048]{1,0:T(8,128)S(1)} %get-tuple-element.120), channel_id=1, source_target_pairs={{0,1},{1,0},{2,3},{3,2},{4,5},{5,4},{6,7},{7,6},{8,9},{9,8},{10,11... | collective-permute-start | bytes 393224 | tf_op jit(solution)/shard_map/ppermute | solution.py:231
  25.9 9.8 %collective-permute-start.9 = (f32[16,2048]{1,0:T(8,128)S(1)}, f32[16,2048]{1,0:T(8,128)S(1)}, u32[]{:S(2)}, u32[]{:S(2)}) collective-permute-start(f32[16,2048]{1,0:T(8,128)S(1)} %added.4), channel_id=1, source_target_pairs={{0,2},{1,3},{2,0},{3,1},{4,6},{5,7},{6,4},{7,5},{8,10},{9,11},{10,... | collective-permute-start | bytes 393224 | tf_op jit(solution)/shard_map/ppermute | solution.py:231
  28.7 9.0 %collective-permute-start.8 = (f32[16,2048]{1,0:T(8,128)S(1)}, f32[16,2048]{1,0:T(8,128)S(1)}, u32[]{:S(2)}, u32[]{:S(2)}) collective-permute-start(f32[16,2048]{1,0:T(8,128)S(1)} %get-tuple-element.113), channel_id=1, source_target_pairs={{0,1},{1,0},{2,3},{3,2},{4,5},{5,4},{6,7},{7,6},{8,9},{9,8},{10,11... | collective-permute-start | bytes 393224 | tf_op jit(solution)/shard_map/ppermute | solution.py:231
  30.3 9.0 %collective-permute-start.11 = (f32[16,2048]{1,0:T(8,128)S(1)}, f32[16,2048]{1,0:T(8,128)S(1)}, u32[]{:S(2)}, u32[]{:S(2)}) collective-permute-start(f32[16,2048]{1,0:T(8,128)S(1)} %added.6), channel_id=1, source_target_pairs={{0,2},{1,3},{2,0},{3,1},{4,6},{5,7},{6,4},{7,5},{8,10},{9,11},{10,... | collective-permute-start | bytes 393224 | tf_op jit(solution)/shard_map/ppermute | solution.py:231
  31.5 8.5 %collective-permute-start.12 = (f32[16,2048]{1,0:T(8,128)S(1)}, f32[16,2048]{1,0:T(8,128)S(1)}, u32[]{:S(2)}, u32[]{:S(2)}) collective-permute-start(f32[16,2048]{1,0:T(8,128)S(1)} %get-tuple-element.122), channel_id=1, source_target_pairs={{0,1},{1,0},{2,3},{3,2},{4,5},{5,4},{6,7},{7,6},{8,9},{9,8},{10,11... | collective-permute-start | bytes 393224 | tf_op jit(solution)/shard_map/ppermute | solution.py:231

commit v5 on v4

--- a/solution.py
+++ b/solution.py
@@ -219,6 +219,26 @@
     )(in_vmem(carried), in_vmem(more))
 
 
+def mix_kernel(flag_ref, far_ref, more_ref, near_ref, first_ref, second_ref):
+    total = far_ref[...] + more_ref[...]
+    near = near_ref[...]
+    inner = flag_ref[0] > 0
+    first_ref[...] = jnp.where(inner, total, near)
+    second_ref[...] = jnp.where(inner, near, total)
+
+
+def mixed(flag, far, more, near):
+    block = pltpu.VMEM(far.shape, far.dtype)
+    return pl.pallas_call(
+        mix_kernel,
+        out_shape=[block, block],
+        in_specs=[SMEM, VMEM, VMEM, VMEM],
+        out_specs=[VMEM, VMEM],
+        compiler_params=PARAMS,
+        name="mixed",
+    )(flag, in_vmem(far), in_vmem(more), in_vmem(near))
+
+
 def local(n_occ, n_vir, amplitudes, amp_cols, integrals, int_rows, int_cols):
     side, width = integrals.shape[2:]
     count = width // side
@@ -261,21 +281,23 @@
 
     blocks = iter(blocks)
     blocks = [[next(blocks) for _ in range(pieces[r])] for r in range(n_vir)]
+    if n_vir == 4:
+        mine, near, away, far = blocks
+        inner = ((place + 1) // 2 == 1).astype(jnp.int32)
+        rings = [(0, 1), (1, 3), (2, 0), (3, 2)], [(0, 2), (1, 0), (2, 3), (3, 1)]
+        come = [along(piece, 1) for piece in far]
+        sent = [mixed(inner, *group) for group in zip(away, come, near)]
+        got = [[lax.ppermute(piece, "vir", ring) for piece, ring in zip(pair, rings)] for pair in sent]
+        upper = added(added(mine[0], got[0][0]), got[0][1])
+        upper, mine[1] = together(upper, mine[1])
+        return jnp.concatenate([upper, added(mine[1], got[1][0]) + got[1][1]], axis=0)
     bit = 1
     while bit < n_vir:
-        for r in range(n_vir - bit, 1, -2 * bit):
+        for r in range(n_vir - bit, 0, -2 * bit):
             got = [along(piece, bit) for piece in blocks[r]]
-            goal = blocks[r ^ bit]
-            goal[0] = added(goal[0], got[0])
-            if r == 2:
-                upper = along(blocks[1][0], 1)
-                upper, goal[0], goal[1] = together(upper, goal[0], goal[1])
-            goal[1] = added(goal[1], got[1])
-        if bit == 1:
-            blocks[2][0], *blocks[1] = together(blocks[2][0], *blocks[1])
+            blocks[r ^ bit] = [added(old, new) for old, new in zip(blocks[r ^ bit], got)]
         bit *= 2
-    lower = along(blocks[1][1], 1)
-    return jnp.concatenate(blocks[0], axis=0) + jnp.concatenate([upper, lower], axis=0)
+    return jnp.concatenate(blocks[0], axis=0)
 
 
 def solution(mesh):

time: 41 us -> 40.3 us (0.983)
  starting transfers between devices: 14.2 us -> 13.1 us
    ppermute x0 -> x4, waiting for transfers between devices: none -> 7.4 us  [local(): lax.ppermute(piece, 'vir', ring)]
    ppermute x6 -> x2, starting transfers between devices: 9.16 us -> 2.09 us  [along(): return lax.ppermute(value, 'vir', [(i, i ^ mask) for i in range(n_vir)])]
    ppermute x6 -> x2, waiting for transfers between devices: 11.3 us -> 4.32 us  [along(): return lax.ppermute(value, 'vir', [(i, i ^ mask) for i in range(n_vir)])]
    ppermute x0 -> x4, starting transfers between devices: none -> 5.95 us  [local(): lax.ppermute(piece, 'vir', ring)]
    add x1, other arithmetic: 0.74 us -> 0.02 us  [local(): added(mine[1], got[1][0]) + got[1][1]]
    concatenate x0 -> x1, other arithmetic: none -> 0.72 us  [local(): jnp.concatenate([upper, added(mine[1], got[1][0]) + got[1][1]], axis=0)]
  transfers between devices with their start and end apart: 13 -> 13, of which waited for: 9 -> 9; matrix products, arithmetic and copies ran while one was open for 0% -> 0% of each run, Pallas kernels for 11% -> 12%
where the time goes in v5:
time: 40.3 us; the launch traced here: 40.1 us
  waiting for transfers between devices  20 us (50%)
  starting transfers between devices  13.1 us (33%)
  Pallas kernels  6.17 us (15%)
  other arithmetic  0.74 us (2%)
    ppermute x7, waiting for transfers between devices, swap(): return lax.ppermute(value, 'occ', [(i, i ^ mask) for i in range(n_occ)])  8.32 us
    ppermute x4, waiting for transfers between devices, local(): lax.ppermute(piece, 'vir', ring)  7.4 us
    ppermute x4, starting transfers between devices, local(): lax.ppermute(piece, 'vir', ring)  5.95 us
    ppermute x7, starting transfers between devices, swap(): return lax.ppermute(value, 'occ', [(i, i ^ mask) for i in range(n_occ)])  5.09 us
    ppermute x2, waiting for transfers between devices, along(): return lax.ppermute(value, 'vir', [(i, i ^ mask) for i in range(n_vir)])  4.32 us
    pallas_call x4, Pallas kernels, accumulate(): pl.pallas_call(functools.partial(product_kernel, n_in, len(heights), tota...  3.49 us
    ppermute x2, starting transfers between devices, along(): return lax.ppermute(value, 'vir', [(i, i ^ mask) for i in range(n_vir)])  2.09 us
    pallas_call x1, Pallas kernels, prepare(): pl.pallas_call(functools.partial(prepare_kernel, n_blocks, side), out_sha...  1.56 us
  transfers between devices with their start and end apart: 13, of which 9 were waited for; matrix products, arithmetic and copies ran while one was open for 0% of the time, Pallas kernels for 12%

profile of v5, /device:TPU:0, one launch (start us, length us, event | category | flops | bytes accessed | tf_op | source)
XLA Modules:
  0.0 40.1 jit_solution(14610825423285880757)
XLA Ops:
  0.0 1.0 %pack.1.refs_0_ = f32[520,128]{1,0:T(8,128)S(1)} custom-call(f32[64,1024]{1,0:T(8,128)} %bitcast.4, s32[1,16]{1,0:T(1,128)} %bitcast.5, s32[1,16]{1,0:T(1,128)} %bitcast.6), custom_call_target="tpu_custom_call" | custom-call | tf_op jit(solution)/shard_map/pack/pallas_call | solution.py:67
  1.0 3.0 %collective-permute-start.2 = (f32[520,128]{1,0:T(8,128)S(1)}, f32[520,128]{1,0:T(8,128)S(1)}, u32[]{:S(2)}, u32[]{:S(2)}) collective-permute-start(f32[520,128]{1,0:T(8,128)S(1)} %pack.1.refs_0_), channel_id=1, source_target_pairs={{0,16},{4,20},{8,24},{12,28},{16,0},{20,4},{24,8},{28,12},{1,17},{... | collective-permute-start | bytes 798728 | tf_op jit(solution)/shard_map/ppermute | solution.py:248
  4.0 1.5 %collective-permute-start.1 = (f32[520,128]{1,0:T(8,128)S(1)}, f32[520,128]{1,0:T(8,128)S(1)}, u32[]{:S(2)}, u32[]{:S(2)}) collective-permute-start(f32[520,128]{1,0:T(8,128)S(1)} %pack.1.refs_0_), channel_id=1, source_target_pairs={{0,8},{4,12},{8,0},{12,4},{16,24},{20,28},{24,16},{28,20},{1,9},{5... | collective-permute-start | bytes 798728 | tf_op jit(solution)/shard_map/ppermute | solution.py:248
  5.5 0.0 collective-permute-start.3
  5.5 0.0 collective-permute-start
  5.6 1.6 %prepare.1 = (bf16[32,128,192]{2,1,0:T(8,128)(2,1)S(1)}, s32[32,128]{1,0:T(8,128)S(1)}) custom-call(s32[1]{0:T(128)} %bitcast.place_ref, s32[1,32]{1,0:T(1,128)} %names_in.1, f32[128,2048]{1,0:T(8,128)} %amp_ref.1), custom_call_target="tpu_custom_call" | custom-call | flops 100 | bytes 100 | tf_op jit(solution)/shard_map/prepare/pallas_call | solution.py:123
  7.1 0.6 %products.4 = (f32[16,2048]{1,0:T(8,128)S(1)}, f32[16,2048]{1,0:T(8,128)S(1)}, f32[16,2048]{1,0:T(8,128)S(1)}, f32[16,2048]{1,0:T(8,128)S(1)}, f32[16,2048]{1,0:...) custom-call(s32[32,128]{1,0:T(8,128)S(1)} %get-tuple-element.64.names_ref, ...), custom_call_target="tpu_custom_call" | custom-call | flops 100 | bytes 100 | tf_op jit(solution)/shard_map/products/pallas_call | solution.py:193
  7.7 2.7 %collective-permute-done.2.refs_1_ = f32[520,128]{1,0:T(8,128)S(1)} collective-permute-done((f32[520,128]{1,0:T(8,128)S(1)}, f32[520,128]{1,0:T(8,128)S(1)}, u32[]{:S(2)}, u32[]{:S(2)}) %collective-permute-start.2) | collective-permute-done | bytes 266272 | tf_op jit(solution)/shard_map/ppermute | solution.py:248
  10.4 2.9 %collective-permute-done.1.refs_0_ = f32[520,128]{1,0:T(8,128)S(1)} collective-permute-done((f32[520,128]{1,0:T(8,128)S(1)}, f32[520,128]{1,0:T(8,128)S(1)}, u32[]{:S(2)}, u32[]{:S(2)}) %collective-permute-start.1) | collective-permute-done | bytes 266272 | tf_op jit(solution)/shard_map/ppermute | solution.py:248
  13.3 0.0 collective-permute-start.5
  13.4 0.5 %collective-permute-start.6 = (f32[520,128]{1,0:T(8,128)S(1)}, f32[520,128]{1,0:T(8,128)S(1)}, u32[]{:S(2)}, u32[]{:S(2)}) collective-permute-start(f32[520,128]{1,0:T(8,128)S(1)} %collective-permute-done.2.refs_1_), channel_id=1, source_target_pairs={{0,4},{4,0},{8,12},{12,8},{16,20},{20,16},{24,28},{28,24},{1,5},{5... | collective-permute-start | bytes 798728 | tf_op jit(solution)/shard_map/ppermute | solution.py:248
  13.9 0.0 collective-permute-done.3.refs_2_
  13.9 1.2 %products.5 = (f32[16,2048]{1,0:T(8,128)S(1)}, f32[16,2048]{1,0:T(8,128)S(1)}, f32[16,2048]{1,0:T(8,128)S(1)}, f32[16,2048]{1,0:T(8,128)S(1)}, f32[16,2048]{1,0:...) custom-call(s32[32,128]{1,0:T(8,128)S(1)} %get-tuple-element.64.name, ...), custom_call_target="tpu_custom_call", output_to_operand_aliasing={{0}: (5, {}), {1}: (6, {}), {2}: (7, {}), {3}: (8, {}), {4}... | custom-call | flops 100 | bytes 100 | tf_op jit(solution)/shard_map/products/pallas_call | solution.py:193
  15.0 2.3 %collective-permute-done.refs_2_ = f32[520,128]{1,0:T(8,128)S(1)} collective-permute-done((f32[520,128]{1,0:T(8,128)S(1)}, f32[520,128]{1,0:T(8,128)S(1)}, u32[]{:S(2)}, u32[]{:S(2)}) %collective-permute-start) | collective-permute-done | bytes 266272 | tf_op jit(solution)/shard_map/ppermute | solution.py:248
  17.4 0.0 collective-permute-start.4
  17.4 0.0 collective-permute-done.5.refs_0_
  17.4 0.0 collective-permute-done.6.refs_1_
  17.4 1.2 %products.6 = (f32[16,2048]{1,0:T(8,128)S(1)}, f32[16,2048]{1,0:T(8,128)S(1)}, f32[16,2048]{1,0:T(8,128)S(1)}, f32[16,2048]{1,0:T(8,128)S(1)}, f32[16,2048]{1,0:...) custom-call(s32[32,128]{1,0:T(8,128)S(1)} %get-tuple-element.64.name, ...), custom_call_target="tpu_custom_call", output_to_operand_aliasing={{0}: (5, {}), {1}: (6, {}), {2}: (7, {}), {3}: (8, {}), {4}... | custom-call | flops 100 | bytes 100 | tf_op jit(solution)/shard_map/products/pallas_call | solution.py:193
  18.6 0.3 collective-permute-done.4.refs_0_
  18.9 0.6 %products.7 = (f32[16,2048]{1,0:T(8,128)S(1)}, f32[16,2048]{1,0:T(8,128)S(1)}, f32[16,2048]{1,0:T(8,128)S(1)}, f32[16,2048]{1,0:T(8,128)S(1)}, f32[16,2048]{1,0:...) custom-call(s32[32,128]{1,0:T(8,128)S(1)} %get-tuple-element.64.name, ...), custom_call_target="tpu_custom_call", output_to_operand_aliasing={{0}: (3, {}), {1}: (4, {}), {2}: (5, {}), {3}: (6, {}), {4}... | custom-call | flops 100 | bytes 100 | tf_op jit(solution)/shard_map/products/pallas_call | solution.py:193
  19.5 1.8 %collective-permute-start.7 = (f32[16,2048]{1,0:T(8,128)S(1)}, f32[16,2048]{1,0:T(8,128)S(1)}, u32[]{:S(2)}, u32[]{:S(2)}) collective-permute-start(f32[16,2048]{1,0:T(8,128)S(1)} %get-tuple-element.111), channel_id=1, source_target_pairs={{0,1},{1,0},{2,3},{3,2},{4,5},{5,4},{6,7},{7,6},{8,9},{9,8},{10,11... | collective-permute-start | bytes 393224 | tf_op jit(solution)/shard_map/ppermute | solution.py:251
  21.3 0.3 collective-permute-start.10
  21.6 4.3 %collective-permute-done.7.more_ref = f32[16,2048]{1,0:T(8,128)S(1)} collective-permute-done((f32[16,2048]{1,0:T(8,128)S(1)}, f32[16,2048]{1,0:T(8,128)S(1)}, u32[]{:S(2)}, u32[]{:S(2)}) %collective-permute-start.7) | collective-permute-done | bytes 131104 | tf_op jit(solution)/shard_map/ppermute | solution.py:251
  25.9 1.8 %collective-permute-start.8 = (f32[16,2048]{1,0:T(8,128)S(1)}, f32[16,2048]{1,0:T(8,128)S(1)}, u32[]{:S(2)}, u32[]{:S(2)}) collective-permute-start(f32[16,2048]{1,0:T(8,128)S(1)} %get-tuple-element.113), channel_id=1, source_target_pairs={{0,1},{1,3},{2,0},{3,2},{4,5},{5,7},{6,4},{7,6},{8,9},{9,11},{10,8... | collective-permute-start | bytes 393224 | tf_op jit(solution)/shard_map/ppermute | solution.py:290
  27.7 1.2 %collective-permute-start.9 = (f32[16,2048]{1,0:T(8,128)S(1)}, f32[16,2048]{1,0:T(8,128)S(1)}, u32[]{:S(2)}, u32[]{:S(2)}) collective-permute-start(f32[16,2048]{1,0:T(8,128)S(1)} %get-tuple-element.114), channel_id=1, source_target_pairs={{0,2},{1,0},{2,3},{3,1},{4,6},{5,4},{6,7},{7,5},{8,10},{9,8},{10,1... | collective-permute-start | bytes 393224 | tf_op jit(solution)/shard_map/ppermute | solution.py:290
  28.9 0.0 collective-permute-done.10.more_ref
  28.9 1.6 %collective-permute-start.11 = (f32[16,2048]{1,0:T(8,128)S(1)}, f32[16,2048]{1,0:T(8,128)S(1)}, u32[]{:S(2)}, u32[]{:S(2)}) collective-permute-start(f32[16,2048]{1,0:T(8,128)S(1)} %get-tuple-element.121), channel_id=1, source_target_pairs={{0,1},{1,3},{2,0},{3,2},{4,5},{5,7},{6,4},{7,6},{8,9},{9,11},{10,8... | collective-permute-start | bytes 393224 | tf_op jit(solution)/shard_map/ppermute | solution.py:290
  30.5 1.4 %collective-permute-start.12 = (f32[16,2048]{1,0:T(8,128)S(1)}, f32[16,2048]{1,0:T(8,128)S(1)}, u32[]{:S(2)}, u32[]{:S(2)}) collective-permute-start(f32[16,2048]{1,0:T(8,128)S(1)} %get-tuple-element.122), channel_id=1, source_target_pairs={{0,2},{1,0},{2,3},{3,1},{4,6},{5,4},{6,7},{7,5},{8,10},{9,8},{10,1... | collective-permute-start | bytes 393224 | tf_op jit(solution)/shard_map/ppermute | solution.py:290
  31.9 2.3 %collective-permute-done.8.more_ref = f32[16,2048]{1,0:T(8,128)S(1)} collective-permute-done((f32[16,2048]{1,0:T(8,128)S(1)}, f32[16,2048]{1,0:T(8,128)S(1)}, u32[]{:S(2)}, u32[]{:S(2)}) %collective-permute-start.8) | collective-permute-done | bytes 131104 | tf_op jit(solution)/shard_map/ppermute | solution.py:290
  34.3 3.2 %collective-permute-done.9.more_ref = f32[16,2048]{1,0:T(8,128)S(1)} collective-permute-done((f32[16,2048]{1,0:T(8,128)S(1)}, f32[16,2048]{1,0:T(8,128)S(1)}, u32[]{:S(2)}, u32[]{:S(2)}) %collective-permute-start.9) | collective-permute-done | bytes 131104 | tf_op jit(solution)/shard_map/ppermute | solution.py:290
  37.5 0.6 %collective-permute-done.11.more_ref = f32[16,2048]{1,0:T(8,128)S(1)} collective-permute-done((f32[16,2048]{1,0:T(8,128)S(1)}, f32[16,2048]{1,0:T(8,128)S(1)}, u32[]{:S(2)}, u32[]{:S(2)}) %collective-permute-start.11) | collective-permute-done | bytes 131104 | tf_op jit(solution)/shard_map/ppermute | solution.py:290
  38.1 1.3 %collective-permute-done.12 = f32[16,2048]{1,0:T(8,128)S(1)} collective-permute-done((f32[16,2048]{1,0:T(8,128)S(1)}, f32[16,2048]{1,0:T(8,128)S(1)}, u32[]{:S(2)}, u32[]{:S(2)}) %collective-permute-start.12) | collective-permute-done | bytes 131104 | tf_op jit(solution)/shard_map/ppermute | solution.py:290
  39.4 0.7 %pad_maximum_fusion = f32[32,2048]{1,0:T(8,128)} fusion(f32[16,2048]{1,0:T(8,128)S(1)} %add.8, f32[16,2048]{1,0:T(8,128)S(1)} %added.4), kind=kLoop, calls=%fused_computation | loop fusion | flops 65536 | bytes 524288 | tf_op jit(solution)/shard_map/concatenate | solution.py:293
  (6 shorter events, 0.1 us)
Async XLA Ops:
  1.0 9.4 %collective-permute-start.2 = (f32[520,128]{1,0:T(8,128)S(1)}, f32[520,128]{1,0:T(8,128)S(1)}, u32[]{:S(2)}, u32[]{:S(2)}) collective-permute-start(f32[520,128]{1,0:T(8,128)S(1)} %pack.1.refs_0_), channel_id=1, source_target_pairs={{0,16},{4,20},{8,24},{12,28},{16,0},{20,4},{24,8},{28,12},{1,17},{... | collective-permute-start | bytes 798728 | tf_op jit(solution)/shard_map/ppermute | solution.py:248
  4.0 9.3 %collective-permute-start.1 = (f32[520,128]{1,0:T(8,128)S(1)}, f32[520,128]{1,0:T(8,128)S(1)}, u32[]{:S(2)}, u32[]{:S(2)}) collective-permute-start(f32[520,128]{1,0:T(8,128)S(1)} %pack.1.refs_0_), channel_id=1, source_target_pairs={{0,8},{4,12},{8,0},{12,4},{16,24},{20,28},{24,16},{28,20},{1,9},{5... | collective-permute-start | bytes 798728 | tf_op jit(solution)/shard_map/ppermute | solution.py:248
  5.5 8.3 %collective-permute-start.3 = (f32[520,128]{1,0:T(8,128)S(1)}, f32[520,128]{1,0:T(8,128)S(1)}, u32[]{:S(2)}, u32[]{:S(2)}) collective-permute-start(f32[520,128]{1,0:T(8,128)S(1)} %pack.1.refs_0_), channel_id=1, source_target_pairs={{0,4},{4,0},{8,12},{12,8},{16,20},{20,16},{24,28},{28,24},{1,5},{5... | collective-permute-start | bytes 798728 | tf_op jit(solution)/shard_map/ppermute | solution.py:248
  5.5 11.9 %collective-permute-start = (f32[520,128]{1,0:T(8,128)S(1)}, f32[520,128]{1,0:T(8,128)S(1)}, u32[]{:S(2)}, u32[]{:S(2)}) collective-permute-start(f32[520,128]{1,0:T(8,128)S(1)} %pack.1.refs_0_), channel_id=1, source_target_pairs={{0,24},{4,28},{8,16},{12,20},{16,8},{20,12},{24,0},{28,4},{1,25},{... | collective-permute-start | bytes 798728 | tf_op jit(solution)/shard_map/ppermute | solution.py:248
  13.3 4.0 %collective-permute-start.5 = (f32[520,128]{1,0:T(8,128)S(1)}, f32[520,128]{1,0:T(8,128)S(1)}, u32[]{:S(2)}, u32[]{:S(2)}) collective-permute-start(f32[520,128]{1,0:T(8,128)S(1)} %collective-permute-done.1.refs_0_), channel_id=1, source_target_pairs={{0,4},{4,0},{8,12},{12,8},{16,20},{20,16},{24,28},{28,24},{1,5},{5... | collective-permute-start | bytes 798728 | tf_op jit(solution)/shard_map/ppermute | solution.py:248
  13.4 4.0 %collective-permute-start.6 = (f32[520,128]{1,0:T(8,128)S(1)}, f32[520,128]{1,0:T(8,128)S(1)}, u32[]{:S(2)}, u32[]{:S(2)}) collective-permute-start(f32[520,128]{1,0:T(8,128)S(1)} %collective-permute-done.2.refs_1_), channel_id=1, source_target_pairs={{0,4},{4,0},{8,12},{12,8},{16,20},{20,16},{24,28},{28,24},{1,5},{5... | collective-permute-start | bytes 798728 | tf_op jit(solution)/shard_map/ppermute | solution.py:248
  17.4 1.5 %collective-permute-start.4 = (f32[520,128]{1,0:T(8,128)S(1)}, f32[520,128]{1,0:T(8,128)S(1)}, u32[]{:S(2)}, u32[]{:S(2)}) collective-permute-start(f32[520,128]{1,0:T(8,128)S(1)} %collective-permute-done.refs_2_), channel_id=1, source_target_pairs={{0,4},{4,0},{8,12},{12,8},{16,20},{20,16},{24,28},{28,24},{1,5},{5... | collective-permute-start | bytes 798728 | tf_op jit(solution)/shard_map/ppermute | solution.py:248
  19.5 6.4 %collective-permute-start.7 = (f32[16,2048]{1,0:T(8,128)S(1)}, f32[16,2048]{1,0:T(8,128)S(1)}, u32[]{:S(2)}, u32[]{:S(2)}) collective-permute-start(f32[16,2048]{1,0:T(8,128)S(1)} %get-tuple-element.111), channel_id=1, source_target_pairs={{0,1},{1,0},{2,3},{3,2},{4,5},{5,4},{6,7},{7,6},{8,9},{9,8},{10,11... | collective-permute-start | bytes 393224 | tf_op jit(solution)/shard_map/ppermute | solution.py:251
  21.3 7.6 %collective-permute-start.10 = (f32[16,2048]{1,0:T(8,128)S(1)}, f32[16,2048]{1,0:T(8,128)S(1)}, u32[]{:S(2)}, u32[]{:S(2)}) collective-permute-start(f32[16,2048]{1,0:T(8,128)S(1)} %get-tuple-element.119), channel_id=1, source_target_pairs={{0,1},{1,0},{2,3},{3,2},{4,5},{5,4},{6,7},{7,6},{8,9},{9,8},{10,11... | collective-permute-start | bytes 393224 | tf_op jit(solution)/shard_map/ppermute | solution.py:251
  25.9 8.3 %collective-permute-start.8 = (f32[16,2048]{1,0:T(8,128)S(1)}, f32[16,2048]{1,0:T(8,128)S(1)}, u32[]{:S(2)}, u32[]{:S(2)}) collective-permute-start(f32[16,2048]{1,0:T(8,128)S(1)} %get-tuple-element.113), channel_id=1, source_target_pairs={{0,1},{1,3},{2,0},{3,2},{4,5},{5,7},{6,4},{7,6},{8,9},{9,11},{10,8... | collective-permute-start | bytes 393224 | tf_op jit(solution)/shard_map/ppermute | solution.py:290
  27.7 9.8 %collective-permute-start.9 = (f32[16,2048]{1,0:T(8,128)S(1)}, f32[16,2048]{1,0:T(8,128)S(1)}, u32[]{:S(2)}, u32[]{:S(2)}) collective-permute-start(f32[16,2048]{1,0:T(8,128)S(1)} %get-tuple-element.114), channel_id=1, source_target_pairs={{0,2},{1,0},{2,3},{3,1},{4,6},{5,4},{6,7},{7,5},{8,10},{9,8},{10,1... | collective-permute-start | bytes 393224 | tf_op jit(solution)/shard_map/ppermute | solution.py:290
  28.9 9.2 %collective-permute-start.11 = (f32[16,2048]{1,0:T(8,128)S(1)}, f32[16,2048]{1,0:T(8,128)S(1)}, u32[]{:S(2)}, u32[]{:S(2)}) collective-permute-start(f32[16,2048]{1,0:T(8,128)S(1)} %get-tuple-element.121), channel_id=1, source_target_pairs={{0,1},{1,3},{2,0},{3,2},{4,5},{5,7},{6,4},{7,6},{8,9},{9,11},{10,8... | collective-permute-start | bytes 393224 | tf_op jit(solution)/shard_map/ppermute | solution.py:290
  30.5 8.9 %collective-permute-start.12 = (f32[16,2048]{1,0:T(8,128)S(1)}, f32[16,2048]{1,0:T(8,128)S(1)}, u32[]{:S(2)}, u32[]{:S(2)}) collective-permute-start(f32[16,2048]{1,0:T(8,128)S(1)} %get-tuple-element.122), channel_id=1, source_target_pairs={{0,2},{1,0},{2,3},{3,1},{4,6},{5,4},{6,7},{7,5},{8,10},{9,8},{10,1... | collective-permute-start | bytes 393224 | tf_op jit(solution)/shard_map/ppermute | solution.py:290

commit v6 on v5

--- a/solution.py
+++ b/solution.py
@@ -10,7 +10,7 @@
 AB_TILES = 32
 LANES = 128
 UNROLL = 8
-PARTS = 1
+PARTS = 2
 HBM = pl.BlockSpec(memory_space=pltpu.HBM)
 SMEM = pl.BlockSpec(memory_space=pltpu.SMEM)
 VMEM = pl.BlockSpec(memory_space=pltpu.VMEM)
@@ -29,46 +29,48 @@
     return lax.optimization_barrier(values)
 
 
-def pack_kernel(tiles_ref, rows_ref, cols_ref, out_ref, numbers, sems):
+def pack_kernel(tiles_ref, rows_ref, cols_ref, *refs):
+    outs, numbers, sems = refs[:-2], refs[-2], refs[-1]
     side, width = tiles_ref.shape
-    count = rows_ref.shape[1] // PARTS
-    groups = width // LANES // PARTS
-    rows = groups * side + 8
+    count = rows_ref.shape[1] // len(outs)
+    groups = width // LANES // len(outs)
+    base = groups * side
     copies = [
         pltpu.make_async_copy(rows_ref, numbers.at[0], sems.at[0]),
         pltpu.make_async_copy(cols_ref, numbers.at[1], sems.at[1]),
     ]
-    for n in range(PARTS * groups):
-        copies.append(
-            pltpu.make_async_copy(
-                tiles_ref.at[:, pl.ds(n * LANES, LANES)],
-                out_ref.at[pl.ds(n // groups * rows + n % groups * side, side)],
-                sems.at[2 + n],
+    for p, out_ref in enumerate(outs):
+        for g in range(groups):
+            n = p * groups + g
+            copies.append(
+                pltpu.make_async_copy(
+                    tiles_ref.at[:, pl.ds(n * LANES, LANES)],
+                    out_ref.at[pl.ds(g * side, side)],
+                    sems.at[2 + n],
+                )
             )
-        )
     for copy in copies:
         copy.start()
-    for p in range(PARTS):
-        out_ref[(p + 1) * rows - 8 : (p + 1) * rows, :] = jnp.zeros((8, LANES), jnp.float32)
+    for out_ref in outs:
+        out_ref[base : base + 8, :] = jnp.zeros((8, LANES), jnp.float32)
     for copy in copies[:2]:
         copy.wait()
-    for p in range(PARTS):
+    for p, out_ref in enumerate(outs):
         for k in range(2):
-            place = (p + 1) * rows - 8 + k
             values = numbers[k][:, p * count : (p + 1) * count]
-            out_ref[place : place + 1, :count] = values.astype(jnp.float32)
+            out_ref[base + k : base + k + 1, :count] = values.astype(jnp.float32)
     for copy in copies[2:]:
         copy.wait()
 
 
-def pack(tiles, rows, cols):
+def pack(tiles, rows, cols, parts):
     side, width = tiles.shape
     groups = width // LANES
     return pl.pallas_call(
         pack_kernel,
-        out_shape=pltpu.VMEM((groups * side + PARTS * 8, LANES), jnp.float32),
+        out_shape=[pltpu.VMEM((groups // parts * side + 8, LANES), jnp.float32)] * parts,
         in_specs=[HBM] * 3,
-        out_specs=VMEM,
+        out_specs=[VMEM] * parts,
         scratch_shapes=[
             pltpu.VMEM((2, 1, rows.shape[1]), jnp.int32),
             pltpu.SemaphoreType.DMA((2 + groups,)),
@@ -250,10 +252,11 @@
     def along(value, mask):
         return lax.ppermute(value, "vir", [(i, i ^ mask) for i in range(n_vir)])
 
-    own = pack(
+    low, high = pack(
         integrals.reshape(side, width),
         int_rows.reshape(1, count),
         int_cols.reshape(1, count),
+        PARTS,
     )
     height = amplitudes.shape[0] // n_vir
     pieces = [2] * n_vir
@@ -263,21 +266,26 @@
         return accumulate(names, three, packs, blocks, heights, side, count // PARTS)
 
     if n_occ == 8:
-        x, y, far, close = (swap(own, mask) for mask in (2, 4, 6, 1))
+        x_low, y_high, x_high, y_low = swap(low, 2), swap(high, 4), swap(high, 2), swap(low, 4)
+        close = [swap(low, 1), swap(high, 1)]
         three, names = prepare(place, amp_cols, amplitudes, n_vir)
-        blocks = add([own], None)
-        x, y, blocks = together(x, y, blocks)
-        x_turned, y_turned = swap(x, 1), swap(y, 1)
-        blocks = add([x, y, close], blocks)
-        far, blocks = together(far, blocks)
-        far_turned = swap(far, 1)
-        blocks = add([x_turned, y_turned, far], blocks)
-        blocks = add([far_turned], blocks)
+        blocks = add([low, high], None)
+        x_low, y_high, blocks = together(x_low, y_high, blocks)
+        far = [swap(x_low, 4), swap(y_high, 2)]
+        direct = [x_low, y_high, x_high, y_low]
+        blocks = add(direct, blocks)
+        x_low, y_high, x_high, y_low, blocks = together(*direct, blocks)
+        turned = [swap(value, 1) for value in (x_low, y_high, x_high, y_low)]
+        blocks = add(close, blocks)
+        *far, blocks = together(*far, blocks)
+        last = [swap(value, 1) for value in far]
+        blocks = add([*turned, *far], blocks)
+        blocks = add(last, blocks)
     else:
         three, names = prepare(place, amp_cols, amplitudes, n_vir)
-        blocks = add([own], None)
+        blocks = add([low, high], None)
         for mask in range(1, n_occ):
-            blocks = add([swap(own, mask)], blocks)
+            blocks = add([swap(low, mask), swap(high, mask)], blocks)
 
     blocks = iter(blocks)
     blocks = [[next(blocks) for _ in range(pieces[r])] for r in range(n_vir)]

time: 40.3 us -> 40 us (level)
  waiting for transfers between devices: 20 us -> 15.7 us
  starting transfers between devices: 13.1 us -> 16.9 us
    ppermute x7 -> x14, waiting for transfers between devices: 8.32 us -> 4.17 us  [swap(): return lax.ppermute(value, 'occ', [(i, i ^ mask) for i in range(n_occ)])]
    ppermute x7 -> x14, starting transfers between devices: 5.09 us -> 8.85 us  [swap(): return lax.ppermute(value, 'occ', [(i, i ^ mask) for i in range(n_occ)])]
    pallas_call x4 -> x5, Pallas kernels: 3.49 us -> 3.72 us  [accumulate(): pl.pallas_call(functools.partial(product_kernel, n_in, len(heights), tota...]
  transfers between devices with their start and end apart: 13 -> 20, of which waited for: 9 -> 9; matrix products, arithmetic and copies ran while one was open for 0% -> 0% of each run, Pallas kernels for 12% -> 12%
where the time goes in v6:
time: 40 us; the launch traced here: 39.8 us
  starting transfers between devices  16.9 us (42%)
  waiting for transfers between devices  15.7 us (39%)
  Pallas kernels  6.4 us (16%)
  other arithmetic  0.74 us (2%)
    ppermute x14, starting transfers between devices, swap(): return lax.ppermute(value, 'occ', [(i, i ^ mask) for i in range(n_occ)])  8.85 us
    ppermute x4, waiting for transfers between devices, local(): lax.ppermute(piece, 'vir', ring)  7.22 us
    ppermute x4, starting transfers between devices, local(): lax.ppermute(piece, 'vir', ring)  5.95 us
    ppermute x2, waiting for transfers between devices, along(): return lax.ppermute(value, 'vir', [(i, i ^ mask) for i in range(n_vir)])  4.32 us
    ppermute x14, waiting for transfers between devices, swap(): return lax.ppermute(value, 'occ', [(i, i ^ mask) for i in range(n_occ)])  4.17 us
    pallas_call x5, Pallas kernels, accumulate(): pl.pallas_call(functools.partial(product_kernel, n_in, len(heights), tota...  3.72 us
    ppermute x2, starting transfers between devices, along(): return lax.ppermute(value, 'vir', [(i, i ^ mask) for i in range(n_vir)])  2.09 us
    pallas_call x1, Pallas kernels, prepare(): pl.pallas_call(functools.partial(prepare_kernel, n_blocks, side), out_sha...  1.56 us
  transfers between devices with their start and end apart: 20, of which 9 were waited for; matrix products, arithmetic and copies ran while one was open for 0% of the time, Pallas kernels for 12%

profile of v6, /device:TPU:0, one launch (start us, length us, event | category | flops | bytes accessed | tf_op | source)
XLA Modules:
  0.0 39.8 jit_solution(3631080682862649743)
XLA Ops:
  0.0 1.0 %pack.1 = (f32[264,128]{1,0:T(8,128)S(1)}, f32[264,128]{1,0:T(8,128)S(1)}) custom-call(f32[64,1024]{1,0:T(8,128)} %bitcast.4, s32[1,16]{1,0:T(1,128)} %bitcast.5, s32[1,16]{1,0:T(1,128)} %bitcast.6), custom_call_target="tpu_custom_call" | custom-call | tf_op jit(solution)/shard_map/pack/pallas_call | solution.py:69
  1.0 3.0 %collective-permute-start = (f32[264,128]{1,0:T(8,128)S(1)}, f32[264,128]{1,0:T(8,128)S(1)}, u32[]{:S(2)}, u32[]{:S(2)}) collective-permute-start(f32[264,128]{1,0:T(8,128)S(1)} %get-tuple-element.89.refs_0_), channel_id=1, source_target_pairs={{0,8},{4,12},{8,0},{12,4},{16,24},{20,28},{24,16},{28,20},{1,9},{5... | collective-permute-start | bytes 405512 | tf_op jit(solution)/shard_map/ppermute | solution.py:250
  4.0 1.5 %collective-permute-start.1 = (f32[264,128]{1,0:T(8,128)S(1)}, f32[264,128]{1,0:T(8,128)S(1)}, u32[]{:S(2)}, u32[]{:S(2)}) collective-permute-start(f32[264,128]{1,0:T(8,128)S(1)} %get-tuple-element.90.refs_1_), channel_id=1, source_target_pairs={{0,16},{4,20},{8,24},{12,28},{16,0},{20,4},{24,8},{28,12},{1,17},{... | collective-permute-start | bytes 405512 | tf_op jit(solution)/shard_map/ppermute | solution.py:250
  5.5 0.5 %collective-permute-start.7 = (f32[264,128]{1,0:T(8,128)S(1)}, f32[264,128]{1,0:T(8,128)S(1)}, u32[]{:S(2)}, u32[]{:S(2)}) collective-permute-start(f32[264,128]{1,0:T(8,128)S(1)} %get-tuple-element.89.refs_0_), channel_id=1, source_target_pairs={{0,16},{4,20},{8,24},{12,28},{16,0},{20,4},{24,8},{28,12},{1,17},{... | collective-permute-start | bytes 405512 | tf_op jit(solution)/shard_map/ppermute | solution.py:250
  6.0 0.1 collective-permute-start.6
  6.1 0.0 collective-permute-start.4
  6.1 1.6 %prepare.1 = (bf16[32,128,192]{2,1,0:T(8,128)(2,1)S(1)}, s32[32,128]{1,0:T(8,128)S(1)}) custom-call(s32[1]{0:T(128)} %bitcast.place_ref, s32[1,32]{1,0:T(1,128)} %names_in.1, f32[128,2048]{1,0:T(8,128)} %amp_ref.1), custom_call_target="tpu_custom_call" | custom-call | flops 100 | bytes 100 | tf_op jit(solution)/shard_map/prepare/pallas_call | solution.py:125
  7.7 0.6 %products.5 = (f32[16,2048]{1,0:T(8,128)S(1)}, f32[16,2048]{1,0:T(8,128)S(1)}, f32[16,2048]{1,0:T(8,128)S(1)}, f32[16,2048]{1,0:T(8,128)S(1)}, f32[16,2048]{1,0:...) custom-call(s32[32,128]{1,0:T(8,128)S(1)} %get-tuple-element.87.names_ref, ...), custom_call_target="tpu_custom_call" | custom-call | flops 100 | bytes 100 | tf_op jit(solution)/shard_map/products/pallas_call | solution.py:195
  8.2 0.0 collective-permute-done.refs_0_
  8.2 0.6 %collective-permute-start.5 = (f32[264,128]{1,0:T(8,128)S(1)}, f32[264,128]{1,0:T(8,128)S(1)}, u32[]{:S(2)}, u32[]{:S(2)}) collective-permute-start(f32[264,128]{1,0:T(8,128)S(1)} %get-tuple-element.90.refs_1_), channel_id=1, source_target_pairs={{0,4},{4,0},{8,12},{12,8},{16,20},{20,16},{24,28},{28,24},{1,5},{5... | collective-permute-start | bytes 405512 | tf_op jit(solution)/shard_map/ppermute | solution.py:250
  8.8 1.7 %collective-permute-done.1.refs_1_ = f32[264,128]{1,0:T(8,128)S(1)} collective-permute-done((f32[264,128]{1,0:T(8,128)S(1)}, f32[264,128]{1,0:T(8,128)S(1)}, u32[]{:S(2)}, u32[]{:S(2)}) %collective-permute-start.1) | collective-permute-done | bytes 135200 | tf_op jit(solution)/shard_map/ppermute | solution.py:250
  10.5 1.5 %collective-permute-start.2 = (f32[264,128]{1,0:T(8,128)S(1)}, f32[264,128]{1,0:T(8,128)S(1)}, u32[]{:S(2)}, u32[]{:S(2)}) collective-permute-start(f32[264,128]{1,0:T(8,128)S(1)} %collective-permute-done.refs_0_), channel_id=1, source_target_pairs={{0,16},{4,20},{8,24},{12,28},{16,0},{20,4},{24,8},{28,12},{1,17},{... | collective-permute-start | bytes 405512 | tf_op jit(solution)/shard_map/ppermute | solution.py:250
  12.0 0.1 collective-permute-done.7.refs_3_
  12.1 0.5 %collective-permute-start.3 = (f32[264,128]{1,0:T(8,128)S(1)}, f32[264,128]{1,0:T(8,128)S(1)}, u32[]{:S(2)}, u32[]{:S(2)}) collective-permute-start(f32[264,128]{1,0:T(8,128)S(1)} %collective-permute-done.1.refs_1_), channel_id=1, source_target_pairs={{0,8},{4,12},{8,0},{12,4},{16,24},{20,28},{24,16},{28,20},{1,9},{5... | collective-permute-start | bytes 405512 | tf_op jit(solution)/shard_map/ppermute | solution.py:250
  12.6 0.0 collective-permute-done.6.refs_2_
  12.6 0.9 %products.6 = (f32[16,2048]{1,0:T(8,128)S(1)}, f32[16,2048]{1,0:T(8,128)S(1)}, f32[16,2048]{1,0:T(8,128)S(1)}, f32[16,2048]{1,0:T(8,128)S(1)}, f32[16,2048]{1,0:...) custom-call(s32[32,128]{1,0:T(8,128)S(1)} %get-tuple-element.87.name, ...), custom_call_target="tpu_custom_call", output_to_operand_aliasing={{0}: (6, {}), {1}: (7, {}), {2}: (8, {}), {3}: (9, {}), {4}... | custom-call | flops 100 | bytes 100 | tf_op jit(solution)/shard_map/products/pallas_call | solution.py:195
  13.4 0.1 collective-permute-start.10
  13.5 0.0 collective-permute-done.4.refs_0_
  13.5 0.5 %collective-permute-start.11 = (f32[264,128]{1,0:T(8,128)S(1)}, f32[264,128]{1,0:T(8,128)S(1)}, u32[]{:S(2)}, u32[]{:S(2)}) collective-permute-start(f32[264,128]{1,0:T(8,128)S(1)} %collective-permute-done.1.refs_1_), channel_id=1, source_target_pairs={{0,4},{4,0},{8,12},{12,8},{16,20},{20,16},{24,28},{28,24},{1,5},{5... | collective-permute-start | bytes 405512 | tf_op jit(solution)/shard_map/ppermute | solution.py:250
  14.0 0.0 collective-permute-done.5.refs_1_
  14.0 0.1 collective-permute-start.12
  14.1 0.6 %products.7 = (f32[16,2048]{1,0:T(8,128)S(1)}, f32[16,2048]{1,0:T(8,128)S(1)}, f32[16,2048]{1,0:T(8,128)S(1)}, f32[16,2048]{1,0:T(8,128)S(1)}, f32[16,2048]{1,0:...) custom-call(s32[32,128]{1,0:T(8,128)S(1)} %get-tuple-element.87.name, ...), custom_call_target="tpu_custom_call", output_to_operand_aliasing={{0}: (4, {}), {1}: (5, {}), {2}: (6, {}), {3}: (7, {}), {4}... | custom-call | flops 100 | bytes 100 | tf_op jit(solution)/shard_map/products/pallas_call | solution.py:195
  14.7 0.8 %collective-permute-done.2.refs_4_ = f32[264,128]{1,0:T(8,128)S(1)} collective-permute-done((f32[264,128]{1,0:T(8,128)S(1)}, f32[264,128]{1,0:T(8,128)S(1)}, u32[]{:S(2)}, u32[]{:S(2)}) %collective-permute-start.2) | collective-permute-done | bytes 135200 | tf_op jit(solution)/shard_map/ppermute | solution.py:250
  15.5 0.0 collective-permute-start.13
  15.5 1.6 %collective-permute-done.3.refs_5_ = f32[264,128]{1,0:T(8,128)S(1)} collective-permute-done((f32[264,128]{1,0:T(8,128)S(1)}, f32[264,128]{1,0:T(8,128)S(1)}, u32[]{:S(2)}, u32[]{:S(2)}) %collective-permute-start.3) | collective-permute-done | bytes 135200 | tf_op jit(solution)/shard_map/ppermute | solution.py:250
  17.1 0.0 collective-permute-start.8
  17.1 0.0 collective-permute-done.10.refs_0_
  17.1 0.5 %collective-permute-start.9 = (f32[264,128]{1,0:T(8,128)S(1)}, f32[264,128]{1,0:T(8,128)S(1)}, u32[]{:S(2)}, u32[]{:S(2)}) collective-permute-start(f32[264,128]{1,0:T(8,128)S(1)} %collective-permute-done.3.refs_5_), channel_id=1, source_target_pairs={{0,4},{4,0},{8,12},{12,8},{16,20},{20,16},{24,28},{28,24},{1,5},{5... | collective-permute-start | bytes 405512 | tf_op jit(solution)/shard_map/ppermute | solution.py:250
  17.6 0.0 collective-permute-done.11.refs_1_
  17.6 0.0 collective-permute-done.12.refs_2_
  17.6 0.0 collective-permute-done.13.refs_3_
  17.6 1.2 %products.8 = (f32[16,2048]{1,0:T(8,128)S(1)}, f32[16,2048]{1,0:T(8,128)S(1)}, f32[16,2048]{1,0:T(8,128)S(1)}, f32[16,2048]{1,0:T(8,128)S(1)}, f32[16,2048]{1,0:...) custom-call(s32[32,128]{1,0:T(8,128)S(1)} %get-tuple-element.87.name, ...), custom_call_target="tpu_custom_call", output_to_operand_aliasing={{0}: (8, {}), {1}: (9, {}), {2}: (10, {}), {3}: (11, {}), {... | custom-call | flops 100 | bytes 100 | tf_op jit(solution)/shard_map/products/pallas_call | solution.py:195
  18.8 0.0 collective-permute-done.8.refs_0_
  18.8 0.0 collective-permute-done.9.refs_1_
  18.8 0.6 %products.9 = (f32[16,2048]{1,0:T(8,128)S(1)}, f32[16,2048]{1,0:T(8,128)S(1)}, f32[16,2048]{1,0:T(8,128)S(1)}, f32[16,2048]{1,0:T(8,128)S(1)}, f32[16,2048]{1,0:...) custom-call(s32[32,128]{1,0:T(8,128)S(1)} %get-tuple-element.87.name, ...), custom_call_target="tpu_custom_call", output_to_operand_aliasing={{0}: (4, {}), {1}: (5, {}), {2}: (6, {}), {3}: (7, {}), {4}... | custom-call | flops 100 | bytes 100 | tf_op jit(solution)/shard_map/products/pallas_call | solution.py:195
  19.4 1.6 %collective-permute-start.14 = (f32[16,2048]{1,0:T(8,128)S(1)}, f32[16,2048]{1,0:T(8,128)S(1)}, u32[]{:S(2)}, u32[]{:S(2)}) collective-permute-start(f32[16,2048]{1,0:T(8,128)S(1)} %get-tuple-element.157), channel_id=1, source_target_pairs={{0,1},{1,0},{2,3},{3,2},{4,5},{5,4},{6,7},{7,6},{8,9},{9,8},{10,11... | collective-permute-start | bytes 393224 | tf_op jit(solution)/shard_map/ppermute | solution.py:253
  21.0 0.5 %collective-permute-start.17 = (f32[16,2048]{1,0:T(8,128)S(1)}, f32[16,2048]{1,0:T(8,128)S(1)}, u32[]{:S(2)}, u32[]{:S(2)}) collective-permute-start(f32[16,2048]{1,0:T(8,128)S(1)} %get-tuple-element.165), channel_id=1, source_target_pairs={{0,1},{1,0},{2,3},{3,2},{4,5},{5,4},{6,7},{7,6},{8,9},{9,8},{10,11... | collective-permute-start | bytes 393224 | tf_op jit(solution)/shard_map/ppermute | solution.py:253
  21.5 4.3 %collective-permute-done.14.more_ref = f32[16,2048]{1,0:T(8,128)S(1)} collective-permute-done((f32[16,2048]{1,0:T(8,128)S(1)}, f32[16,2048]{1,0:T(8,128)S(1)}, u32[]{:S(2)}, u32[]{:S(2)}) %collective-permute-start.14) | collective-permute-done | bytes 131104 | tf_op jit(solution)/shard_map/ppermute | solution.py:253
  25.8 1.6 %collective-permute-start.15 = (f32[16,2048]{1,0:T(8,128)S(1)}, f32[16,2048]{1,0:T(8,128)S(1)}, u32[]{:S(2)}, u32[]{:S(2)}) collective-permute-start(f32[16,2048]{1,0:T(8,128)S(1)} %get-tuple-element.159), channel_id=1, source_target_pairs={{0,1},{1,3},{2,0},{3,2},{4,5},{5,7},{6,4},{7,6},{8,9},{9,11},{10,8... | collective-permute-start | bytes 393224 | tf_op jit(solution)/shard_map/ppermute | solution.py:298
  27.4 1.4 %collective-permute-start.16 = (f32[16,2048]{1,0:T(8,128)S(1)}, f32[16,2048]{1,0:T(8,128)S(1)}, u32[]{:S(2)}, u32[]{:S(2)}) collective-permute-start(f32[16,2048]{1,0:T(8,128)S(1)} %get-tuple-element.160), channel_id=1, source_target_pairs={{0,2},{1,0},{2,3},{3,1},{4,6},{5,4},{6,7},{7,5},{8,10},{9,8},{10,1... | collective-permute-start | bytes 393224 | tf_op jit(solution)/shard_map/ppermute | solution.py:298
  28.8 0.0 collective-permute-done.17.more_ref
  28.8 1.4 %collective-permute-start.18 = (f32[16,2048]{1,0:T(8,128)S(1)}, f32[16,2048]{1,0:T(8,128)S(1)}, u32[]{:S(2)}, u32[]{:S(2)}) collective-permute-start(f32[16,2048]{1,0:T(8,128)S(1)} %get-tuple-element.167), channel_id=1, source_target_pairs={{0,1},{1,3},{2,0},{3,2},{4,5},{5,7},{6,4},{7,6},{8,9},{9,11},{10,8... | collective-permute-start | bytes 393224 | tf_op jit(solution)/shard_map/ppermute | solution.py:298
  30.2 1.6 %collective-permute-start.19 = (f32[16,2048]{1,0:T(8,128)S(1)}, f32[16,2048]{1,0:T(8,128)S(1)}, u32[]{:S(2)}, u32[]{:S(2)}) collective-permute-start(f32[16,2048]{1,0:T(8,128)S(1)} %get-tuple-element.168), channel_id=1, source_target_pairs={{0,2},{1,0},{2,3},{3,1},{4,6},{5,4},{6,7},{7,5},{8,10},{9,8},{10,1... | collective-permute-start | bytes 393224 | tf_op jit(solution)/shard_map/ppermute | solution.py:298
  31.8 2.5 %collective-permute-done.15.more_ref = f32[16,2048]{1,0:T(8,128)S(1)} collective-permute-done((f32[16,2048]{1,0:T(8,128)S(1)}, f32[16,2048]{1,0:T(8,128)S(1)}, u32[]{:S(2)}, u32[]{:S(2)}) %collective-permute-start.15) | collective-permute-done | bytes 131104 | tf_op jit(solution)/shard_map/ppermute | solution.py:298
  34.3 2.8 %collective-permute-done.16.more_ref = f32[16,2048]{1,0:T(8,128)S(1)} collective-permute-done((f32[16,2048]{1,0:T(8,128)S(1)}, f32[16,2048]{1,0:T(8,128)S(1)}, u32[]{:S(2)}, u32[]{:S(2)}) %collective-permute-start.16) | collective-permute-done | bytes 131104 | tf_op jit(solution)/shard_map/ppermute | solution.py:298
  37.1 1.1 %collective-permute-done.18.more_ref = f32[16,2048]{1,0:T(8,128)S(1)} collective-permute-done((f32[16,2048]{1,0:T(8,128)S(1)}, f32[16,2048]{1,0:T(8,128)S(1)}, u32[]{:S(2)}, u32[]{:S(2)}) %collective-permute-start.18) | collective-permute-done | bytes 131104 | tf_op jit(solution)/shard_map/ppermute | solution.py:298
  38.2 0.9 %collective-permute-done.19 = f32[16,2048]{1,0:T(8,128)S(1)} collective-permute-done((f32[16,2048]{1,0:T(8,128)S(1)}, f32[16,2048]{1,0:T(8,128)S(1)}, u32[]{:S(2)}, u32[]{:S(2)}) %collective-permute-start.19) | collective-permute-done | bytes 131104 | tf_op jit(solution)/shard_map/ppermute | solution.py:298
  39.1 0.7 %pad_maximum_fusion = f32[32,2048]{1,0:T(8,128)} fusion(f32[16,2048]{1,0:T(8,128)S(1)} %add.8, f32[16,2048]{1,0:T(8,128)S(1)} %added.4), kind=kLoop, calls=%fused_computation | loop fusion | flops 65536 | bytes 524288 | tf_op jit(solution)/shard_map/concatenate | solution.py:301
  (6 shorter events, 0.2 us)
Async XLA Ops:
  1.0 7.2 %collective-permute-start = (f32[264,128]{1,0:T(8,128)S(1)}, f32[264,128]{1,0:T(8,128)S(1)}, u32[]{:S(2)}, u32[]{:S(2)}) collective-permute-start(f32[264,128]{1,0:T(8,128)S(1)} %get-tuple-element.89.refs_0_), channel_id=1, source_target_pairs={{0,8},{4,12},{8,0},{12,4},{16,24},{20,28},{24,16},{28,20},{1,9},{5... | collective-permute-start | bytes 405512 | tf_op jit(solution)/shard_map/ppermute | solution.py:250
  4.0 6.5 %collective-permute-start.1 = (f32[264,128]{1,0:T(8,128)S(1)}, f32[264,128]{1,0:T(8,128)S(1)}, u32[]{:S(2)}, u32[]{:S(2)}) collective-permute-start(f32[264,128]{1,0:T(8,128)S(1)} %get-tuple-element.90.refs_1_), channel_id=1, source_target_pairs={{0,16},{4,20},{8,24},{12,28},{16,0},{20,4},{24,8},{28,12},{1,17},{... | collective-permute-start | bytes 405512 | tf_op jit(solution)/shard_map/ppermute | solution.py:250
  5.5 6.5 %collective-permute-start.7 = (f32[264,128]{1,0:T(8,128)S(1)}, f32[264,128]{1,0:T(8,128)S(1)}, u32[]{:S(2)}, u32[]{:S(2)}) collective-permute-start(f32[264,128]{1,0:T(8,128)S(1)} %get-tuple-element.89.refs_0_), channel_id=1, source_target_pairs={{0,16},{4,20},{8,24},{12,28},{16,0},{20,4},{24,8},{28,12},{1,17},{... | collective-permute-start | bytes 405512 | tf_op jit(solution)/shard_map/ppermute | solution.py:250
  6.0 6.5 %collective-permute-start.6 = (f32[264,128]{1,0:T(8,128)S(1)}, f32[264,128]{1,0:T(8,128)S(1)}, u32[]{:S(2)}, u32[]{:S(2)}) collective-permute-start(f32[264,128]{1,0:T(8,128)S(1)} %get-tuple-element.90.refs_1_), channel_id=1, source_target_pairs={{0,8},{4,12},{8,0},{12,4},{16,24},{20,28},{24,16},{28,20},{1,9},{5... | collective-permute-start | bytes 405512 | tf_op jit(solution)/shard_map/ppermute | solution.py:250
  6.1 7.4 %collective-permute-start.4 = (f32[264,128]{1,0:T(8,128)S(1)}, f32[264,128]{1,0:T(8,128)S(1)}, u32[]{:S(2)}, u32[]{:S(2)}) collective-permute-start(f32[264,128]{1,0:T(8,128)S(1)} %get-tuple-element.89.refs_0_), channel_id=1, source_target_pairs={{0,4},{4,0},{8,12},{12,8},{16,20},{20,16},{24,28},{28,24},{1,5},{5... | collective-permute-start | bytes 405512 | tf_op jit(solution)/shard_map/ppermute | solution.py:250
  8.2 5.8 %collective-permute-start.5 = (f32[264,128]{1,0:T(8,128)S(1)}, f32[264,128]{1,0:T(8,128)S(1)}, u32[]{:S(2)}, u32[]{:S(2)}) collective-permute-start(f32[264,128]{1,0:T(8,128)S(1)} %get-tuple-element.90.refs_1_), channel_id=1, source_target_pairs={{0,4},{4,0},{8,12},{12,8},{16,20},{20,16},{24,28},{28,24},{1,5},{5... | collective-permute-start | bytes 405512 | tf_op jit(solution)/shard_map/ppermute | solution.py:250
  10.5 5.0 %collective-permute-start.2 = (f32[264,128]{1,0:T(8,128)S(1)}, f32[264,128]{1,0:T(8,128)S(1)}, u32[]{:S(2)}, u32[]{:S(2)}) collective-permute-start(f32[264,128]{1,0:T(8,128)S(1)} %collective-permute-done.refs_0_), channel_id=1, source_target_pairs={{0,16},{4,20},{8,24},{12,28},{16,0},{20,4},{24,8},{28,12},{1,17},{... | collective-permute-start | bytes 405512 | tf_op jit(solution)/shard_map/ppermute | solution.py:250
  12.1 5.0 %collective-permute-start.3 = (f32[264,128]{1,0:T(8,128)S(1)}, f32[264,128]{1,0:T(8,128)S(1)}, u32[]{:S(2)}, u32[]{:S(2)}) collective-permute-start(f32[264,128]{1,0:T(8,128)S(1)} %collective-permute-done.1.refs_1_), channel_id=1, source_target_pairs={{0,8},{4,12},{8,0},{12,4},{16,24},{20,28},{24,16},{28,20},{1,9},{5... | collective-permute-start | bytes 405512 | tf_op jit(solution)/shard_map/ppermute | solution.py:250
  13.4 3.7 %collective-permute-start.10 = (f32[264,128]{1,0:T(8,128)S(1)}, f32[264,128]{1,0:T(8,128)S(1)}, u32[]{:S(2)}, u32[]{:S(2)}) collective-permute-start(f32[264,128]{1,0:T(8,128)S(1)} %collective-permute-done.refs_0_), channel_id=1, source_target_pairs={{0,4},{4,0},{8,12},{12,8},{16,20},{20,16},{24,28},{28,24},{1,5},{5... | collective-permute-start | bytes 405512 | tf_op jit(solution)/shard_map/ppermute | solution.py:250
  13.5 4.1 %collective-permute-start.11 = (f32[264,128]{1,0:T(8,128)S(1)}, f32[264,128]{1,0:T(8,128)S(1)}, u32[]{:S(2)}, u32[]{:S(2)}) collective-permute-start(f32[264,128]{1,0:T(8,128)S(1)} %collective-permute-done.1.refs_1_), channel_id=1, source_target_pairs={{0,4},{4,0},{8,12},{12,8},{16,20},{20,16},{24,28},{28,24},{1,5},{5... | collective-permute-start | bytes 405512 | tf_op jit(solution)/shard_map/ppermute | solution.py:250
  14.0 3.6 %collective-permute-start.12 = (f32[264,128]{1,0:T(8,128)S(1)}, f32[264,128]{1,0:T(8,128)S(1)}, u32[]{:S(2)}, u32[]{:S(2)}) collective-permute-start(f32[264,128]{1,0:T(8,128)S(1)} %collective-permute-done.6.refs_2_), channel_id=1, source_target_pairs={{0,4},{4,0},{8,12},{12,8},{16,20},{20,16},{24,28},{28,24},{1,5},{5... | collective-permute-start | bytes 405512 | tf_op jit(solution)/shard_map/ppermute | solution.py:250
  15.5 2.1 %collective-permute-start.13 = (f32[264,128]{1,0:T(8,128)S(1)}, f32[264,128]{1,0:T(8,128)S(1)}, u32[]{:S(2)}, u32[]{:S(2)}) collective-permute-start(f32[264,128]{1,0:T(8,128)S(1)} %collective-permute-done.7.refs_3_), channel_id=1, source_target_pairs={{0,4},{4,0},{8,12},{12,8},{16,20},{20,16},{24,28},{28,24},{1,5},{5... | collective-permute-start | bytes 405512 | tf_op jit(solution)/shard_map/ppermute | solution.py:250
  17.1 1.7 %collective-permute-start.8 = (f32[264,128]{1,0:T(8,128)S(1)}, f32[264,128]{1,0:T(8,128)S(1)}, u32[]{:S(2)}, u32[]{:S(2)}) collective-permute-start(f32[264,128]{1,0:T(8,128)S(1)} %collective-permute-done.2.refs_4_), channel_id=1, source_target_pairs={{0,4},{4,0},{8,12},{12,8},{16,20},{20,16},{24,28},{28,24},{1,5},{5... | collective-permute-start | bytes 405512 | tf_op jit(solution)/shard_map/ppermute | solution.py:250
  17.1 1.7 %collective-permute-start.9 = (f32[264,128]{1,0:T(8,128)S(1)}, f32[264,128]{1,0:T(8,128)S(1)}, u32[]{:S(2)}, u32[]{:S(2)}) collective-permute-start(f32[264,128]{1,0:T(8,128)S(1)} %collective-permute-done.3.refs_5_), channel_id=1, source_target_pairs={{0,4},{4,0},{8,12},{12,8},{16,20},{20,16},{24,28},{28,24},{1,5},{5... | collective-permute-start | bytes 405512 | tf_op jit(solution)/shard_map/ppermute | solution.py:250
  19.4 6.4 %collective-permute-start.14 = (f32[16,2048]{1,0:T(8,128)S(1)}, f32[16,2048]{1,0:T(8,128)S(1)}, u32[]{:S(2)}, u32[]{:S(2)}) collective-permute-start(f32[16,2048]{1,0:T(8,128)S(1)} %get-tuple-element.157), channel_id=1, source_target_pairs={{0,1},{1,0},{2,3},{3,2},{4,5},{5,4},{6,7},{7,6},{8,9},{9,8},{10,11... | collective-permute-start | bytes 393224 | tf_op jit(solution)/shard_map/ppermute | solution.py:253
  21.0 7.8 %collective-permute-start.17 = (f32[16,2048]{1,0:T(8,128)S(1)}, f32[16,2048]{1,0:T(8,128)S(1)}, u32[]{:S(2)}, u32[]{:S(2)}) collective-permute-start(f32[16,2048]{1,0:T(8,128)S(1)} %get-tuple-element.165), channel_id=1, source_target_pairs={{0,1},{1,0},{2,3},{3,2},{4,5},{5,4},{6,7},{7,6},{8,9},{9,8},{10,11... | collective-permute-start | bytes 393224 | tf_op jit(solution)/shard_map/ppermute | solution.py:253
  25.8 8.5 %collective-permute-start.15 = (f32[16,2048]{1,0:T(8,128)S(1)}, f32[16,2048]{1,0:T(8,128)S(1)}, u32[]{:S(2)}, u32[]{:S(2)}) collective-permute-start(f32[16,2048]{1,0:T(8,128)S(1)} %get-tuple-element.159), channel_id=1, source_target_pairs={{0,1},{1,3},{2,0},{3,2},{4,5},{5,7},{6,4},{7,6},{8,9},{9,11},{10,8... | collective-permute-start | bytes 393224 | tf_op jit(solution)/shard_map/ppermute | solution.py:298
  27.4 9.7 %collective-permute-start.16 = (f32[16,2048]{1,0:T(8,128)S(1)}, f32[16,2048]{1,0:T(8,128)S(1)}, u32[]{:S(2)}, u32[]{:S(2)}) collective-permute-start(f32[16,2048]{1,0:T(8,128)S(1)} %get-tuple-element.160), channel_id=1, source_target_pairs={{0,2},{1,0},{2,3},{3,1},{4,6},{5,4},{6,7},{7,5},{8,10},{9,8},{10,1... | collective-permute-start | bytes 393224 | tf_op jit(solution)/shard_map/ppermute | solution.py:298
  28.8 9.4 %collective-permute-start.18 = (f32[16,2048]{1,0:T(8,128)S(1)}, f32[16,2048]{1,0:T(8,128)S(1)}, u32[]{:S(2)}, u32[]{:S(2)}) collective-permute-start(f32[16,2048]{1,0:T(8,128)S(1)} %get-tuple-element.167), channel_id=1, source_target_pairs={{0,1},{1,3},{2,0},{3,2},{4,5},{5,7},{6,4},{7,6},{8,9},{9,11},{10,8... | collective-permute-start | bytes 393224 | tf_op jit(solution)/shard_map/ppermute | solution.py:298
  30.2 8.9 %collective-permute-start.19 = (f32[16,2048]{1,0:T(8,128)S(1)}, f32[16,2048]{1,0:T(8,128)S(1)}, u32[]{:S(2)}, u32[]{:S(2)}) collective-permute-start(f32[16,2048]{1,0:T(8,128)S(1)} %get-tuple-element.168), channel_id=1, source_target_pairs={{0,2},{1,0},{2,3},{3,1},{4,6},{5,4},{6,7},{7,5},{8,10},{9,8},{10,1... | collective-permute-start | bytes 393224 | tf_op jit(solution)/shard_map/ppermute | solution.py:298
